TPU v7x, 256 devices: a whole 4x4x8 slice. The times are simulated.
256 devices in a mesh: section: 2 (over x_hi), expert: 64 (over z, y, x_lo), dp: 2 (over core).
Axes of the slice: x: 4 (x_hi: 2, x_lo: 2; x = x_hi * 2 + x_lo), y: 4, z: 8, core: 2. Of those that a mesh axis runs over, the one named last changes fastest.
Arguments:
- tokens: bfloat16 [2, 16384, 3072], P('section', ('expert', 'dp')), may hold values from -6 to 6
- expert_ids: int32 [2, 16384, 2], P('section', ('expert', 'dp')), may hold values from 0 to 63, all different within a row; in each aligned block of 64 rows (0 to 63, 64 to 127, ..., all dimensions but the last counted through in order) at most 4 rows name the same one
- combine: bfloat16 [2, 16384, 2], P('section', ('expert', 'dp')), may hold values from 0.099609375 to 0.8984375
- upstream: bfloat16 [2, 16384, 3072], P('section', ('expert', 'dp')), may hold values from -6 to 6
- w_gate: bfloat16 [2, 64, 3072, 128], P('section', 'expert', 'dp'), may hold values from -0.109375 to 0.109375
- w_up: bfloat16 [2, 64, 3072, 128], P('section', 'expert', 'dp'), may hold values from -0.109375 to 0.109375
- w_down: bfloat16 [2, 64, 128, 3072], P('section', 'expert', None, 'dp'), may hold values from -0.5 to 0.5
Outputs:
- grad_x: bfloat16 [2, 16384, 3072], P('section', ('expert', 'dp'))
- grad_combine: bfloat16 [2, 16384, 2], P('section', ('expert', 'dp'))
- grad_gate: bfloat16 [2, 64, 3072, 128], P('section', 'expert', 'dp')
- grad_up: bfloat16 [2, 64, 3072, 128], P('section', 'expert', 'dp')
- grad_down: bfloat16 [2, 64, 128, 3072], P('section', 'expert', None, 'dp')
Inputs may be any that keep to these rules, and one draw needn't show every extreme that they name: `expert_ids`: each token names two different experts. In each aligned block of 64 tokens (one micro-batch of one device) no expert is named by more than 4 tokens, and this bound is reached in some block.
All inputs are finite; a program needn't handle non-finite values.
Results may differ from a plain program's by a relative error of at most 0.0065.
Values may be sent and summed in bfloat16 or wider, within the bound.
No kernel may reach another device: no remote copies, remote signals or barrier semaphores. Data moves between devices by JAX's collectives and lax.ppermute only.
A program may use at most 64 MiB of HBM per device.

v0:
```python
import jax
import jax.numpy as jnp
from jax import lax
from jax.sharding import PartitionSpec as P

TOK_MB = 64


def passed_along(shard, axis, by):
    peers = lax.axis_size(axis)
    return lax.ppermute(shard, axis, [(i, (i + by) % peers) for i in range(peers)])


def build_table(block_ids, expert_count, slot_cap):
    flat_ids = block_ids.reshape(-1)
    labels = jnp.arange(expert_count, dtype=jnp.int32)
    hits_mask = (flat_ids[:, None] == labels[None, :]).astype(jnp.int32)
    earlier = jnp.cumsum(hits_mask, axis=0) - hits_mask
    position = jnp.sum(earlier * hits_mask, axis=1)
    target = flat_ids * slot_cap + position
    columns = jnp.arange(expert_count * slot_cap, dtype=jnp.int32)
    picked = (target[:, None] == columns[None, :]).astype(jnp.bfloat16)
    return picked.reshape(block_ids.shape[0], 2, expert_count * slot_cap)


def contract_rows(former, latter):
    return lax.dot_general(
        former, latter, (((0,), (0,)), ((), ())), preferred_element_type=jnp.float32
    )


def contract_last(former, latter):
    return lax.dot_general(
        former, latter, (((1,), (1,)), ((), ())), preferred_element_type=jnp.float32
    )


def expert_pass(arrived_rows, arrived_grads, arrived_weight, gate_full, up_full, down_full):
    gate_pre = jnp.dot(arrived_rows, gate_full, preferred_element_type=jnp.float32)
    up_pre = jnp.dot(arrived_rows, up_full, preferred_element_type=jnp.float32)
    sigmoid_gate = jax.nn.sigmoid(gate_pre)
    active = gate_pre * sigmoid_gate
    hidden = (active * up_pre).astype(jnp.bfloat16)
    expert_out = jnp.dot(hidden, down_full, preferred_element_type=jnp.float32)
    weight_grad = jnp.sum(expert_out * arrived_grads.astype(jnp.float32), axis=1).astype(
        jnp.bfloat16
    )
    scaled = (
        arrived_weight.astype(jnp.float32)[:, None] * arrived_grads.astype(jnp.float32)
    ).astype(jnp.bfloat16)
    hidden_grad = contract_last(scaled, down_full)
    gate_grad = (
        hidden_grad * up_pre * sigmoid_gate * (1.0 + gate_pre * (1.0 - sigmoid_gate))
    ).astype(jnp.bfloat16)
    up_grad = (hidden_grad * active).astype(jnp.bfloat16)
    back_rows = (contract_last(gate_grad, gate_full) + contract_last(up_grad, up_full)).astype(
        jnp.bfloat16
    )
    part_gate = contract_rows(arrived_rows, gate_grad)
    part_up = contract_rows(arrived_rows, up_grad)
    part_down = contract_rows(hidden, scaled)
    return (back_rows, weight_grad, part_gate, part_up, part_down)


def body(tokens, expert_ids, combine, upstream, w_gate, w_up, w_down):
    expert_count = lax.axis_size("expert")
    slot_cap = max(4 * TOK_MB // expert_count, 2)
    slot_count = expert_count * slot_cap
    feature_width = tokens.shape[2]
    gate_all, up_all, down_all = (
        lax.all_gather(w_gate, "dp", axis=2, tiled=True),
        lax.all_gather(w_up, "dp", axis=2, tiled=True),
        lax.all_gather(w_down, "dp", axis=3, tiled=True),
    )
    gate_full = gate_all[0, 0]
    up_full = up_all[0, 0]
    down_full = down_all[0, 0]
    micro_count = tokens.shape[1] // TOK_MB
    table_list = []
    send_list = []
    for block_index in range(micro_count):
        first_row = block_index * TOK_MB
        picked = build_table(expert_ids[0, first_row : first_row + TOK_MB], expert_count, slot_cap)
        token_table = picked[:, 0] + picked[:, 1]
        send_rows = contract_rows(token_table, tokens[0, first_row : first_row + TOK_MB]).astype(
            jnp.bfloat16
        )
        send_grads = contract_rows(token_table, upstream[0, first_row : first_row + TOK_MB]).astype(
            jnp.bfloat16
        )
        send_weight = jnp.einsum(
            "tkc,tk->c",
            picked,
            combine[0, first_row : first_row + TOK_MB],
            preferred_element_type=jnp.float32,
        ).astype(jnp.bfloat16)
        table_list.append((picked, token_table))
        send_list.append(
            (
                send_rows.reshape(expert_count, slot_cap, feature_width),
                send_grads.reshape(expert_count, slot_cap, feature_width),
                send_weight.reshape(expert_count, slot_cap),
            )
        )
    results = []
    partial_list = []
    for block_index in range(micro_count):
        send_rows, send_grads, send_weight = send_list[block_index]
        arrived_rows, arrived_grads, arrived_weight = (
            lax.all_to_all(send_rows, "expert", split_axis=0, concat_axis=0, tiled=True),
            lax.all_to_all(send_grads, "expert", split_axis=0, concat_axis=0, tiled=True),
            lax.all_to_all(send_weight, "expert", split_axis=0, concat_axis=0, tiled=True),
        )
        outcome = expert_pass(
            arrived_rows.reshape(slot_count, feature_width),
            arrived_grads.reshape(slot_count, feature_width),
            arrived_weight.reshape(slot_count),
            gate_full,
            up_full,
            down_full,
        )
        back_send = outcome[0].reshape(expert_count, slot_cap, feature_width)
        weight_send = outcome[1].reshape(expert_count, slot_cap)
        back_rows, back_weight = (
            lax.all_to_all(back_send, "expert", split_axis=0, concat_axis=0, tiled=True),
            lax.all_to_all(weight_send, "expert", split_axis=0, concat_axis=0, tiled=True),
        )
        finish_picked, finish_token_table = table_list[block_index]
        token_grad = jnp.dot(
            finish_token_table,
            back_rows.reshape(slot_count, feature_width),
            preferred_element_type=jnp.float32,
        ).astype(jnp.bfloat16)
        weight_out = jnp.einsum(
            "tkc,c->tk",
            finish_picked,
            back_weight.reshape(slot_count),
            preferred_element_type=jnp.float32,
        ).astype(jnp.bfloat16)
        results.append((token_grad, weight_out))
        partial_list.append(outcome[2:])
    part_gate = partial_list[0][0]
    part_up = partial_list[0][1]
    part_down = partial_list[0][2]
    for member in partial_list[1:]:
        part_gate = part_gate + member[0]
        part_up = part_up + member[1]
        part_down = part_down + member[2]
    token_grads = jnp.concatenate([member[0] for member in results], axis=0)
    token_grads = passed_along(token_grads, "section", -1)
    weight_outs = jnp.concatenate([member[1] for member in results], axis=0)
    grad_gate, grad_up, grad_down = (
        lax.psum_scatter(
            part_gate.astype(jnp.bfloat16), "dp", scatter_dimension=0, tiled=True
        ).astype(jnp.float32),
        lax.psum_scatter(
            part_up.astype(jnp.bfloat16), "dp", scatter_dimension=0, tiled=True
        ).astype(jnp.float32),
        lax.psum_scatter(
            part_down.astype(jnp.bfloat16), "dp", scatter_dimension=1, tiled=True
        ).astype(jnp.float32),
    )
    return (
        token_grads[None],
        weight_outs[None],
        grad_gate.astype(jnp.bfloat16)[None, None],
        grad_up.astype(jnp.bfloat16)[None, None],
        grad_down.astype(jnp.bfloat16)[None, None],
    )


def solution(mesh):
    return jax.shard_map(
        body,
        mesh=mesh,
        in_specs=(
            P("section", ("expert", "dp"), None),
            P("section", ("expert", "dp"), None),
            P("section", ("expert", "dp"), None),
            P("section", ("expert", "dp"), None),
            P("section", "expert", "dp", None),
            P("section", "expert", "dp", None),
            P("section", "expert", None, "dp"),
        ),
        out_specs=(
            P("section", ("expert", "dp"), None),
            P("section", ("expert", "dp"), None),
            P("section", "expert", "dp", None),
            P("section", "expert", "dp", None),
            P("section", "expert", None, "dp"),
        ),
        check_vma=False,
    )
```

profile of v0, /device:TPU:32, one launch (start us, length us, event | category | flops | bytes accessed | tf_op | source)
XLA Modules:
  0.0 357.6 jit_solution(13981431306722404856)
XLA Ops:
  12.4 12.7 %all-to-all-start.4 = ((bf16[64,1,4]{2,1,0:T(2,128)(2,1)}), bf16[64,1,4]{2,1,0:T(2,128)(2,1)S(1)}, u32[]{:S(2)}, u32[]{:S(2)}) async-start(bf16[64,1,4]{2,1,0:T(2,128)(2,1)} %all_to_all.51), calls=%async_computation.4 | async-start | bytes 65536 | tf_op jit(solution)/shard_map/all_to_all | solution.py:112
  26.2 8.4 %all-to-all-done.4 = bf16[64,1,4]{2,1,0:T(2,128)(2,1)S(1)} async-done(((bf16[64,1,4]{2,1,0:T(2,128)(2,1)}), bf16[64,1,4]{2,1,0:T(2,128)(2,1)S(1)}, u32[]{:S(2)}, u32[]{:S(2)}) %all-to-all-start.4) | async-done | bytes 544 | tf_op jit(solution)/shard_map/all_to_all | solution.py:112
  34.5 5.5 %all-to-all-start = ((bf16[64,1,4]{2,1,0:T(2,128)(2,1)}), bf16[64,1,4]{2,1,0:T(2,128)(2,1)S(1)}, u32[]{:S(2)}, u32[]{:S(2)}) async-start(bf16[64,1,4]{2,1,0:T(2,128)(2,1)} %all_to_all.50), calls=%async_computation | async-start | bytes 65536 | tf_op jit(solution)/shard_map/all_to_all | solution.py:112
  40.0 1.6 convolution_convert_fusion
  41.6 1.5 reshape.228
  43.1 6.4 %all-to-all-done = bf16[64,1,4]{2,1,0:T(2,128)(2,1)S(1)} async-done(((bf16[64,1,4]{2,1,0:T(2,128)(2,1)}), bf16[64,1,4]{2,1,0:T(2,128)(2,1)S(1)}, u32[]{:S(2)}, u32[]{:S(2)}) %all-to-all-start) | async-done | bytes 544 | tf_op jit(solution)/shard_map/all_to_all | solution.py:112
  49.5 5.6 %all-to-all-start.6 = ((bf16[64,4,3072]{2,1,0:T(4,128)(2,1)}), bf16[64,4,3072]{2,1,0:T(4,128)(2,1)S(1)}, u32[]{:S(2)}, u32[]{:S(2)}) async-start(bf16[64,4,3072]{2,1,0:T(4,128)(2,1)} %reshape.228), calls=%async_computation.6 | async-start | bytes 3145728 | tf_op jit(solution)/shard_map/all_to_all | solution.py:110
  55.1 1.6 convolution_convert_fusion.1
  56.7 1.5 reshape.227
  58.2 34.4 %all-to-all-done.6 = bf16[64,4,3072]{2,1,0:T(4,128)(2,1)S(1)} async-done(((bf16[64,4,3072]{2,1,0:T(4,128)(2,1)}), bf16[64,4,3072]{2,1,0:T(4,128)(2,1)S(1)}, u32[]{:S(2)}, u32[]{:S(2)}) %all-to-all-start.6) | async-done | bytes 1572896 | tf_op jit(solution)/shard_map/all_to_all | solution.py:110
  93.7 6.2 %all-to-all-start.5 = ((bf16[64,4,3072]{2,1,0:T(4,128)(2,1)}), bf16[64,4,3072]{2,1,0:T(4,128)(2,1)S(1)}, u32[]{:S(2)}, u32[]{:S(2)}) async-start(bf16[64,4,3072]{2,1,0:T(4,128)(2,1)} %reshape.227), calls=%async_computation.5 | async-start | bytes 3145728 | tf_op jit(solution)/shard_map/all_to_all | solution.py:111
  100.1 1.6 convolution_convert_fusion.2
  103.1 34.5 %all-to-all-done.5 = bf16[64,4,3072]{2,1,0:T(4,128)(2,1)S(1)} async-done(((bf16[64,4,3072]{2,1,0:T(4,128)(2,1)}), bf16[64,4,3072]{2,1,0:T(4,128)(2,1)S(1)}, u32[]{:S(2)}, u32[]{:S(2)}) %all-to-all-start.5) | async-done | bytes 1572896 | tf_op jit(solution)/shard_map/all_to_all | solution.py:111
  137.7 6.2 %all-to-all-start.2 = ((bf16[64,4,3072]{2,1,0:T(4,128)(2,1)}), bf16[64,4,3072]{2,1,0:T(4,128)(2,1)S(1)}, u32[]{:S(2)}, u32[]{:S(2)}) async-start(bf16[64,4,3072]{2,1,0:T(4,128)(2,1)} %reshape.223), calls=%async_computation.2 | async-start | bytes 3145728 | tf_op jit(solution)/shard_map/all_to_all | solution.py:110
  143.9 2.7 convolution_convert_fusion.3
  146.7 3.9 %reshape.222 = bf16[64,4,3072]{2,1,0:T(4,128)(2,1)} reshape(bf16[256,3072]{1,0:T(8,128)(2,1)} %convolution_convert_fusion.3) | data formatting | bytes 3145728 | tf_op jit(solution)/shard_map/reshape | solution.py:101
  150.5 31.1 %all-to-all-done.2 = bf16[64,4,3072]{2,1,0:T(4,128)(2,1)S(1)} async-done(((bf16[64,4,3072]{2,1,0:T(4,128)(2,1)}), bf16[64,4,3072]{2,1,0:T(4,128)(2,1)S(1)}, u32[]{:S(2)}, u32[]{:S(2)}) %all-to-all-start.2) | async-done | bytes 1572896 | tf_op jit(solution)/shard_map/all_to_all | solution.py:110
  182.8 6.4 %all-to-all-start.1 = ((bf16[64,4,3072]{2,1,0:T(4,128)(2,1)}), bf16[64,4,3072]{2,1,0:T(4,128)(2,1)}, u32[]{:S(2)}, u32[]{:S(2)}) async-start(bf16[64,4,3072]{2,1,0:T(4,128)(2,1)} %reshape.222), calls=%async_computation.1 | async-start | bytes 3145728 | tf_op jit(solution)/shard_map/all_to_all | solution.py:111
  189.3 2.7 all_gather.11
  192.0 2.6 all_gather.9
  194.5 2.7 all_gather.10
  197.3 1.9 multiply_convert_fusion.2
  199.2 3.7 %convert_element_type.201 = bf16[256,3072]{1,0:T(8,128)(2,1)} reshape(bf16[64,4,3072]{2,1,0:T(4,128)(2,1)} %multiply_convert_fusion.2) | data formatting | bytes 3145728 | tf_op jit(solution)/shard_map/convert_element_type | solution.py:50
  202.9 2.7 reshape.229
  211.4 15.5 %all-to-all-done.1 = bf16[64,4,3072]{2,1,0:T(4,128)(2,1)} async-done(((bf16[64,4,3072]{2,1,0:T(4,128)(2,1)}), bf16[64,4,3072]{2,1,0:T(4,128)(2,1)}, u32[]{:S(2)}, u32[]{:S(2)}) %all-to-all-start.1) | async-done | bytes 1572896 | tf_op jit(solution)/shard_map/all_to_all | solution.py:111
  226.9 6.4 %all-to-all-start.7 = ((bf16[64,4,3072]{2,1,0:T(4,128)(2,1)}), bf16[64,4,3072]{2,1,0:T(4,128)(2,1)}, u32[]{:S(2)}, u32[]{:S(2)}) async-start(bf16[64,4,3072]{2,1,0:T(4,128)(2,1)} %reshape.230), calls=%async_computation.7 | async-start | bytes 3145728 | tf_op jit(solution)/shard_map/all_to_all | solution.py:125
  233.7 2.2 multiply_convert_fusion.3
  237.3 2.7 reshape.224
  240.0 1.8 fusion.16
  245.5 1.5 fusion.2
  247.1 1.8 fusion.14
  248.9 1.8 fusion
  250.7 3.8 %reshape.225 = bf16[64,4,3072]{2,1,0:T(4,128)(2,1)} reshape(bf16[256,3072]{1,0:T(8,128)(2,1)} %fusion) | data formatting | bytes 3145728 | tf_op jit(solution)/shard_map/reshape | solution.py:122
  254.6 16.5 %all-to-all-done.7 = bf16[64,4,3072]{2,1,0:T(4,128)(2,1)} async-done(((bf16[64,4,3072]{2,1,0:T(4,128)(2,1)}), bf16[64,4,3072]{2,1,0:T(4,128)(2,1)}, u32[]{:S(2)}, u32[]{:S(2)}) %all-to-all-start.7) | async-done | bytes 1572896 | tf_op jit(solution)/shard_map/all_to_all | solution.py:125
  271.1 6.4 %all-to-all-start.3 = ((bf16[64,4,3072]{2,1,0:T(4,128)(2,1)}), bf16[64,4,3072]{2,1,0:T(4,128)(2,1)}, u32[]{:S(2)}, u32[]{:S(2)}) async-start(bf16[64,4,3072]{2,1,0:T(4,128)(2,1)} %reshape.225), calls=%async_computation.3 | async-start | bytes 3145728 | tf_op jit(solution)/shard_map/all_to_all | solution.py:125
  278.2 1.5 fusion.3
  280.4 2.6 reshape.237
  283.1 1.8 fusion.9
  285.6 3.9 %reshape.236 = f32[256,3072]{1,0:T(8,128)} reshape(bf16[64,4,3072]{2,1,0:T(4,128)(2,1)} %all-to-all-done.1) | data formatting | bytes 4718592 | tf_op jit(solution)/shard_map/convert_element_type | solution.py:49
  289.5 2.3 fusion.5
  293.3 2.8 reshape.231
  296.5 18.8 %all-to-all-done.3 = bf16[64,4,3072]{2,1,0:T(4,128)(2,1)} async-done(((bf16[64,4,3072]{2,1,0:T(4,128)(2,1)}), bf16[64,4,3072]{2,1,0:T(4,128)(2,1)}, u32[]{:S(2)}, u32[]{:S(2)}) %all-to-all-start.3) | async-done | bytes 1572896 | tf_op jit(solution)/shard_map/all_to_all | solution.py:125
  315.3 6.2 %all-to-all-start.9 = ((bf16[64,1,4]{2,1,0:T(2,128)(2,1)}), bf16[64,1,4]{2,1,0:T(2,128)(2,1)S(1)}, u32[]{:S(2)}, u32[]{:S(2)}) async-start(bf16[64,1,4]{2,1,0:T(2,128)(2,1)} %convert_element_type.235), calls=%async_computation.9 | async-start | bytes 65536 | tf_op jit(solution)/shard_map/all_to_all | solution.py:126
  321.5 2.8 reshape.226
  324.8 2.8 collective-permute-start
  329.0 2.0 all-to-all-done.9
  331.0 8.6 %all-to-all-start.8 = ((bf16[64,1,4]{2,1,0:T(2,128)(2,1)}), bf16[64,1,4]{2,1,0:T(2,128)(2,1)S(1)}, u32[]{:S(2)}, u32[]{:S(2)}) async-start(bf16[64,1,4]{2,1,0:T(2,128)(2,1)} %convert_element_type.234), calls=%async_computation.8 | async-start | bytes 65536 | tf_op jit(solution)/shard_map/all_to_all | solution.py:126
  340.1 9.0 %all-to-all-done.8 = bf16[64,1,4]{2,1,0:T(2,128)(2,1)S(1)} async-done(((bf16[64,1,4]{2,1,0:T(2,128)(2,1)}), bf16[64,1,4]{2,1,0:T(2,128)(2,1)S(1)}, u32[]{:S(2)}, u32[]{:S(2)}) %all-to-all-start.8) | async-done | bytes 544 | tf_op jit(solution)/shard_map/all_to_all | solution.py:126
  (104 shorter events, 29.4 us)
Async XLA Ops:
  12.4 22.1 %all-to-all-start.4 = ((bf16[64,1,4]{2,1,0:T(2,128)(2,1)}), bf16[64,1,4]{2,1,0:T(2,128)(2,1)S(1)}, u32[]{:S(2)}, u32[]{:S(2)}) async-start(bf16[64,1,4]{2,1,0:T(2,128)(2,1)} %all_to_all.51), calls=%async_computation.4 | async-start | bytes 65536 | tf_op jit(solution)/shard_map/all_to_all | solution.py:112
  34.5 15.0 %all-to-all-start = ((bf16[64,1,4]{2,1,0:T(2,128)(2,1)}), bf16[64,1,4]{2,1,0:T(2,128)(2,1)S(1)}, u32[]{:S(2)}, u32[]{:S(2)}) async-start(bf16[64,1,4]{2,1,0:T(2,128)(2,1)} %all_to_all.50), calls=%async_computation | async-start | bytes 65536 | tf_op jit(solution)/shard_map/all_to_all | solution.py:112
  49.5 43.1 %all-to-all-start.6 = ((bf16[64,4,3072]{2,1,0:T(4,128)(2,1)}), bf16[64,4,3072]{2,1,0:T(4,128)(2,1)S(1)}, u32[]{:S(2)}, u32[]{:S(2)}) async-start(bf16[64,4,3072]{2,1,0:T(4,128)(2,1)} %reshape.228), calls=%async_computation.6 | async-start | bytes 3145728 | tf_op jit(solution)/shard_map/all_to_all | solution.py:110
  92.6 1.1 copy-start.10
  93.7 44.0 %all-to-all-start.5 = ((bf16[64,4,3072]{2,1,0:T(4,128)(2,1)}), bf16[64,4,3072]{2,1,0:T(4,128)(2,1)S(1)}, u32[]{:S(2)}, u32[]{:S(2)}) async-start(bf16[64,4,3072]{2,1,0:T(4,128)(2,1)} %reshape.227), calls=%async_computation.5 | async-start | bytes 3145728 | tf_op jit(solution)/shard_map/all_to_all | solution.py:111
  137.7 59.6 %copy-start.5 = (bf16[64,4,3072]{2,1,0:T(4,128)(2,1)}, bf16[64,4,3072]{2,1,0:T(4,128)(2,1)S(1)}, u32[]{:S(2)}) copy-start(bf16[64,4,3072]{2,1,0:T(4,128)(2,1)S(1)} %all-to-all-done.5) | copy-start | bytes 4718596
  137.7 44.0 %all-to-all-start.2 = ((bf16[64,4,3072]{2,1,0:T(4,128)(2,1)}), bf16[64,4,3072]{2,1,0:T(4,128)(2,1)S(1)}, u32[]{:S(2)}, u32[]{:S(2)}) async-start(bf16[64,4,3072]{2,1,0:T(4,128)(2,1)} %reshape.223), calls=%async_computation.2 | async-start | bytes 3145728 | tf_op jit(solution)/shard_map/all_to_all | solution.py:110
  181.7 1.1 copy-start.9
  182.8 44.1 %all-to-all-start.1 = ((bf16[64,4,3072]{2,1,0:T(4,128)(2,1)}), bf16[64,4,3072]{2,1,0:T(4,128)(2,1)}, u32[]{:S(2)}, u32[]{:S(2)}) async-start(bf16[64,4,3072]{2,1,0:T(4,128)(2,1)} %reshape.222), calls=%async_computation.1 | async-start | bytes 3145728 | tf_op jit(solution)/shard_map/all_to_all | solution.py:111
  189.2 5.3 %copy-start.13 = (bf16[1,1,1536,128]{3,2,1,0:T(8,128)(2,1)S(1)}, bf16[1,1,1536,128]{3,2,1,0:T(8,128)(2,1)}, u32[]{:S(2)}) copy-start(bf16[1,1,1536,128]{3,2,1,0:T(8,128)(2,1)} %param.12) | copy-start | bytes 1179652
  192.0 16.8 %copy-start.4 = (bf16[1,1,3072,128]{3,2,1,0:T(8,128)(2,1)}, bf16[1,1,3072,128]{3,2,1,0:T(8,128)(2,1)S(1)}, u32[]{:S(2)}) copy-start(bf16[1,1,3072,128]{3,2,1,0:T(8,128)(2,1)S(1)} %all_gather.11) | copy-start | bytes 2359300
  194.5 11.7 %copy-start.1 = (bf16[1,1,128,3072]{3,2,1,0:T(8,128)(2,1)}, bf16[1,1,128,3072]{3,2,1,0:T(8,128)(2,1)S(1)}, u32[]{:S(2)}) copy-start(bf16[1,1,128,3072]{3,2,1,0:T(8,128)(2,1)S(1)} %all_gather.9) | copy-start | bytes 2359300
  205.6 1.4 copy-start.11
  207.1 1.1 copy-start.6
  226.9 44.1 %all-to-all-start.7 = ((bf16[64,4,3072]{2,1,0:T(4,128)(2,1)}), bf16[64,4,3072]{2,1,0:T(4,128)(2,1)}, u32[]{:S(2)}, u32[]{:S(2)}) async-start(bf16[64,4,3072]{2,1,0:T(4,128)(2,1)} %reshape.230), calls=%async_computation.7 | async-start | bytes 3145728 | tf_op jit(solution)/shard_map/all_to_all | solution.py:125
  233.4 116.8 %reduce-scatter.4.cloned.1.call-start = ((), (), s32[]{:S(2)}) async-start(), calls=%async_computation.13 | async-start | bytes 1179648 | tf_op jit(solution)/shard_map/reduce_scatter | solution.py:153
  240.0 1.9 copy-start.2
  240.0 1.9 copy-start.12
  241.9 1.1 copy-start.7
  244.2 0.6 copy-start.15
  247.0 1.8 copy-start.8
  247.0 1.8 copy-start.14
  271.1 44.2 %all-to-all-start.3 = ((bf16[64,4,3072]{2,1,0:T(4,128)(2,1)}), bf16[64,4,3072]{2,1,0:T(4,128)(2,1)}, u32[]{:S(2)}, u32[]{:S(2)}) async-start(bf16[64,4,3072]{2,1,0:T(4,128)(2,1)} %reshape.225), calls=%async_computation.3 | async-start | bytes 3145728 | tf_op jit(solution)/shard_map/all_to_all | solution.py:125
  277.5 72.7 %reduce-scatter.6.cloned.1.call-start = ((), (), s32[]{:S(2)}) async-start(), calls=%async_computation.14 | async-start | bytes 1179648 | tf_op jit(solution)/shard_map/reduce_scatter | solution.py:156
  279.7 70.5 %reduce-scatter.8.cloned.1.call-start = ((), (), s32[]{:S(2)}) async-start(), calls=%async_computation.15 | async-start | bytes 1179648 | tf_op jit(solution)/shard_map/reduce_scatter | solution.py:159
  285.6 3.9 %copy-start.16 = (bf16[256,128]{1,0:T(8,128)(2,1)S(1)}, bf16[256,128]{1,0:T(8,128)(2,1)}, u32[]{:S(2)}) copy-start(bf16[256,128]{1,0:T(8,128)(2,1)} %get-tuple-element.5) | copy-start | bytes 196612
  315.3 15.7 %all-to-all-start.9 = ((bf16[64,1,4]{2,1,0:T(2,128)(2,1)}), bf16[64,1,4]{2,1,0:T(2,128)(2,1)S(1)}, u32[]{:S(2)}, u32[]{:S(2)}) async-start(bf16[64,1,4]{2,1,0:T(2,128)(2,1)} %convert_element_type.235), calls=%async_computation.9 | async-start | bytes 65536 | tf_op jit(solution)/shard_map/all_to_all | solution.py:126
  321.5 6.1 %copy-start.3 = (bf16[1,1,128,3072]{3,2,1,0:T(8,128)(2,1)S(1)}, bf16[1,1,128,3072]{3,2,1,0:T(8,128)(2,1)}, u32[]{:S(2)}) copy-start(bf16[1,1,128,3072]{3,2,1,0:T(8,128)(2,1)} %copy-done.1) | copy-start | bytes 2359300
  324.3 3.3 copy-start
  324.8 25.4 %collective-permute-start = (bf16[128,3072]{1,0:T(8,128)(2,1)S(1)}, bf16[128,3072]{1,0:T(8,128)(2,1)S(1)}, u32[]{:S(2)}, u32[]{:S(2)}) collective-permute-start(bf16[128,3072]{1,0:T(8,128)(2,1)S(1)} %pad_maximum_fusion), channel_id=1, source_target_pairs={{0,128},{128,0},{1,129},{129,1},{2,130},{130,2},{3,131},{131,3},{4... | collective-permute-start | bytes 2359304 | tf_op jit(solution)/shard_map/ppermute | solution.py:11
  331.0 18.1 %all-to-all-start.8 = ((bf16[64,1,4]{2,1,0:T(2,128)(2,1)}), bf16[64,1,4]{2,1,0:T(2,128)(2,1)S(1)}, u32[]{:S(2)}, u32[]{:S(2)}) async-start(bf16[64,1,4]{2,1,0:T(2,128)(2,1)} %convert_element_type.234), calls=%async_computation.8 | async-start | bytes 65536 | tf_op jit(solution)/shard_map/all_to_all | solution.py:126
Sparse Core Ops, SparseCore 0:
  247.2 14.4 reduce-scatter.3
  281.6 14.4 reduce-scatter.5
  299.1 14.8 reduce-scatter.7
where the time goes:
time: 360 us; the launch traced here: 358 us
  waiting for transfers between devices  177 us (49%)
  starting transfers between devices  73.8 us (20%)
  local copies, waits for them, and re-layouts  48.2 us (13%)
  matrix products  29.7 us (8%)
  between operations  14.2 us (4%)
  blocking collectives  7.95 us (2%)
  other arithmetic  7.07 us (2%)
    all_to_all x2, waiting for transfers between devices, body(): lax.all_to_all(send_rows, 'expert', split_axis=0, concat_axis=0, tiled=True)  65.5 us
    all_to_all x2, waiting for transfers between devices, body(): lax.all_to_all(send_grads, 'expert', split_axis=0, concat_axis=0, tiled=T...  50.1 us
    all_to_all x2, waiting for transfers between devices, body(): lax.all_to_all(back_send, 'expert', split_axis=0, concat_axis=0, tiled=True)  35.3 us
    all_to_all x2, starting transfers between devices, body(): lax.all_to_all(send_weight, 'expert', split_axis=0, concat_axis=0, tiled=...  18.2 us
    dot_general x10, matrix products, contract_rows(): lax.dot_general(former, latter, (((0,), (0,)), ((), ())), preferred_eleme...  15.5 us
    all_to_all x2, starting transfers between devices, body(): lax.all_to_all(weight_send, 'expert', split_axis=0, concat_axis=0, tiled=...  14.9 us
    all_to_all x2, waiting for transfers between devices, body(): lax.all_to_all(send_weight, 'expert', split_axis=0, concat_axis=0, tiled=...  14.8 us
    all_to_all x2, starting transfers between devices, body(): lax.all_to_all(back_send, 'expert', split_axis=0, concat_axis=0, tiled=True)  12.8 us
  transfers between devices with their start and end apart: 14, of which 10 were waited for; matrix products, arithmetic and copies ran while one was open for 20% of the time, Pallas kernels for 0%

commit v1 on v0

v1 whole, which is shorter than its diff:
```python
import functools

import jax
import jax.numpy as jnp
from jax import lax
from jax.experimental import pallas as pl
from jax.experimental.pallas import tpu as pltpu
from jax.sharding import PartitionSpec as P

TOK_MB = 64
CAP = 4
LANES = 128
VMEM_LIMIT = 48 * 1024 * 1024


def contract_rows(former, latter):
    return lax.dot_general(
        former, latter, (((0,), (0,)), ((), ())), preferred_element_type=jnp.float32
    )


def dispatch_kernel(slots, x_steps, ids_ref, comb_ref, tok_ref, up_ref, out_ref, pick_ref, plain, scaled):
    step = pl.program_id(0)
    rows = ids_ref.shape[0]
    per_expert = slots * CAP

    @pl.when(step == 0)
    def _():
        ids = ids_ref[...]
        first, second = ids[:, 0:1], ids[:, 1:2]
        label = lax.broadcasted_iota(jnp.int32, (rows, LANES), 1)
        hit0 = (first == label).astype(jnp.float32)
        hit1 = (second == label).astype(jnp.float32)
        row = lax.broadcasted_iota(jnp.int32, (rows, rows), 0)
        col = lax.broadcasted_iota(jnp.int32, (rows, rows), 1)
        before = ((col < row) & (col // TOK_MB == row // TOK_MB)).astype(jnp.bfloat16)
        earlier = jnp.dot(
            before, (hit0 + hit1).astype(jnp.bfloat16), preferred_element_type=jnp.float32
        )
        place0 = jnp.sum(earlier * hit0, axis=1, keepdims=True).astype(jnp.int32)
        place1 = jnp.sum(earlier * hit1, axis=1, keepdims=True).astype(jnp.int32)
        block = lax.broadcasted_iota(jnp.int32, (rows, 1), 0) // TOK_MB
        width = pick_ref.shape[1]
        column = lax.broadcasted_iota(jnp.int32, (rows, width), 1)
        table0 = (first * per_expert + block * CAP + place0 == column).astype(jnp.float32)
        table1 = (second * per_expert + block * CAP + place1 == column).astype(jnp.float32)
        comb = comb_ref[...].astype(jnp.float32)
        plain[...] = (table0 + table1).astype(jnp.bfloat16)
        scaled[...] = (table0 * comb[:, 0:1] + table1 * comb[:, 1:2]).astype(jnp.bfloat16)
        pick_ref[0:rows, :] = table0.astype(jnp.bfloat16)
        pick_ref[rows : 2 * rows, :] = table1.astype(jnp.bfloat16)

    @pl.when(step < x_steps)
    def _():
        out_ref[...] = contract_rows(plain[...], tok_ref[...]).astype(jnp.bfloat16)

    @pl.when(step >= x_steps)
    def _():
        out_ref[...] = contract_rows(scaled[...], up_ref[...]).astype(jnp.bfloat16)


def dispatch(ids, comb, tok, up, expert_count):
    rows, width = tok.shape
    slots = rows // TOK_MB
    total = expert_count * slots * CAP
    tile = 1024
    steps = width // tile
    return pl.pallas_call(
        functools.partial(dispatch_kernel, slots, steps),
        grid=(2 * steps,),
        in_specs=[
            pl.BlockSpec((rows, 2), lambda i: (0, 0)),
            pl.BlockSpec((rows, 2), lambda i: (0, 0)),
            pl.BlockSpec((rows, tile), lambda i: (0, jnp.minimum(i, steps - 1))),
            pl.BlockSpec((rows, tile), lambda i: (0, jnp.maximum(i - steps, 0))),
        ],
        out_specs=[
            pl.BlockSpec((total, tile), lambda i: (0, i)),
            pl.BlockSpec((2 * rows, total), lambda i: (0, 0)),
        ],
        out_shape=[
            jax.ShapeDtypeStruct((total, 2 * width), jnp.bfloat16),
            jax.ShapeDtypeStruct((2 * rows, total), jnp.bfloat16),
        ],
        scratch_shapes=[
            pltpu.VMEM((rows, total), jnp.bfloat16),
            pltpu.VMEM((rows, total), jnp.bfloat16),
        ],
        compiler_params=pltpu.CompilerParams(vmem_limit_bytes=VMEM_LIMIT),
        name="dispatch_rows",
    )(ids, comb, tok, up)


def expert_kernel(cut, row_ref, wgu_ref, wgu_t_ref, wd_t_ref, out0_ref, out1_ref, act_ref):
    width = wgu_ref.shape[0]
    hid = wd_t_ref.shape[1]
    pre = jnp.dot(row_ref[:, :width], wgu_ref[...], preferred_element_type=jnp.float32)
    hidden_grad = jnp.dot(row_ref[:, width:], wd_t_ref[...], preferred_element_type=jnp.float32)
    gate_pre, up_pre = pre[:, :hid], pre[:, hid:]
    sig = jax.nn.sigmoid(gate_pre)
    active = gate_pre * sig
    hidden = (active * up_pre).astype(jnp.bfloat16)
    gate_grad = (hidden_grad * up_pre * sig * (1.0 + gate_pre * (1.0 - sig))).astype(jnp.bfloat16)
    up_grad = (hidden_grad * active).astype(jnp.bfloat16)
    both = jnp.concatenate([gate_grad, up_grad], axis=1)
    act_ref[:, :hid] = hidden
    act_ref[:, hid:] = both
    weight = jnp.sum(hidden.astype(jnp.float32) * hidden_grad, axis=1, keepdims=True)
    out0_ref[...] = jnp.dot(
        both, wgu_t_ref[:, :cut], preferred_element_type=jnp.float32
    ).astype(jnp.bfloat16)
    out1_ref[:, : width - cut] = jnp.dot(
        both, wgu_t_ref[:, cut:], preferred_element_type=jnp.float32
    ).astype(jnp.bfloat16)
    out1_ref[:, width - cut :] = jnp.broadcast_to(weight, (weight.shape[0], LANES)).astype(
        jnp.bfloat16
    )


def expert_pass(rows, wgu, wgu_t, wd_t, cut):
    count = rows.shape[0]
    width, pair = wgu.shape
    hid = wd_t.shape[1]
    tile = 128
    return pl.pallas_call(
        functools.partial(expert_kernel, cut),
        grid=(count // tile,),
        in_specs=[
            pl.BlockSpec((tile, 2 * width), lambda i: (i, 0)),
            pl.BlockSpec((width, pair), lambda i: (0, 0)),
            pl.BlockSpec((pair, width), lambda i: (0, 0)),
            pl.BlockSpec((width, hid), lambda i: (0, 0)),
        ],
        out_specs=[
            pl.BlockSpec((tile, cut), lambda i: (i, 0)),
            pl.BlockSpec((tile, width - cut + LANES), lambda i: (i, 0)),
            pl.BlockSpec((tile, hid + pair), lambda i: (i, 0)),
        ],
        out_shape=[
            jax.ShapeDtypeStruct((count, cut), jnp.bfloat16),
            jax.ShapeDtypeStruct((count, width - cut + LANES), jnp.bfloat16),
            jax.ShapeDtypeStruct((count, hid + pair), jnp.bfloat16),
        ],
        compiler_params=pltpu.CompilerParams(vmem_limit_bytes=VMEM_LIMIT),
        name="expert_rows",
    )(rows, wgu, wgu_t, wd_t)


def exchanged(array, axis_name):
    return lax.all_to_all(array, axis_name, split_axis=0, concat_axis=0, tiled=True)


def summed_over_dp(part, dim):
    half = part.shape[dim] // 2
    me = lax.axis_index("dp")
    mine = lax.dynamic_slice_in_dim(part, me * half, half, dim)
    other = lax.dynamic_slice_in_dim(part, (1 - me) * half, half, dim)
    came = lax.ppermute(other, "dp", [(0, 1), (1, 0)])
    return (mine.astype(jnp.float32) + came.astype(jnp.float32)).astype(jnp.bfloat16)


def body(tokens, expert_ids, combine, upstream, w_gate, w_up, w_down):
    expert_count = lax.axis_size("expert")
    sections = lax.axis_size("section")
    width = tokens.shape[2]
    rows = tokens.shape[1]
    per_expert = rows // TOK_MB * CAP
    cut = width * 3 // 4
    back_by_one = [(i, (i - 1) % sections) for i in range(sections)]

    send, pick = dispatch(expert_ids[0], combine[0], tokens[0], upstream[0], expert_count)
    came = exchanged(send.reshape(expert_count, per_expert, 2 * width), "expert")
    came = came.reshape(expert_count * per_expert, 2 * width)

    gate_full = lax.all_gather(w_gate[0, 0], "dp", axis=0, tiled=True)
    up_full = lax.all_gather(w_up[0, 0], "dp", axis=0, tiled=True)
    down_full = lax.all_gather(w_down[0, 0], "dp", axis=1, tiled=True)
    wgu = jnp.concatenate([gate_full, up_full], axis=1)
    wgu_t = wgu.T
    wd_t = down_full.T

    out0, out1, acts = expert_pass(came, wgu, wgu_t, wd_t, cut)
    hid = wd_t.shape[1]

    back0 = exchanged(out0.reshape(expert_count, per_expert, cut), "expert")
    out1 = out1.reshape(expert_count, per_expert, width - cut + LANES)
    out1, back0 = lax.optimization_barrier((out1, back0))
    back1 = exchanged(out1, "expert")

    both_picks = pick[:rows] + pick[rows:]
    grad0 = jnp.dot(
        both_picks, back0.reshape(-1, cut), preferred_element_type=jnp.float32
    ).astype(jnp.bfloat16)
    grad0 = lax.ppermute(grad0, "section", back_by_one)
    tail = jnp.dot(
        pick, back1.reshape(-1, width - cut + LANES), preferred_element_type=jnp.float32
    )
    grad1 = (tail[:rows, : width - cut] + tail[rows:, : width - cut]).astype(jnp.bfloat16)
    grad1 = lax.ppermute(grad1, "section", back_by_one)
    weight = jnp.stack([tail[:rows, width - cut], tail[rows:, width - cut]], axis=1)
    grad_combine = (weight / combine[0].astype(jnp.float32)).astype(jnp.bfloat16)

    part_gu = contract_rows(came[:, :width], acts[:, hid:]).astype(jnp.bfloat16)
    part_down = contract_rows(acts[:, :hid], came[:, width:]).astype(jnp.bfloat16)
    grad_gu = summed_over_dp(part_gu, 0)
    grad_down = summed_over_dp(part_down, 1)
    return (
        jnp.concatenate([grad0, grad1], axis=1)[None],
        grad_combine[None],
        grad_gu[:, :hid][None, None],
        grad_gu[:, hid:][None, None],
        grad_down[None, None],
    )


def solution(mesh):
    return jax.shard_map(
        body,
        mesh=mesh,
        in_specs=(
            P("section", ("expert", "dp"), None),
            P("section", ("expert", "dp"), None),
            P("section", ("expert", "dp"), None),
            P("section", ("expert", "dp"), None),
            P("section", "expert", "dp", None),
            P("section", "expert", "dp", None),
            P("section", "expert", None, "dp"),
        ),
        out_specs=(
            P("section", ("expert", "dp"), None),
            P("section", ("expert", "dp"), None),
            P("section", "expert", "dp", None),
            P("section", "expert", "dp", None),
            P("section", "expert", None, "dp"),
        ),
        check_vma=False,
    )
```

time: 360 us -> 276 us (0.77)
  starting transfers between devices: 73.8 us -> 33.4 us
  local copies, waits for them, and re-layouts: 48.2 us -> 13.8 us
  matrix products: 29.7 us -> 7.14 us
  waiting for transfers between devices: 177 us -> 191 us
  between operations: 14.2 us -> 0.8 us
  Pallas kernels: 0 us -> 12.4 us
    all_to_all x10 -> x3, starting transfers between devices: 70.3 us -> 27.4 us  [exchanged(): lax.all_to_all(array, axis_name, split_axis=0, concat_axis=0, tiled=True)]
    reshape x12 -> x0, local copies, waits for them, and re-layouts: 24.9 us -> none  [the longest x2 5.59 us: body(): back_rows.reshape(slot_count, feature_width)]
    convert_element_type x8 -> x0, local copies, waits for them, and re-layouts: 13.4 us -> none  [the longest x2 6.57 us: expert_pass(): arrived_grads.astype(jnp.float32)]
    pallas_call x0 -> x2, Pallas kernels: none -> 12.4 us  [the longest x1 6.92 us: expert_pass(): pl.pallas_call(functools.partial(expert_kernel, cut), grid=(count // tile...]
    dot_general x18 -> x2, matrix products: 14.1 us -> 1.73 us  [the longest x1 1.3 us: body(): jnp.dot(both_picks, back0.reshape(-1, cut), preferred_element_type=jnp.fl...]
    all_to_all x10 -> x3, waiting for transfers between devices: 177 us -> 187 us  [exchanged(): lax.all_to_all(array, axis_name, split_axis=0, concat_axis=0, tiled=True)]
    dot_general x10 -> x2, matrix products: 15.5 us -> 5.41 us  [contract_rows(): lax.dot_general(former, latter, (((0,), (0,)), ((), ())), preferred_eleme...]
    ppermute x1 -> x4, waiting for transfers between devices: 0.01 us -> 3.82 us  [the longest x1 3.82 us: body(): grad1 = lax.ppermute(grad1, 'section', back_by_one)]
  transfers between devices with their start and end apart: 14 -> 7, of which waited for: 10 -> 4; matrix products, arithmetic and copies ran while one was open for 20% -> 7% of each run, Pallas kernels for 0% -> 0%
where the time goes in v1:
time: 276 us; the launch traced here: 274 us
  waiting for transfers between devices  191 us (69%)
  starting transfers between devices  33.4 us (12%)
  local copies, waits for them, and re-layouts  13.8 us (5%)
  Pallas kernels  12.4 us (4%)
  blocking collectives  8.78 us (3%)
  matrix products  7.14 us (3%)
  other arithmetic  6.61 us (2%)
    all_to_all x3, waiting for transfers between devices, exchanged(): lax.all_to_all(array, axis_name, split_axis=0, concat_axis=0, tiled=True)  187 us
    all_to_all x3, starting transfers between devices, exchanged(): lax.all_to_all(array, axis_name, split_axis=0, concat_axis=0, tiled=True)  27.4 us
    unnamed x25, local copies, waits for them, and re-layouts  9.28 us
    pallas_call x1, Pallas kernels, expert_pass(): pl.pallas_call(functools.partial(expert_kernel, cut), grid=(count // tile...  6.92 us
    pallas_call x1, Pallas kernels, dispatch(): pl.pallas_call(functools.partial(dispatch_kernel, slots, steps), grid=(2...  5.52 us
  transfers between devices with their start and end apart: 7, of which 4 were waited for; matrix products, arithmetic and copies ran while one was open for 7% of the time, Pallas kernels for 0%

profile of v1, /device:TPU:32, one launch (start us, length us, event | category | flops | bytes accessed | tf_op | source)
XLA Modules:
  0.0 274.2 jit_solution(14039294304388975557)
XLA Ops:
  0.6 0.8 copy.18
  1.4 0.8 copy.19
  2.2 1.1 copy-done.1
  3.3 1.1 copy-done.2
  4.5 5.5 %dispatch_rows.1 = (bf16[512,6144]{1,0:T(8,128)(2,1)}, bf16[256,512]{1,0:T(8,128)(2,1)S(1)}) custom-call(s32[128,2]{1,0:T(8,128)S(1)} %bitcast.35, bf16[128,2]{1,0:T(8,128)(2,1)S(1)} %bitcast.36, bf16[128,3072]{1,0:T(8,128)(2,1)S(1)} %bitcast.33, bf16[128,3072]{1,0:T(8,128)(2,1)S(1)} %bitcast.34), custom_call_target="tpu_custom_call" | custom-call | tf_op jit(solution)/shard_map/dispatch_rows/pallas_call | solution.py:68
  10.0 13.0 %all-to-all-start = ((bf16[64,8,6144]{2,1,0:T(8,128)(2,1)}), bf16[64,8,6144]{2,1,0:T(8,128)(2,1)}, u32[]{:S(2)}, u32[]{:S(2)}) async-start(bf16[64,8,6144]{2,1,0:T(8,128)(2,1)} %bitcast.37), calls=%async_computation | async-start | bytes 12582912 | tf_op jit(solution)/shard_map/all_to_all | solution.py:150
  23.0 0.0 copy-done.7
  23.0 0.2 copy.21
  23.2 0.2 copy.20
  23.4 2.4 all-gather.1
  25.8 2.4 all-gather
  28.1 1.6 fusion.13
  29.7 1.7 copy.23.wgu_ref
  31.4 1.9 copy.22
  33.3 4.1 %all-gather.2 = bf16[1,1,128,3072]{2,3,1,0:T(8,128)(2,1)} all-gather(bf16[1,1,128,1536]{2,3,1,0:T(8,128)(2,1)} %copy.22), channel_id=4, replica_groups=mesh['section'=2,'expert'=64,'dp'=2] {'dp'}, dimensions={3}, use_global_device_ids=true | all-gather | bytes 1179648 | tf_op jit(solution)/shard_map/all_gather | solution.py:177
  37.4 124.7 %all-to-all-done = bf16[64,8,6144]{2,1,0:T(8,128)(2,1)} async-done(((bf16[64,8,6144]{2,1,0:T(8,128)(2,1)}), bf16[64,8,6144]{2,1,0:T(8,128)(2,1)}, u32[]{:S(2)}, u32[]{:S(2)}) %all-to-all-start) | async-done | bytes 6291488 | tf_op jit(solution)/shard_map/all_to_all | solution.py:150
  162.1 1.1 copy-done
  163.2 6.9 %expert_rows.1 = (bf16[512,2304]{1,0:T(8,128)(2,1)}, bf16[512,896]{1,0:T(8,128)(2,1)}, bf16[512,384]{1,0:T(8,128)(2,1)S(1)}) custom-call(bf16[512,6144]{1,0:T(8,128)(2,1)} %bitcast.5.row_ref, bf16[3072,256]{1,0:T(8,128)(2,1)S(1)} %copy.23.wgu_ref, bf16[256,3072]{1,0:T(8,128)(2,1)S(1)} %get-tuple-element.21.wgu_t_ref, bf16[3072,128]{1,0:T(8,128)(2,1)S(1)} %bitcast.32), custom_call_target="tpu_custom_call" | custom-call | tf_op jit(solution)/shard_map/expert_rows/pallas_call | solution.py:125
  170.2 0.7 copy-done.3
  170.9 8.0 %all-to-all-start.1 = ((bf16[64,8,2304]{2,1,0:T(8,128)(2,1)}), bf16[64,8,2304]{2,1,0:T(8,128)(2,1)S(1)}, u32[]{:S(2)}, u32[]{:S(2)}) async-start(bf16[64,8,2304]{2,1,0:T(8,128)(2,1)} %bitcast.40), calls=%async_computation.1 | async-start | bytes 4718592 | tf_op jit(solution)/shard_map/all_to_all | solution.py:150
  179.0 0.0 copy-done.4
  179.0 2.5 convolution_convert_fusion.1
  181.5 0.0 copy-start.5
  181.5 0.9 copy-done.5
  182.3 0.8 constant_dynamic-slice_fusion
  183.1 0.0 collective-permute-start.3
  183.1 2.9 %convolution_convert_fusion = bf16[3072,256]{1,0:T(8,128)(2,1)S(1)} fusion(bf16[512,6144]{1,0:T(8,128)(2,1)} %bitcast.5.row_ref, bf16[512,384]{1,0:T(8,128)(2,1)S(1)} %copy-done.4), kind=kOutput, calls=%fused_computation | convolution fusion | flops 806092800 | bytes 4980736 | tf_op jit(solution)/shard_map/dot_general | solution.py:17
  186.0 0.0 copy-start.6
  186.1 1.0 constant_dynamic-slice_fusion.1
  187.1 0.4 copy-done.6
  187.5 0.5 collective-permute-start.2
  188.0 46.5 %all-to-all-done.1 = bf16[64,8,2304]{2,1,0:T(8,128)(2,1)S(1)} async-done(((bf16[64,8,2304]{2,1,0:T(8,128)(2,1)}), bf16[64,8,2304]{2,1,0:T(8,128)(2,1)S(1)}, u32[]{:S(2)}, u32[]{:S(2)}) %all-to-all-start.1) | async-done | bytes 2359328 | tf_op jit(solution)/shard_map/all_to_all | solution.py:150
  234.5 6.4 %all-to-all-start.2 = ((bf16[64,8,896]{2,1,0:T(8,128)(2,1)}), bf16[64,8,896]{2,1,0:T(8,128)(2,1)S(1)}, u32[]{:S(2)}, u32[]{:S(2)}) async-start(bf16[64,8,896]{2,1,0:T(8,128)(2,1)} %bitcast.11), calls=%async_computation.2 | async-start | bytes 1835008 | tf_op jit(solution)/shard_map/all_to_all | solution.py:150
  240.8 0.0 collective-permute-done.3
  240.9 2.0 fusion.5
  242.8 0.0 collective-permute-done.2
  242.8 1.6 add_convert_fusion
  244.4 0.9 slice_bitcast_fusion
  245.3 1.3 convolution_convert_fusion.2
  246.6 2.7 collective-permute-start
  249.3 16.2 %all-to-all-done.2 = bf16[64,8,896]{2,1,0:T(8,128)(2,1)S(1)} async-done(((bf16[64,8,896]{2,1,0:T(8,128)(2,1)}), bf16[64,8,896]{2,1,0:T(8,128)(2,1)S(1)}, u32[]{:S(2)}, u32[]{:S(2)}) %all-to-all-start.2) | async-done | bytes 917536 | tf_op jit(solution)/shard_map/all_to_all | solution.py:150
  265.5 0.4 fusion.3
  266.0 2.8 %collective-permute-start.1 = (bf16[128,768]{1,0:T(8,128)(2,1)S(1)}, bf16[128,768]{1,0:T(8,128)(2,1)S(1)}, u32[]{:S(2)}, u32[]{:S(2)}) collective-permute-start(bf16[128,768]{1,0:T(8,128)(2,1)S(1)} %fusion.6), channel_id=1, source_target_pairs={{0,128},{128,0},{1,129},{129,1},{2,130},{130,2},{3,131},{131,3},{4... | collective-permute-start | bytes 589832 | tf_op jit(solution)/shard_map/ppermute | solution.py:199
  268.8 0.1 slice_reduce_fusion.1
  268.9 0.5 fusion.12
  269.5 0.0 collective-permute-done
  269.5 3.8 %collective-permute-done.1 = bf16[128,768]{1,0:T(8,128)(2,1)S(1)} collective-permute-done((bf16[128,768]{1,0:T(8,128)(2,1)S(1)}, bf16[128,768]{1,0:T(8,128)(2,1)S(1)}, u32[]{:S(2)}, u32[]{:S(2)}) %collective-permute-start.1) | collective-permute-done | bytes 196640 | tf_op jit(solution)/shard_map/ppermute | solution.py:199
  273.3 1.0 maximum_bitcast_fusion
  (11 shorter events, 0.1 us)
Async XLA Ops:
  2.2 1.1 copy-start.1
  3.3 1.1 copy-start.2
  10.0 13.0 %copy-start.7 = (bf16[1,1,1536,128]{3,2,1,0:T(8,128)(2,1)S(1)}, bf16[1,1,1536,128]{3,2,1,0:T(8,128)(2,1)}, u32[]{:S(2)}) copy-start(bf16[1,1,1536,128]{3,2,1,0:T(8,128)(2,1)} %param.12) | copy-start | bytes 1179652
  10.0 13.2 %copy-start.8 = (bf16[1,1,1536,128]{3,2,1,0:T(8,128)(2,1)S(1)}, bf16[1,1,1536,128]{3,2,1,0:T(8,128)(2,1)}, u32[]{:S(2)}) copy-start(bf16[1,1,1536,128]{3,2,1,0:T(8,128)(2,1)} %param.11) | copy-start | bytes 1179652
  10.0 152.1 %all-to-all-start = ((bf16[64,8,6144]{2,1,0:T(8,128)(2,1)}), bf16[64,8,6144]{2,1,0:T(8,128)(2,1)}, u32[]{:S(2)}, u32[]{:S(2)}) async-start(bf16[64,8,6144]{2,1,0:T(8,128)(2,1)} %bitcast.37), calls=%async_computation | async-start | bytes 12582912 | tf_op jit(solution)/shard_map/all_to_all | solution.py:150
  162.1 1.1 copy-start
  170.2 0.7 copy-start.3
  170.9 8.1 %copy-start.4 = (bf16[512,384]{1,0:T(8,128)(2,1)S(1)}, bf16[512,384]{1,0:T(8,128)(2,1)}, u32[]{:S(2)}) copy-start(bf16[512,384]{1,0:T(8,128)(2,1)} %copy-done.3) | copy-start | bytes 1179652
  170.9 63.6 %all-to-all-start.1 = ((bf16[64,8,2304]{2,1,0:T(8,128)(2,1)}), bf16[64,8,2304]{2,1,0:T(8,128)(2,1)S(1)}, u32[]{:S(2)}, u32[]{:S(2)}) async-start(bf16[64,8,2304]{2,1,0:T(8,128)(2,1)} %bitcast.40), calls=%async_computation.1 | async-start | bytes 4718592 | tf_op jit(solution)/shard_map/all_to_all | solution.py:150
  181.5 0.9 copy-start.5
  183.1 57.7 %collective-permute-start.3 = (bf16[128,1536]{1,0:T(8,128)(2,1)}, bf16[128,1536]{1,0:T(8,128)(2,1)}, u32[]{:S(2)}, u32[]{:S(2)}) collective-permute-start(bf16[128,1536]{1,0:T(8,128)(2,1)} %constant_dynamic-slice_fusion), channel_id=1, source_target_pairs={{0,1},{1,0},{2,3},{3,2},{4,5},{5,4},{6,7},{7,6},{8,9},{9,8},{10,11... | collective-permute-start | bytes 1179656 | tf_op jit(solution)/shard_map/ppermute | solution.py:158
  186.0 1.4 copy-start.6
  187.5 55.3 %collective-permute-start.2 = (bf16[1536,256]{1,0:T(8,128)(2,1)}, bf16[1536,256]{1,0:T(8,128)(2,1)}, u32[]{:S(2)}, u32[]{:S(2)}) collective-permute-start(bf16[1536,256]{1,0:T(8,128)(2,1)} %constant_dynamic-slice_fusion.1), channel_id=1, source_target_pairs={{0,1},{1,0},{2,3},{3,2},{4,5},{5,4},{6,7},{7,6},{8,9},{9,8},{10,11... | collective-permute-start | bytes 2359304 | tf_op jit(solution)/shard_map/ppermute | solution.py:158
  234.5 31.1 %all-to-all-start.2 = ((bf16[64,8,896]{2,1,0:T(8,128)(2,1)}), bf16[64,8,896]{2,1,0:T(8,128)(2,1)S(1)}, u32[]{:S(2)}, u32[]{:S(2)}) async-start(bf16[64,8,896]{2,1,0:T(8,128)(2,1)} %bitcast.11), calls=%async_computation.2 | async-start | bytes 1835008 | tf_op jit(solution)/shard_map/all_to_all | solution.py:150
  246.6 22.3 %copy-start.9 = (bf16[1,128,2]{1,2,0:T(2,128)(2,1)S(1)}, bf16[1,128,2]{1,2,0:T(2,128)(2,1)}, u32[]{:S(2)}) copy-start(bf16[1,128,2]{1,2,0:T(2,128)(2,1)} %param.9) | copy-start | bytes 1540
  246.6 22.9 %collective-permute-start = (bf16[128,2304]{1,0:T(8,128)(2,1)}, bf16[128,2304]{1,0:T(8,128)(2,1)S(1)}, u32[]{:S(2)}, u32[]{:S(2)}) collective-permute-start(bf16[128,2304]{1,0:T(8,128)(2,1)} %convolution_convert_fusion.2), channel_id=1, source_target_pairs={{0,128},{128,0},{1,129},{129,1},{2,130},{130,2},{3,131},{131,3},{4... | collective-permute-start | bytes 1769480 | tf_op jit(solution)/shard_map/ppermute | solution.py:194
  266.0 7.3 %collective-permute-start.1 = (bf16[128,768]{1,0:T(8,128)(2,1)S(1)}, bf16[128,768]{1,0:T(8,128)(2,1)S(1)}, u32[]{:S(2)}, u32[]{:S(2)}) collective-permute-start(bf16[128,768]{1,0:T(8,128)(2,1)S(1)} %fusion.6), channel_id=1, source_target_pairs={{0,128},{128,0},{1,129},{129,1},{2,130},{130,2},{3,131},{131,3},{4... | collective-permute-start | bytes 589832 | tf_op jit(solution)/shard_map/ppermute | solution.py:199

commit v2 on v1

v2 whole, which is shorter than its diff:
```python
import functools

import jax
import jax.numpy as jnp
from jax import lax
from jax.experimental import pallas as pl
from jax.experimental.pallas import tpu as pltpu
from jax.sharding import PartitionSpec as P

TOK_MB = 64
CAP = 4
LANES = 128
PLANES = 8
EXPERTS_PLANE = 8
IN_PLANE = [[z * EXPERTS_PLANE + c for c in range(EXPERTS_PLANE)] for z in range(PLANES)]
CHUNKS = ((0,), (1, -1), (2, -2), (3, -3), (4,))
RETURNS = ((0,), (1, -1, 2, -2), (3, -3, 4))
VMEM_LIMIT = 48 * 1024 * 1024
COST = 60000000000


def contract_rows(former, latter):
    return lax.dot_general(
        former, latter, (((0,), (0,)), ((), ())), preferred_element_type=jnp.float32
    )


def plane_tables(meta, plane, source_count, position):
    columns = EXPERTS_PLANE
    meta = meta.astype(jnp.float32).T
    rows = meta.shape[1]
    first, second = meta[0:1, :].astype(jnp.int32), meta[1:2, :].astype(jnp.int32)
    label = lax.broadcasted_iota(jnp.int32, (columns, rows), 0) + plane * columns
    hit0 = (first == label).astype(jnp.float32)
    hit1 = (second == label).astype(jnp.float32)
    row = lax.broadcasted_iota(jnp.int32, (rows, rows), 0)
    col = lax.broadcasted_iota(jnp.int32, (rows, rows), 1)
    before = ((row < col) & (row // TOK_MB == col // TOK_MB)).astype(jnp.bfloat16)
    earlier = jnp.dot(
        (hit0 + hit1).astype(jnp.bfloat16), before, preferred_element_type=jnp.float32
    )
    per_expert = rows // TOK_MB * CAP
    spot = lax.broadcasted_iota(jnp.int32, (1, rows), 1) // TOK_MB * CAP + position * per_expert
    total = columns * per_expert * source_count
    slot = lax.broadcasted_iota(jnp.int32, (total, rows), 0)

    def table(chosen, hit):
        place = jnp.sum(earlier * hit, axis=0, keepdims=True).astype(jnp.int32)
        column = chosen - plane * columns
        inside = (column >= 0) & (column < columns)
        target = jnp.where(inside, column * (per_expert * source_count) + spot + place, -1)
        return (slot == target).astype(jnp.float32)

    table0, table1 = table(first, hit0), table(second, hit1)
    plain = (table0 + table1).astype(jnp.bfloat16)
    scaled = (table0 * meta[2:3, :] + table1 * meta[3:4, :]).astype(jnp.bfloat16)
    return plain, scaled


def plane_kernel(count, x_steps, z_ref, *refs):
    mark_refs, row_refs = refs[:count], refs[count : 2 * count]
    out_ref, table = refs[2 * count :]
    step = pl.program_id(0)

    @pl.when(step == 0)
    def _():
        for place in range(count):
            plain, scaled = plane_tables(mark_refs[place][...], z_ref[0], count, place)
            table[2 * place] = plain
            table[2 * place + 1] = scaled

    kind = (step >= x_steps).astype(jnp.int32)
    total = None
    for place in range(count):
        part = jnp.dot(
            table[2 * place + kind], row_refs[place][...], preferred_element_type=jnp.float32
        )
        total = part if total is None else total + part
    out_ref[...] = total.astype(jnp.bfloat16)


def plane_rows(z, sources):
    rows, full = sources[0].shape
    count = len(sources)
    width = (full - LANES) // 2
    total = EXPERTS_PLANE * rows // TOK_MB * CAP * count
    tile = width // 2
    steps = width // tile
    return pl.pallas_call(
        functools.partial(plane_kernel, count, steps),
        grid=(2 * steps,),
        in_specs=[pl.BlockSpec(memory_space=pltpu.SMEM)]
        + [pl.BlockSpec((rows, LANES), lambda i: (0, 2 * width // LANES))] * count
        + [pl.BlockSpec((rows, tile), lambda i: (0, i))] * count,
        out_specs=pl.BlockSpec((total, tile), lambda i: (0, i)),
        out_shape=jax.ShapeDtypeStruct((total, 2 * width), jnp.bfloat16),
        scratch_shapes=[pltpu.VMEM((2 * count, total, rows), jnp.bfloat16)],
        compiler_params=pltpu.CompilerParams(vmem_limit_bytes=VMEM_LIMIT),
        name="plane_rows",
    )(z, *sources, *sources)


def onward_kernel(steps, z_ref, mark_a, mark_b, row_a, row_b, near_a, near_b, far_a, far_b, table):
    step = pl.program_id(0)
    slots = near_a.shape[0]

    @pl.when(step == 0)
    def _():
        for way, (mark_ref, sign) in enumerate(((mark_a, 1), (mark_b, -1))):
            for hop in (0, 1):
                plane = lax.rem(z_ref[0] + (PLANES + (hop + 1) * sign), PLANES)
                plain, scaled = plane_tables(mark_ref[...], plane, 1, 0)
                table[2 * way, hop * slots : (hop + 1) * slots, :] = plain
                table[2 * way + 1, hop * slots : (hop + 1) * slots, :] = scaled

    def product(table, side):
        return jnp.dot(table, side[...], preferred_element_type=jnp.float32).astype(jnp.bfloat16)

    @pl.when(step < steps)
    def _():
        both = product(table[0], row_a)
        near_a[...] = both[:slots]
        far_a[...] = both[slots:]
        near_b[...] = product(table[2, :slots, :], row_b)

    @pl.when(step >= steps)
    def _():
        near_a[...] = product(table[1, :slots, :], row_a)
        both = product(table[3], row_b)
        near_b[...] = both[:slots]
        far_b[...] = both[slots:]


def onward_rows(z, source_a, source_b):
    rows, full = source_a.shape
    width = (full - LANES) // 2
    total = EXPERTS_PLANE * rows // TOK_MB * CAP
    tile = width // 2
    steps = width // tile
    marks = pl.BlockSpec((rows, LANES), lambda i: (0, 2 * width // LANES))
    block = pl.BlockSpec((rows, tile), lambda i: (0, i))
    return pl.pallas_call(
        functools.partial(onward_kernel, steps),
        grid=(2 * steps,),
        in_specs=[pl.BlockSpec(memory_space=pltpu.SMEM), marks, marks, block, block],
        out_specs=[
            pl.BlockSpec((total, tile), lambda i: (0, i)),
            pl.BlockSpec((total, tile), lambda i: (0, i)),
            pl.BlockSpec((total, tile), lambda i: (0, jnp.minimum(i, steps - 1))),
            pl.BlockSpec((total, tile), lambda i: (0, jnp.maximum(i - steps, 0))),
        ],
        out_shape=[jax.ShapeDtypeStruct((total, 2 * width), jnp.bfloat16)] * 2
        + [jax.ShapeDtypeStruct((total, width), jnp.bfloat16)] * 2,
        scratch_shapes=[pltpu.VMEM((4, 2 * total, rows), jnp.bfloat16)],
        compiler_params=pltpu.CompilerParams(vmem_limit_bytes=VMEM_LIMIT),
        name="onward_rows",
    )(z, source_a, source_b, source_a, source_b)


def own_kernel(z_ref, ids_ref, *pick_refs):
    rows = ids_ref.shape[0]
    per_expert = rows // TOK_MB * CAP
    ids = ids_ref[...]
    label = lax.broadcasted_iota(jnp.int32, (rows, LANES), 1)
    hits = [(ids[:, k : k + 1] == label).astype(jnp.float32) for k in (0, 1)]
    row = lax.broadcasted_iota(jnp.int32, (rows, rows), 0)
    col = lax.broadcasted_iota(jnp.int32, (rows, rows), 1)
    before = ((col < row) & (col // TOK_MB == row // TOK_MB)).astype(jnp.bfloat16)
    earlier = jnp.dot(
        before, (hits[0] + hits[1]).astype(jnp.bfloat16), preferred_element_type=jnp.float32
    )
    block = lax.broadcasted_iota(jnp.int32, (rows, 1), 0) // TOK_MB
    for k in (0, 1):
        chosen = ids[:, k : k + 1]
        place = jnp.sum(earlier * hits[k], axis=1, keepdims=True).astype(jnp.int32)
        behind = (z_ref[0] - chosen // EXPERTS_PLANE + PLANES) % PLANES
        column = chosen % EXPERTS_PLANE
        for pick_ref, offsets in zip(pick_refs, RETURNS):
            spot = jnp.full((rows, 1), -1, jnp.int32)
            for turn, offset in enumerate(offsets):
                target = (column * len(offsets) + turn) * per_expert + block * CAP + place
                spot = jnp.where(behind == offset % PLANES, target, spot)
            slot = lax.broadcasted_iota(jnp.int32, (rows, pick_ref.shape[1]), 1)
            pick_ref[k * rows : (k + 1) * rows, :] = (slot == spot).astype(jnp.bfloat16)


def own_picks(z, ids):
    rows = ids.shape[0]
    group = EXPERTS_PLANE * rows // TOK_MB * CAP
    vector = pl.BlockSpec(memory_space=pltpu.VMEM)
    return pl.pallas_call(
        own_kernel,
        in_specs=[pl.BlockSpec(memory_space=pltpu.SMEM), vector],
        out_specs=[vector] * len(RETURNS),
        out_shape=[
            jax.ShapeDtypeStruct((2 * rows, group * len(offsets)), jnp.bfloat16)
            for offsets in RETURNS
        ],
        name="own_picks",
    )(z, ids)


def expert_kernel(row_ref, wgu_ref, wgu_t_ref, wd_t_ref, act_ref, *out_refs):
    width = wgu_ref.shape[0]
    hid = wd_t_ref.shape[1]
    count = row_ref.shape[0]
    pre = jnp.dot(row_ref[:, :width], wgu_ref[...], preferred_element_type=jnp.float32)
    hidden_grad = jnp.dot(row_ref[:, width:], wd_t_ref[...], preferred_element_type=jnp.float32)
    gate_pre, up_pre = pre[:, :hid], pre[:, hid:]
    sig = jax.nn.sigmoid(gate_pre)
    active = gate_pre * sig
    hidden = (active * up_pre).astype(jnp.bfloat16)
    gate_grad = hidden_grad * up_pre * sig * (1.0 + gate_pre * (1.0 - sig))
    weight = jnp.sum(hidden.astype(jnp.float32) * hidden_grad, axis=1, keepdims=True)
    weight = jnp.broadcast_to(weight, (count, LANES))
    coarse = weight.astype(jnp.bfloat16)
    fine = (weight - coarse.astype(jnp.float32)).astype(jnp.bfloat16)
    lane = lax.broadcasted_iota(jnp.int32, weight.shape, 1)
    both = jnp.concatenate(
        [gate_grad.astype(jnp.bfloat16), (hidden_grad * active).astype(jnp.bfloat16)], axis=1
    )
    act_ref[:, :hid] = hidden
    act_ref[:, hid:] = both
    marks = jnp.where(lane == 0, coarse, fine)
    sources = len(out_refs)
    size = count // sources
    group = size // EXPERTS_PLANE
    for place in range(sources):
        if sources > 1:
            out_row = lax.broadcasted_iota(jnp.int32, (size, count), 0)
            in_row = lax.broadcasted_iota(jnp.int32, (size, count), 1)
            wanted = out_row // group * (group * sources) + place * group + out_row % group
            picked = (in_row == wanted).astype(jnp.bfloat16)
            mine = jnp.dot(picked, both, preferred_element_type=jnp.float32).astype(jnp.bfloat16)
            mark = jnp.dot(picked, marks, preferred_element_type=jnp.float32).astype(jnp.bfloat16)
        else:
            mine, mark = both, marks
        out_refs[place][:, :width] = jnp.dot(
            mine, wgu_t_ref[...], preferred_element_type=jnp.float32
        ).astype(jnp.bfloat16)
        out_refs[place][:, width:] = mark


def expert_pass(rows, sources, cost, wgu, wgu_t, wd_t):
    count = rows.shape[0]
    width, pair = wgu.shape
    hid = wd_t.shape[1]
    back = jax.ShapeDtypeStruct((count // sources, width + LANES), jnp.bfloat16)
    act, *backs = pl.pallas_call(
        expert_kernel,
        out_shape=[jax.ShapeDtypeStruct((count, hid + pair), jnp.bfloat16)] + [back] * sources,
        compiler_params=pltpu.CompilerParams(vmem_limit_bytes=VMEM_LIMIT),
        cost_estimate=pl.CostEstimate(
            flops=cost, bytes_accessed=4 * wgu.size, transcendentals=0
        ),
        name="expert_rows",
    )(rows, wgu, wgu_t, wd_t)
    return act, backs


def exchanged(array, groups=None):
    return lax.all_to_all(
        array, "expert", split_axis=0, concat_axis=0, tiled=True, axis_index_groups=groups
    )


def along_z(array, by):
    size = PLANES * EXPERTS_PLANE
    step = by * EXPERTS_PLANE
    return lax.ppermute(array, "expert", [(i, (i + step) % size) for i in range(size)])


def summed_over_dp(part, dim):
    half = part.shape[dim] // 2
    me = lax.axis_index("dp")
    mine = lax.dynamic_slice_in_dim(part, me * half, half, dim)
    other = lax.dynamic_slice_in_dim(part, (1 - me) * half, half, dim)
    came = lax.ppermute(other, "dp", [(0, 1), (1, 0)])
    return (mine.astype(jnp.float32) + came.astype(jnp.float32)).astype(jnp.bfloat16)


def side_by_side(arrays):
    group = arrays[0].shape[0] // EXPERTS_PLANE
    return jnp.concatenate(
        [array.reshape(EXPERTS_PLANE, group, array.shape[1]) for array in arrays], axis=1
    )


def body(tokens, expert_ids, combine, upstream, w_gate, w_up, w_down):
    sections = lax.axis_size("section")
    tokens, upstream, ids, comb = tokens[0], upstream[0], expert_ids[0], combine[0]
    rows, width = tokens.shape
    group = rows // TOK_MB * CAP
    back_by_one = [(i, (i - 1) % sections) for i in range(sections)]
    z = (lax.axis_index("expert") // EXPERTS_PLANE).astype(jnp.int32).reshape(1)
    tie = lax.optimization_barrier

    marks = jnp.concatenate([ids.astype(jnp.bfloat16), comb], axis=1)
    raw = jnp.concatenate([tokens, upstream, jnp.pad(marks, ((0, 0), (0, LANES - 4)))], axis=1)
    from_m1, from_p1 = along_z(raw, 1), along_z(raw, -1)

    def rows_for(sources):
        send = plane_rows(z, sources)
        return send.reshape(EXPERTS_PLANE, group * len(sources), 2 * width)

    def in_plane(send, before):
        send, before = tie((send, before))
        return exchanged(send, IN_PLANE), before

    came = [exchanged(rows_for([raw]), IN_PLANE)]
    picks = own_picks(z, ids)
    gate_full = lax.all_gather(w_gate[0, 0], "dp", axis=0, tiled=True)
    up_full = lax.all_gather(w_up[0, 0], "dp", axis=0, tiled=True)
    down_full = lax.all_gather(w_down[0, 0], "dp", axis=1, tiled=True)
    wgu = jnp.concatenate([gate_full, up_full], axis=1)
    weights = (wgu, wgu.T, down_full.T)
    hid = w_gate.shape[3]
    act, back = expert_pass(came[0].reshape(-1, 2 * width), 1, COST, *weights)
    acts, backs = [act] + [None] * 4, [None] * 5
    back_0 = exchanged(back[0].reshape(EXPERTS_PLANE, group, width + LANES), IN_PLANE)
    from_p1, from_m1, weights, picks, acts[0] = tie((from_p1, from_m1, weights, picks, acts[0]))

    from_m2, from_p2 = along_z(from_m1, 1), along_z(from_p1, -1)

    def expert(turn, cost=1):
        return expert_pass(
            came[turn].reshape(-1, 2 * width),
            len(CHUNKS[turn]),
            cost,
            *weights,
        )

    got, back_0 = in_plane(rows_for([from_p1, from_m1]), back_0)
    came.append(got)

    near_a, near_b, far_a, far_b = onward_rows(z, from_m2, from_p2)
    from_m3, from_p3 = along_z(near_a, 1), along_z(near_b, -1)
    four_a = along_z(along_z(far_a, 1), 1)
    four_b = along_z(along_z(far_b, -1), -1)
    from_p2, from_m2, near_a = tie((from_p2, from_m2, near_a))
    send, came[1] = tie((rows_for([from_p2, from_m2]), came[1]))
    came.append(exchanged(send, IN_PLANE))

    acts[1], backs[1] = expert(1)
    send = side_by_side([from_p3, from_m3])
    got, came[2] = in_plane(send, came[2])
    came.append(got)

    first = [along_z(backs[1][i], by) for i, by in enumerate(CHUNKS[1])]
    came[2], first = tie((came[2], first))
    acts[2], backs[2] = expert(2, COST)
    four_a, four_b, backs[1], backs[2] = tie((four_a, four_b, backs[1], backs[2]))
    send = jnp.concatenate([four_a, four_b], axis=1).reshape(EXPERTS_PLANE, group, 2 * width)
    got, came[3] = in_plane(send, came[3])
    came.append(got)
    acts[3], backs[3] = expert(3, COST)

    first += [along_z(backs[2][i], by) for i, by in enumerate(CHUNKS[2])]
    second = [along_z(backs[3][i], by) for i, by in enumerate(CHUNKS[3])]
    first, acts[3] = tie((first, acts[3]))
    came[4], _ = tie((came[4], first))
    acts[4], backs[4] = expert(4)
    second.append(along_z(backs[4][0], CHUNKS[4][0]))
    send = side_by_side(first)
    send, came, acts = tie((send, came, acts))
    back_a = exchanged(send, IN_PLANE)
    back_b, back_a = in_plane(side_by_side(second), back_a)

    back_0, back_a, back_b = (
        array.reshape(-1, array.shape[2]) for array in (back_0, back_a, back_b)
    )
    boths = [pick[:rows] + pick[rows:] for pick in picks]

    def product(left, right):
        return jnp.dot(left, right, preferred_element_type=jnp.float32)

    grad = product(boths[0], back_0[:, :width]) + product(boths[1], back_a[:, :width])
    grad = (grad + product(boths[2], back_b[:, :width])).astype(jnp.bfloat16)
    grad = lax.ppermute(grad, "section", back_by_one)
    weight = product(picks[0], back_0[:, width:]) + product(picks[1], back_a[:, width:])
    weight = weight + product(picks[2], back_b[:, width:])
    weight = weight[:, 0] + weight[:, 1]
    weight = jnp.stack([weight[:rows], weight[rows:]], axis=1)
    grad_combine = (weight / comb.astype(jnp.float32)).astype(jnp.bfloat16)

    part_gu, part_down = 0.0, 0.0
    for row, act in zip(came, acts):
        row = row.reshape(-1, 2 * width)
        part_gu = part_gu + contract_rows(row[:, :width], act[:, hid:])
        part_down = part_down + contract_rows(act[:, :hid], row[:, width:])
    grad_gu = summed_over_dp(part_gu.astype(jnp.bfloat16), 0)
    grad_down = summed_over_dp(part_down.astype(jnp.bfloat16), 1)
    return (
        grad[None],
        grad_combine[None],
        grad_gu[:, :hid][None, None],
        grad_gu[:, hid:][None, None],
        grad_down[None, None],
    )


def solution(mesh):
    return jax.shard_map(
        body,
        mesh=mesh,
        in_specs=(
            P("section", ("expert", "dp"), None),
            P("section", ("expert", "dp"), None),
            P("section", ("expert", "dp"), None),
            P("section", ("expert", "dp"), None),
            P("section", "expert", "dp", None),
            P("section", "expert", "dp", None),
            P("section", "expert", None, "dp"),
        ),
        out_specs=(
            P("section", ("expert", "dp"), None),
            P("section", ("expert", "dp"), None),
            P("section", "expert", "dp", None),
            P("section", "expert", "dp", None),
            P("section", "expert", None, "dp"),
        ),
        check_vma=False,
    )
```

time: 276 us -> 254 us (0.920)
  waiting for transfers between devices: 191 us -> 81.3 us
  starting transfers between devices: 33.4 us -> 73.7 us
  Pallas kernels: 12.4 us -> 30.3 us
  matrix products: 7.14 us -> 22.5 us
  other arithmetic: 6.61 us -> 17.2 us
    all_to_all x3 -> x8, waiting for transfers between devices: 187 us -> 19.5 us  [exchanged(): lax.all_to_all(array, 'expert', split_axis=0, concat_axis=0, tiled=True,...]
    ppermute x2 -> x18, waiting for transfers between devices: 3.82 us -> 61.8 us  [the longest x17 47.5 us: along_z(): lax.ppermute(array, 'expert', [(i, (i + step) % size) for i in range(size)])]
    ppermute x2 -> x18, starting transfers between devices: 5.51 us -> 30.7 us  [the longest x17 28.1 us: along_z(): lax.ppermute(array, 'expert', [(i, (i + step) % size) for i in range(size)])]
    pallas_call x2 -> x10, Pallas kernels: 12.4 us -> 30.3 us  [the longest x5 16.6 us: expert_pass(): pl.pallas_call(expert_kernel, out_shape=[jax.ShapeDtypeStruct((count, hid...]
    all_to_all x3 -> x8, starting transfers between devices: 27.4 us -> 42.4 us  [exchanged(): lax.all_to_all(array, 'expert', split_axis=0, concat_axis=0, tiled=True,...]
    dot_general x2 -> x10, matrix products: 5.41 us -> 15.8 us  [contract_rows(): lax.dot_general(former, latter, (((0,), (0,)), ((), ())), preferred_eleme...]
    concatenate x0 -> x5, other arithmetic: none -> 9.43 us  [the longest x3 7.85 us: side_by_side(): jnp.concatenate([array.reshape(EXPERTS_PLANE, group, array.shape[1]) for...]
    dot_general x2 -> x6, matrix products: 1.73 us -> 6.76 us  [product(): return jnp.dot(left, right, preferred_element_type=jnp.float32)]
  transfers between devices with their start and end apart: 7 -> 28, of which waited for: 4 -> 7; matrix products, arithmetic and copies ran while one was open for 7% -> 17% of each run, Pallas kernels for 0% -> 12%
where the time goes in v2:
time: 254 us; the launch traced here: 252 us
  waiting for transfers between devices  81.3 us (32%)
  starting transfers between devices  73.7 us (29%)
  Pallas kernels  30.3 us (12%)
  matrix products  22.5 us (9%)
  other arithmetic  17.2 us (7%)
  local copies, waits for them, and re-layouts  16.4 us (6%)
  blocking collectives  9.2 us (4%)
    ppermute x17, waiting for transfers between devices, along_z(): lax.ppermute(array, 'expert', [(i, (i + step) % size) for i in range(size)])  47.5 us
    all_to_all x8, starting transfers between devices, exchanged(): lax.all_to_all(array, 'expert', split_axis=0, concat_axis=0, tiled=True,...  42.4 us
    ppermute x17, starting transfers between devices, along_z(): lax.ppermute(array, 'expert', [(i, (i + step) % size) for i in range(size)])  28.1 us
    all_to_all x8, waiting for transfers between devices, exchanged(): lax.all_to_all(array, 'expert', split_axis=0, concat_axis=0, tiled=True,...  19.5 us
    pallas_call x5, Pallas kernels, expert_pass(): pl.pallas_call(expert_kernel, out_shape=[jax.ShapeDtypeStruct((count, hid...  16.6 us
    dot_general x10, matrix products, contract_rows(): lax.dot_general(former, latter, (((0,), (0,)), ((), ())), preferred_eleme...  15.8 us
    ppermute x1, waiting for transfers between devices, body(): grad = lax.ppermute(grad, 'section', back_by_one)  14.2 us
    unnamed x46, local copies, waits for them, and re-layouts  10.6 us
  transfers between devices with their start and end apart: 28, of which 7 were waited for; matrix products, arithmetic and copies ran while one was open for 17% of the time, Pallas kernels for 12%

profile of v2, /device:TPU:32, one launch (start us, length us, event | category | flops | bytes accessed | tf_op | source)
XLA Modules:
  0.0 251.6 jit_solution(11398364334779299148)
XLA Ops:
  3.8 2.0 collective-permute-start.1
  5.9 2.4 plane_rows.3
  8.3 5.5 %all-to-all-start = ((bf16[8,8,6144]{2,1,0:T(8,128)(2,1)}), bf16[8,8,6144]{2,1,0:T(8,128)(2,1)}, u32[]{:S(2)}, u32[]{:S(2)}) async-start(bf16[8,8,6144]{2,1,0:T(8,128)(2,1)} %bitcast.10), calls=%async_computation | async-start | bytes 1572864 | tf_op jit(solution)/shard_map/all_to_all | solution.py:262
  14.0 2.6 %all-gather = bf16[1,1,3072,128]{2,3,1,0:T(8,128)(2,1)} all-gather(bf16[1,1,1536,128]{2,3,1,0:T(8,128)(2,1)S(1)} %copy.35), channel_id=2, replica_groups=mesh['section'=2,'expert'=64,'dp'=2] {'dp'}, dimensions={2}, use_global_device_ids=true | all-gather | bytes 1179648 | tf_op jit(solution)/shard_map/all_gather | solution.py:312
  16.8 2.5 all-gather.1
  20.3 2.9 %fusion.53 = (bf16[256,3072]{1,0:T(8,128)(2,1)S(1)}, bf16[3072,256]{0,1:T(8,128)(2,1)}) fusion(bf16[3072,128]{0,1:T(8,128)(2,1)} %bitcast.66, bf16[3072,128]{0,1:T(8,128)(2,1)} %bitcast.65), kind=kLoop, calls=%fused_computation.80 | loop fusion | flops 3145728 | bytes 4718592 | tf_op jit(solution)/shard_map/transpose | solution.py:316
  23.2 3.1 %copy.38.wgu_ref = bf16[3072,256]{1,0:T(8,128)(2,1)} copy(bf16[3072,256]{0,1:T(8,128)(2,1)} %get-tuple-element.87) | data formatting | bytes 3145728 | tf_op jit(solution)/shard_map/concatenate | solution.py:315
  26.3 4.1 %all-gather.2 = bf16[1,1,128,3072]{2,3,1,0:T(8,128)(2,1)} all-gather(bf16[1,1,128,1536]{2,3,1,0:T(8,128)(2,1)} %copy.37), channel_id=4, replica_groups=mesh['section'=2,'expert'=64,'dp'=2] {'dp'}, dimensions={3}, use_global_device_ids=true | all-gather | bytes 1179648 | tf_op jit(solution)/shard_map/all_gather | solution.py:314
  32.9 2.2 expert_rows.5
  35.8 5.7 %all-to-all-start.1 = ((bf16[8,8,3200]{2,1,0:T(8,128)(2,1)}), bf16[8,8,3200]{2,1,0:T(8,128)(2,1)}, u32[]{:S(2)}, u32[]{:S(2)}) async-start(bf16[8,8,3200]{2,1,0:T(8,128)(2,1)} %bitcast.62), calls=%async_computation.1 | async-start | bytes 819200 | tf_op jit(solution)/shard_map/all_to_all | solution.py:262
  41.6 2.1 own_picks.1
  43.7 4.1 %collective-permute-start.3 = (bf16[128,6272]{1,0:T(8,128)(2,1)}, bf16[128,6272]{1,0:T(8,128)(2,1)S(1)}, u32[]{:S(2)}, u32[]{:S(2)}) collective-permute-start(bf16[128,6272]{1,0:T(8,128)(2,1)} %collective-permute-done.refs_0_.refs_2_), channel_id=1, source_target_pairs={{0,112},{2,114},{4,116},{6,118},{8,120},{10,122},{12,124},{14,126}... | collective-permute-start | bytes 4816904 | tf_op jit(solution)/shard_map/ppermute | solution.py:270
  47.8 3.7 %plane_rows.4 = bf16[128,6144]{1,0:T(8,128)(2,1)S(1)} custom-call(s32[1]{0:T(128)} %bitcast.9.z_ref, bf16[128,6272]{1,0:T(8,128)(2,1)} %collective-permute-done.refs_0_.refs_2_, bf16[128,6272]{1,0:T(8,128)(2,1)} %collective-permute-done.1.refs_1_.refs_3_, bf16[128,6272]{1,0:T(8,128)(2,1)} %collective-permute-done.refs_0_.refs_2_, ...), custom_call_target="tpu_custom_call" | custom-call | tf_op jit(solution)/shard_map/plane_rows/pallas_call | solution.py:89
  52.6 5.7 %all-to-all-start.2 = ((bf16[8,16,6144]{2,1,0:T(8,128)(2,1)}), bf16[8,16,6144]{2,1,0:T(8,128)(2,1)}, u32[]{:S(2)}, u32[]{:S(2)}) async-start(bf16[8,16,6144]{2,1,0:T(8,128)(2,1)} %bitcast.61), calls=%async_computation.2 | async-start | bytes 3145728 | tf_op jit(solution)/shard_map/all_to_all | solution.py:262
  58.3 24.3 %collective-permute-done.3.mark_b.row_b.refs_0_.refs_2_ = bf16[128,6272]{1,0:T(8,128)(2,1)S(1)} collective-permute-done((bf16[128,6272]{1,0:T(8,128)(2,1)}, bf16[128,6272]{1,0:T(8,128)(2,1)S(1)}, u32[]{:S(2)}, u32[]{:S(2)}) %collective-permute-start.3) | collective-permute-done | bytes 1605664 | tf_op jit(solution)/shard_map/ppermute | solution.py:270
  82.7 2.3 collective-permute-done.2.mark_a.row_a.refs_1_.refs_3_
  84.9 3.3 %onward_rows.1 = (bf16[64,6144]{1,0:T(8,128)(2,1)}, bf16[64,6144]{1,0:T(8,128)(2,1)}, bf16[64,3072]{1,0:T(8,128)(2,1)}, bf16[64,3072]{1,0:T(8,128)(2,1)}) custom-call(s32[1]{0:T(128)} %bitcast.9.z_ref, bf16[128,6272]{1,0:T(8,128)(2,1)S(1)} %collective-permute-done.2.mark_a.row_a.refs_1_.refs_3_, ...), custom_call_target="tpu_custom_call" | custom-call | tf_op jit(solution)/shard_map/onward_rows/pallas_call | solution.py:142
  88.2 2.9 %collective-permute-start.8 = (bf16[64,6144]{1,0:T(8,128)(2,1)}, bf16[64,6144]{1,0:T(8,128)(2,1)}, u32[]{:S(2)}, u32[]{:S(2)}) collective-permute-start(bf16[64,6144]{1,0:T(8,128)(2,1)} %get-tuple-element.92), channel_id=1, source_target_pairs={{0,112},{2,114},{4,116},{6,118},{8,120},{10,122},{12,124},{14,126}... | collective-permute-start | bytes 2359304 | tf_op jit(solution)/shard_map/ppermute | solution.py:270
  91.2 2.2 plane_rows.5
  94.6 5.6 %all-to-all-start.3 = ((bf16[8,16,6144]{2,1,0:T(8,128)(2,1)}), bf16[8,16,6144]{2,1,0:T(8,128)(2,1)}, u32[]{:S(2)}, u32[]{:S(2)}) async-start(bf16[8,16,6144]{2,1,0:T(8,128)(2,1)} %bitcast.60), calls=%async_computation.3 | async-start | bytes 3145728 | tf_op jit(solution)/shard_map/all_to_all | solution.py:262
  100.2 2.3 collective-permute-start.6
  103.3 2.6 %fusion.23 = f32[128,3072]{1,0:T(8,128)} fusion(bf16[64,3200]{1,0:T(8,128)(2,1)} %bitcast.15, bf16[256,64]{1,0:T(8,128)(2,1)S(1)} %copy-done.17), kind=kOutput, calls=%fused_computation.42 | convolution fusion | flops 50339840 | bytes 1998848 | tf_op jit(solution)/shard_map/dot_general | solution.py:375
  105.8 3.7 %expert_rows.6 = (bf16[128,384]{1,0:T(8,128)(2,1)S(1)}, bf16[64,3200]{1,0:T(8,128)(2,1)}, bf16[64,3200]{1,0:T(8,128)(2,1)S(1)}) custom-call(bf16[128,6144]{1,0:T(8,128)(2,1)} %bitcast.17.row_ref, bf16[3072,256]{1,0:T(8,128)(2,1)S(1)} %copy.39.wgu_ref, bf16[256,3072]{1,0:T(8,128)(2,1)} %copy-done, bf16[3072,128]{1,0:T(8,128)(2,1)S(1)} %bitcast.56), custom_call_target="tpu_custom_call" | custom-call | flops 1 | bytes 3145728 | tf_op jit(solution)/shard_map/expert_rows/pallas_call | solution.py:249
  110.0 10.4 %collective-permute-done.4 = bf16[64,3072]{1,0:T(8,128)(2,1)} collective-permute-done((bf16[64,3072]{1,0:T(8,128)(2,1)}, bf16[64,3072]{1,0:T(8,128)(2,1)}, u32[]{:S(2)}, u32[]{:S(2)}) %collective-permute-start.4) | collective-permute-done | bytes 393248 | tf_op jit(solution)/shard_map/ppermute | solution.py:270
  124.0 2.7 %pad_maximum_fusion.3 = bf16[8,16,6144]{2,1,0:T(8,128)(2,1)} fusion(bf16[8,8,6144]{2,1,0:T(8,128)(2,1)} %bitcast.19, bf16[8,8,6144]{2,1,0:T(8,128)(2,1)} %bitcast.18), kind=kLoop, calls=%fused_computation.17 | loop fusion | flops 3145728 | bytes 3145728 | tf_op jit(solution)/shard_map/concatenate | solution.py:284
  126.6 5.4 %all-to-all-start.4 = ((bf16[8,16,6144]{2,1,0:T(8,128)(2,1)}), bf16[8,16,6144]{2,1,0:T(8,128)(2,1)}, u32[]{:S(2)}, u32[]{:S(2)}) async-start(bf16[8,16,6144]{2,1,0:T(8,128)(2,1)} %pad_maximum_fusion.3), calls=%async_computation.4 | async-start | bytes 3145728 | tf_op jit(solution)/shard_map/all_to_all | solution.py:262
  132.1 3.7 %expert_rows.7 = (bf16[128,384]{1,0:T(8,128)(2,1)S(1)}, bf16[64,3200]{1,0:T(8,128)(2,1)}, bf16[64,3200]{1,0:T(8,128)(2,1)S(1)}) custom-call(bf16[128,6144]{1,0:T(8,128)(2,1)} %bitcast.20.row_ref, bf16[3072,256]{1,0:T(8,128)(2,1)S(1)} %copy.39.wgu_ref, bf16[256,3072]{1,0:T(8,128)(2,1)} %copy-done, bf16[3072,128]{1,0:T(8,128)(2,1)S(1)} %bitcast.57), custom_call_target="tpu_custom_call" | custom-call | flops 60000002048 | bytes 3145728 | tf_op jit(solution)/shard_map/expert_rows/pallas_call | solution.py:249
  135.8 2.6 %collective-permute-start.14 = (bf16[64,3200]{1,0:T(8,128)(2,1)}, bf16[64,3200]{1,0:T(8,128)(2,1)}, u32[]{:S(2)}, u32[]{:S(2)}) collective-permute-start(bf16[64,3200]{1,0:T(8,128)(2,1)} %get-tuple-element.107), channel_id=1, source_target_pairs={{0,32},{2,34},{4,36},{6,38},{8,40},{10,42},{12,44},{14,46},{16,48}... | collective-permute-start | bytes 1228808 | tf_op jit(solution)/shard_map/ppermute | solution.py:270
  139.9 2.0 maximum_bitcast_fusion
  142.0 6.2 %all-to-all-done.4 = bf16[8,16,6144]{2,1,0:T(8,128)(2,1)} async-done(((bf16[8,16,6144]{2,1,0:T(8,128)(2,1)}), bf16[8,16,6144]{2,1,0:T(8,128)(2,1)}, u32[]{:S(2)}, u32[]{:S(2)}) %all-to-all-start.4) | async-done | bytes 1572896 | tf_op jit(solution)/shard_map/all_to_all | solution.py:262
  148.2 4.2 %all-to-all-start.5 = ((bf16[8,8,6144]{2,1,0:T(8,128)(2,1)}), bf16[8,8,6144]{2,1,0:T(8,128)(2,1)}, u32[]{:S(2)}, u32[]{:S(2)}) async-start(bf16[8,8,6144]{2,1,0:T(8,128)(2,1)} %maximum_bitcast_fusion), calls=%async_computation.5 | async-start | bytes 1572864 | tf_op jit(solution)/shard_map/all_to_all | solution.py:262
  152.4 4.1 %expert_rows.8 = (bf16[128,384]{1,0:T(8,128)(2,1)S(1)}, bf16[64,3200]{1,0:T(8,128)(2,1)}, bf16[64,3200]{1,0:T(8,128)(2,1)}) custom-call(bf16[128,6144]{1,0:T(8,128)(2,1)} %bitcast.22.row_ref, bf16[3072,256]{1,0:T(8,128)(2,1)S(1)} %copy.39.wgu_ref, bf16[256,3072]{1,0:T(8,128)(2,1)} %copy-done, bf16[3072,128]{1,0:T(8,128)(2,1)S(1)} %bitcast.58), custom_call_target="tpu_custom_call" | custom-call | flops 60000002048 | bytes 3145728 | tf_op jit(solution)/shard_map/expert_rows/pallas_call | solution.py:249
  156.5 3.6 %collective-permute-start.12 = (bf16[64,3200]{1,0:T(8,128)(2,1)}, bf16[64,3200]{1,0:T(8,128)(2,1)}, u32[]{:S(2)}, u32[]{:S(2)}) collective-permute-start(bf16[64,3200]{1,0:T(8,128)(2,1)} %get-tuple-element.102), channel_id=1, source_target_pairs={{0,48},{2,50},{4,52},{6,54},{8,56},{10,58},{12,60},{14,62},{16,64}... | collective-permute-start | bytes 1228808 | tf_op jit(solution)/shard_map/ppermute | solution.py:270
  161.6 2.8 %pad_maximum_fusion = bf16[8,32,3200]{2,1,0:T(8,128)(2,1)} fusion(bf16[8,8,3200]{2,1,0:T(8,128)(2,1)} %bitcast.30, bf16[8,8,3200]{2,1,0:T(8,128)(2,1)} %bitcast.29, bf16[8,8,3200]{2,1,0:T(8,128)(2,1)} %bitcast.28, bf16[8,8,3200]{2,1,0:T(8,128)(2,1)} %bitcast.27), kind=kLoop, calls=%fused_computation.13 | loop fusion | flops 6553600 | bytes 3276800 | tf_op jit(solution)/shard_map/concatenate | solution.py:284
  165.6 2.9 %expert_rows.9 = (bf16[64,384]{1,0:T(8,128)(2,1)S(1)}, bf16[64,3200]{1,0:T(8,128)(2,1)}) custom-call(bf16[64,6144]{1,0:T(8,128)(2,1)} %bitcast.25.row_ref, bf16[3072,256]{1,0:T(8,128)(2,1)S(1)} %copy.39.wgu_ref, bf16[256,3072]{1,0:T(8,128)(2,1)S(1)} %copy-done.1, bf16[3072,128]{1,0:T(8,128)(2,1)S(1)} %bitcast.59), custom_call_target="tpu_custom_call" | custom-call | flops 1 | bytes 3145728 | tf_op jit(solution)/shard_map/expert_rows/pallas_call | solution.py:249
  168.5 3.5 %collective-permute-start.16 = (bf16[64,3200]{1,0:T(8,128)(2,1)}, bf16[64,3200]{1,0:T(8,128)(2,1)}, u32[]{:S(2)}, u32[]{:S(2)}) collective-permute-start(bf16[64,3200]{1,0:T(8,128)(2,1)} %get-tuple-element.115), channel_id=1, source_target_pairs={{0,64},{2,66},{4,68},{6,70},{8,72},{10,74},{12,76},{14,78},{16,80}... | collective-permute-start | bytes 1228808 | tf_op jit(solution)/shard_map/ppermute | solution.py:270
  172.0 5.6 %all-to-all-start.6 = ((bf16[8,32,3200]{2,1,0:T(8,128)(2,1)}), bf16[8,32,3200]{2,1,0:T(8,128)(2,1)S(1)}, u32[]{:S(2)}, u32[]{:S(2)}) async-start(bf16[8,32,3200]{2,1,0:T(8,128)(2,1)} %pad_maximum_fusion), calls=%async_computation.6 | async-start | bytes 3276800 | tf_op jit(solution)/shard_map/all_to_all | solution.py:262
  178.9 1.7 fusion.15
  182.2 1.7 fusion.13
  185.5 1.7 fusion.11
  190.3 1.6 fusion.1
  195.8 10.5 %collective-permute-done.13 = bf16[64,3200]{1,0:T(8,128)(2,1)} collective-permute-done((bf16[64,3200]{1,0:T(8,128)(2,1)}, bf16[64,3200]{1,0:T(8,128)(2,1)}, u32[]{:S(2)}, u32[]{:S(2)}) %collective-permute-start.13) | collective-permute-done | bytes 409632 | tf_op jit(solution)/shard_map/ppermute | solution.py:270
  206.4 2.3 pad_maximum_fusion.4
  208.7 4.7 %all-to-all-start.7 = ((bf16[8,24,3200]{2,1,0:T(8,128)(2,1)}), bf16[8,24,3200]{2,1,0:T(8,128)(2,1)}, u32[]{:S(2)}, u32[]{:S(2)}) async-start(bf16[8,24,3200]{2,1,0:T(8,128)(2,1)} %pad_maximum_fusion.4), calls=%async_computation.7 | async-start | bytes 2457600 | tf_op jit(solution)/shard_map/all_to_all | solution.py:262
  216.5 13.3 %all-to-all-done.7 = bf16[8,24,3200]{2,1,0:T(8,128)(2,1)} async-done(((bf16[8,24,3200]{2,1,0:T(8,128)(2,1)}), bf16[8,24,3200]{2,1,0:T(8,128)(2,1)}, u32[]{:S(2)}, u32[]{:S(2)}) %all-to-all-start.7) | async-done | bytes 1228832 | tf_op jit(solution)/shard_map/all_to_all | solution.py:262
  230.8 1.7 fusion.4
  232.5 2.6 %collective-permute-start.17 = (bf16[128,3072]{1,0:T(8,128)(2,1)S(1)}, bf16[128,3072]{1,0:T(8,128)(2,1)S(1)}, u32[]{:S(2)}, u32[]{:S(2)}) collective-permute-start(bf16[128,3072]{1,0:T(8,128)(2,1)S(1)} %fusion.4), channel_id=1, source_target_pairs={{0,128},{128,0},{1,129},{129,1},{2,130},{130,2},{3,131},{131,3},{4... | collective-permute-start | bytes 2359304 | tf_op jit(solution)/shard_map/ppermute | solution.py:379
  236.5 14.2 %collective-permute-done.17 = bf16[128,3072]{1,0:T(8,128)(2,1)S(1)} collective-permute-done((bf16[128,3072]{1,0:T(8,128)(2,1)S(1)}, bf16[128,3072]{1,0:T(8,128)(2,1)S(1)}, u32[]{:S(2)}, u32[]{:S(2)}) %collective-permute-start.17) | collective-permute-done | bytes 786464 | tf_op jit(solution)/shard_map/ppermute | solution.py:379
  (101 shorter events, 37.0 us)
Async XLA Ops:
  2.2 1.6 copy-start.11
  3.8 39.8 %collective-permute-start.1 = (bf16[128,6272]{1,0:T(8,128)(2,1)S(1)}, bf16[128,6272]{1,0:T(8,128)(2,1)}, u32[]{:S(2)}, u32[]{:S(2)}) collective-permute-start(bf16[128,6272]{1,0:T(8,128)(2,1)S(1)} %pad_maximum_fusion.1.refs_0_.refs_1_), channel_id=1, source_target_pairs={{0,16},{2,18},{4,20},{6,22},{8,24},{10,26},{12,28},{14,30},{16,32}... | collective-permute-start | bytes 4816904 | tf_op jit(solution)/shard_map/ppermute | solution.py:270
  5.8 37.9 %collective-permute-start = (bf16[128,6272]{1,0:T(8,128)(2,1)S(1)}, bf16[128,6272]{1,0:T(8,128)(2,1)}, u32[]{:S(2)}, u32[]{:S(2)}) collective-permute-start(bf16[128,6272]{1,0:T(8,128)(2,1)S(1)} %pad_maximum_fusion.1.refs_0_.refs_1_), channel_id=1, source_target_pairs={{0,112},{2,114},{4,116},{6,118},{8,120},{10,122},{12,124},{14,126}... | collective-permute-start | bytes 4816904 | tf_op jit(solution)/shard_map/ppermute | solution.py:270
  8.3 5.5 %copy-start.12 = (bf16[1,1,1536,128]{3,2,1,0:T(8,128)(2,1)S(1)}, bf16[1,1,1536,128]{3,2,1,0:T(8,128)(2,1)}, u32[]{:S(2)}) copy-start(bf16[1,1,1536,128]{3,2,1,0:T(8,128)(2,1)} %param.11) | copy-start | bytes 1179652
  8.3 8.4 %copy-start.13 = (bf16[1,1,1536,128]{3,2,1,0:T(8,128)(2,1)S(1)}, bf16[1,1,1536,128]{3,2,1,0:T(8,128)(2,1)}, u32[]{:S(2)}) copy-start(bf16[1,1,1536,128]{3,2,1,0:T(8,128)(2,1)} %param.12) | copy-start | bytes 1179652
  8.3 22.1 %all-to-all-start = ((bf16[8,8,6144]{2,1,0:T(8,128)(2,1)}), bf16[8,8,6144]{2,1,0:T(8,128)(2,1)}, u32[]{:S(2)}, u32[]{:S(2)}) async-start(bf16[8,8,6144]{2,1,0:T(8,128)(2,1)} %bitcast.10), calls=%async_computation | async-start | bytes 1572864 | tf_op jit(solution)/shard_map/all_to_all | solution.py:262
  14.0 5.3 %copy-start.14 = (bf16[1,1,128,1536]{3,2,1,0:T(8,128)(2,1)S(1)}, bf16[1,1,128,1536]{3,2,1,0:T(8,128)(2,1)}, u32[]{:S(2)}) copy-start(bf16[1,1,128,1536]{3,2,1,0:T(8,128)(2,1)} %param.13) | copy-start | bytes 1179652
  23.2 7.2 %copy-start = (bf16[256,3072]{1,0:T(8,128)(2,1)}, bf16[256,3072]{1,0:T(8,128)(2,1)S(1)}, u32[]{:S(2)}) copy-start(bf16[256,3072]{1,0:T(8,128)(2,1)S(1)} %get-tuple-element.88.wgu_t_ref) | copy-start | bytes 4718596
  30.4 1.1 copy-start.2
  31.5 1.4 copy-start.7
  35.1 0.8 copy-start.8
  35.8 16.8 %all-to-all-start.1 = ((bf16[8,8,3200]{2,1,0:T(8,128)(2,1)}), bf16[8,8,3200]{2,1,0:T(8,128)(2,1)}, u32[]{:S(2)}, u32[]{:S(2)}) async-start(bf16[8,8,3200]{2,1,0:T(8,128)(2,1)} %bitcast.62), calls=%async_computation.1 | async-start | bytes 819200 | tf_op jit(solution)/shard_map/all_to_all | solution.py:262
  43.7 39.0 %collective-permute-start.3 = (bf16[128,6272]{1,0:T(8,128)(2,1)}, bf16[128,6272]{1,0:T(8,128)(2,1)S(1)}, u32[]{:S(2)}, u32[]{:S(2)}) collective-permute-start(bf16[128,6272]{1,0:T(8,128)(2,1)} %collective-permute-done.refs_0_.refs_2_), channel_id=1, source_target_pairs={{0,112},{2,114},{4,116},{6,118},{8,120},{10,122},{12,124},{14,126}... | collective-permute-start | bytes 4816904 | tf_op jit(solution)/shard_map/ppermute | solution.py:270
  47.8 37.2 %collective-permute-start.2 = (bf16[128,6272]{1,0:T(8,128)(2,1)}, bf16[128,6272]{1,0:T(8,128)(2,1)S(1)}, u32[]{:S(2)}, u32[]{:S(2)}) collective-permute-start(bf16[128,6272]{1,0:T(8,128)(2,1)} %collective-permute-done.1.refs_1_.refs_3_), channel_id=1, source_target_pairs={{0,16},{2,18},{4,20},{6,22},{8,24},{10,26},{12,28},{14,30},{16,32}... | collective-permute-start | bytes 4816904 | tf_op jit(solution)/shard_map/ppermute | solution.py:270
  51.5 1.2 copy-start.6
  52.6 42.0 %all-to-all-start.2 = ((bf16[8,16,6144]{2,1,0:T(8,128)(2,1)}), bf16[8,16,6144]{2,1,0:T(8,128)(2,1)}, u32[]{:S(2)}, u32[]{:S(2)}) async-start(bf16[8,16,6144]{2,1,0:T(8,128)(2,1)} %bitcast.61), calls=%async_computation.2 | async-start | bytes 3145728 | tf_op jit(solution)/shard_map/all_to_all | solution.py:262
  88.2 34.2 %collective-permute-start.8 = (bf16[64,6144]{1,0:T(8,128)(2,1)}, bf16[64,6144]{1,0:T(8,128)(2,1)}, u32[]{:S(2)}, u32[]{:S(2)}) collective-permute-start(bf16[64,6144]{1,0:T(8,128)(2,1)} %get-tuple-element.92), channel_id=1, source_target_pairs={{0,112},{2,114},{4,116},{6,118},{8,120},{10,122},{12,124},{14,126}... | collective-permute-start | bytes 2359304 | tf_op jit(solution)/shard_map/ppermute | solution.py:270
  91.2 32.8 %collective-permute-start.9 = (bf16[64,6144]{1,0:T(8,128)(2,1)}, bf16[64,6144]{1,0:T(8,128)(2,1)}, u32[]{:S(2)}, u32[]{:S(2)}) collective-permute-start(bf16[64,6144]{1,0:T(8,128)(2,1)} %get-tuple-element.82), channel_id=1, source_target_pairs={{0,16},{2,18},{4,20},{6,22},{8,24},{10,26},{12,28},{14,30},{16,32}... | collective-permute-start | bytes 2359304 | tf_op jit(solution)/shard_map/ppermute | solution.py:270
  93.4 1.1 copy-start.5
  94.6 7.9 %copy-start.9 = (bf16[3072,256]{0,1:T(8,128)(2,1)S(1)}, bf16[3072,256]{0,1:T(8,128)(2,1)}, u32[]{:S(2)}) copy-start(bf16[3072,256]{0,1:T(8,128)(2,1)} %get-tuple-element.87) | copy-start | bytes 4718596
  94.6 32.0 %all-to-all-start.3 = ((bf16[8,16,6144]{2,1,0:T(8,128)(2,1)}), bf16[8,16,6144]{2,1,0:T(8,128)(2,1)}, u32[]{:S(2)}, u32[]{:S(2)}) async-start(bf16[8,16,6144]{2,1,0:T(8,128)(2,1)} %bitcast.60), calls=%async_computation.3 | async-start | bytes 3145728 | tf_op jit(solution)/shard_map/all_to_all | solution.py:262
  100.2 20.3 %collective-permute-start.4 = (bf16[64,3072]{1,0:T(8,128)(2,1)}, bf16[64,3072]{1,0:T(8,128)(2,1)}, u32[]{:S(2)}, u32[]{:S(2)}) collective-permute-start(bf16[64,3072]{1,0:T(8,128)(2,1)} %get-tuple-element.80), channel_id=1, source_target_pairs={{0,16},{2,18},{4,20},{6,22},{8,24},{10,26},{12,28},{14,30},{16,32}... | collective-permute-start | bytes 1179656 | tf_op jit(solution)/shard_map/ppermute | solution.py:270
  100.2 21.8 %collective-permute-start.6 = (bf16[64,3072]{1,0:T(8,128)(2,1)}, bf16[64,3072]{1,0:T(8,128)(2,1)}, u32[]{:S(2)}, u32[]{:S(2)}) collective-permute-start(bf16[64,3072]{1,0:T(8,128)(2,1)} %get-tuple-element.81), channel_id=1, source_target_pairs={{0,112},{2,114},{4,116},{6,118},{8,120},{10,122},{12,124},{14,126}... | collective-permute-start | bytes 1179656 | tf_op jit(solution)/shard_map/ppermute | solution.py:270
  102.5 0.8 copy-start.17
  103.2 2.7 %copy-start.3 = (bf16[1,1,128,3072]{2,3,1,0:T(8,128)(2,1)S(1)}, bf16[1,1,128,3072]{2,3,1,0:T(8,128)(2,1)}, u32[]{:S(2)}) copy-start(bf16[1,1,128,3072]{2,3,1,0:T(8,128)(2,1)} %all-gather.2) | copy-start | bytes 2359300
  109.6 22.5 %collective-permute-start.10 = (bf16[64,3200]{1,0:T(8,128)(2,1)}, bf16[64,3200]{1,0:T(8,128)(2,1)}, u32[]{:S(2)}, u32[]{:S(2)}) collective-permute-start(bf16[64,3200]{1,0:T(8,128)(2,1)} %get-tuple-element.90), channel_id=1, source_target_pairs={{0,16},{2,18},{4,20},{6,22},{8,24},{10,26},{12,28},{14,30},{16,32}... | collective-permute-start | bytes 1228808 | tf_op jit(solution)/shard_map/ppermute | solution.py:270
  120.4 11.6 %collective-permute-start.11 = (bf16[64,3200]{1,0:T(8,128)(2,1)S(1)}, bf16[64,3200]{1,0:T(8,128)(2,1)}, u32[]{:S(2)}, u32[]{:S(2)}) collective-permute-start(bf16[64,3200]{1,0:T(8,128)(2,1)S(1)} %get-tuple-element.91), channel_id=1, source_target_pairs={{0,112},{2,114},{4,116},{6,118},{8,120},{10,122},{12,124},{14,126}... | collective-permute-start | bytes 1228808 | tf_op jit(solution)/shard_map/ppermute | solution.py:270
  121.9 13.9 %collective-permute-start.5 = (bf16[64,3072]{1,0:T(8,128)(2,1)}, bf16[64,3072]{1,0:T(8,128)(2,1)}, u32[]{:S(2)}, u32[]{:S(2)}) collective-permute-start(bf16[64,3072]{1,0:T(8,128)(2,1)} %collective-permute-done.4), channel_id=1, source_target_pairs={{0,16},{2,18},{4,20},{6,22},{8,24},{10,26},{12,28},{14,30},{16,32}... | collective-permute-start | bytes 1179656 | tf_op jit(solution)/shard_map/ppermute | solution.py:270
  122.5 13.3 %collective-permute-start.7 = (bf16[64,3072]{1,0:T(8,128)(2,1)}, bf16[64,3072]{1,0:T(8,128)(2,1)}, u32[]{:S(2)}, u32[]{:S(2)}) collective-permute-start(bf16[64,3072]{1,0:T(8,128)(2,1)} %collective-permute-done.6), channel_id=1, source_target_pairs={{0,112},{2,114},{4,116},{6,118},{8,120},{10,122},{12,124},{14,126}... | collective-permute-start | bytes 1179656 | tf_op jit(solution)/shard_map/ppermute | solution.py:270
  126.6 21.6 %all-to-all-start.4 = ((bf16[8,16,6144]{2,1,0:T(8,128)(2,1)}), bf16[8,16,6144]{2,1,0:T(8,128)(2,1)}, u32[]{:S(2)}, u32[]{:S(2)}) async-start(bf16[8,16,6144]{2,1,0:T(8,128)(2,1)} %pad_maximum_fusion.3), calls=%async_computation.4 | async-start | bytes 3145728 | tf_op jit(solution)/shard_map/all_to_all | solution.py:262
  135.8 20.7 %collective-permute-start.14 = (bf16[64,3200]{1,0:T(8,128)(2,1)}, bf16[64,3200]{1,0:T(8,128)(2,1)}, u32[]{:S(2)}, u32[]{:S(2)}) collective-permute-start(bf16[64,3200]{1,0:T(8,128)(2,1)} %get-tuple-element.107), channel_id=1, source_target_pairs={{0,32},{2,34},{4,36},{6,38},{8,40},{10,42},{12,44},{14,46},{16,48}... | collective-permute-start | bytes 1228808 | tf_op jit(solution)/shard_map/ppermute | solution.py:270
  138.4 18.1 %collective-permute-start.15 = (bf16[64,3200]{1,0:T(8,128)(2,1)S(1)}, bf16[64,3200]{1,0:T(8,128)(2,1)}, u32[]{:S(2)}, u32[]{:S(2)}) collective-permute-start(bf16[64,3200]{1,0:T(8,128)(2,1)S(1)} %get-tuple-element.108), channel_id=1, source_target_pairs={{0,96},{2,98},{4,100},{6,102},{8,104},{10,106},{12,108},{14,110},{... | collective-permute-start | bytes 1228808 | tf_op jit(solution)/shard_map/ppermute | solution.py:270
  148.2 16.3 %all-to-all-start.5 = ((bf16[8,8,6144]{2,1,0:T(8,128)(2,1)}), bf16[8,8,6144]{2,1,0:T(8,128)(2,1)}, u32[]{:S(2)}, u32[]{:S(2)}) async-start(bf16[8,8,6144]{2,1,0:T(8,128)(2,1)} %maximum_bitcast_fusion), calls=%async_computation.5 | async-start | bytes 1572864 | tf_op jit(solution)/shard_map/all_to_all | solution.py:262
  156.5 39.3 %collective-permute-start.12 = (bf16[64,3200]{1,0:T(8,128)(2,1)}, bf16[64,3200]{1,0:T(8,128)(2,1)}, u32[]{:S(2)}, u32[]{:S(2)}) collective-permute-start(bf16[64,3200]{1,0:T(8,128)(2,1)} %get-tuple-element.102), channel_id=1, source_target_pairs={{0,48},{2,50},{4,52},{6,54},{8,56},{10,58},{12,60},{14,62},{16,64}... | collective-permute-start | bytes 1228808 | tf_op jit(solution)/shard_map/ppermute | solution.py:270
  160.1 46.3 %collective-permute-start.13 = (bf16[64,3200]{1,0:T(8,128)(2,1)}, bf16[64,3200]{1,0:T(8,128)(2,1)}, u32[]{:S(2)}, u32[]{:S(2)}) collective-permute-start(bf16[64,3200]{1,0:T(8,128)(2,1)} %get-tuple-element.103), channel_id=1, source_target_pairs={{0,80},{2,82},{4,84},{6,86},{8,88},{10,90},{12,92},{14,94},{16,96}... | collective-permute-start | bytes 1228808 | tf_op jit(solution)/shard_map/ppermute | solution.py:270
  161.6 2.9 %copy-start.1 = (bf16[256,3072]{1,0:T(8,128)(2,1)S(1)}, bf16[256,3072]{1,0:T(8,128)(2,1)}, u32[]{:S(2)}) copy-start(bf16[256,3072]{1,0:T(8,128)(2,1)} %copy-done) | copy-start | bytes 4718596
  164.5 1.1 copy-start.4
  168.5 37.9 %collective-permute-start.16 = (bf16[64,3200]{1,0:T(8,128)(2,1)}, bf16[64,3200]{1,0:T(8,128)(2,1)}, u32[]{:S(2)}, u32[]{:S(2)}) collective-permute-start(bf16[64,3200]{1,0:T(8,128)(2,1)} %get-tuple-element.115), channel_id=1, source_target_pairs={{0,64},{2,66},{4,68},{6,70},{8,72},{10,74},{12,76},{14,78},{16,80}... | collective-permute-start | bytes 1228808 | tf_op jit(solution)/shard_map/ppermute | solution.py:270
  172.0 36.8 %all-to-all-start.6 = ((bf16[8,32,3200]{2,1,0:T(8,128)(2,1)}), bf16[8,32,3200]{2,1,0:T(8,128)(2,1)S(1)}, u32[]{:S(2)}, u32[]{:S(2)}) async-start(bf16[8,32,3200]{2,1,0:T(8,128)(2,1)} %pad_maximum_fusion), calls=%async_computation.6 | async-start | bytes 3276800 | tf_op jit(solution)/shard_map/all_to_all | solution.py:262
  190.2 4.8 %collective-permute-start.19 = (bf16[128,1536]{1,0:T(8,128)(2,1)S(1)}, bf16[128,1536]{1,0:T(8,128)(2,1)S(1)}, u32[]{:S(2)}, u32[]{:S(2)}) collective-permute-start(bf16[128,1536]{1,0:T(8,128)(2,1)S(1)} %constant_dynamic-slice_fusion), channel_id=1, source_target_pairs={{0,1},{1,0},{2,3},{3,2},{4,5},{5,4},{6,7},{7,6},{8,9},{9,8},{10,11... | collective-permute-start | bytes 1179656 | tf_op jit(solution)/shard_map/ppermute | solution.py:278
  194.5 18.9 %collective-permute-start.18 = (bf16[1536,256]{1,0:T(8,128)(2,1)}, bf16[1536,256]{1,0:T(8,128)(2,1)}, u32[]{:S(2)}, u32[]{:S(2)}) collective-permute-start(bf16[1536,256]{1,0:T(8,128)(2,1)} %constant_dynamic-slice_fusion.1), channel_id=1, source_target_pairs={{0,1},{1,0},{2,3},{3,2},{4,5},{5,4},{6,7},{7,6},{8,9},{9,8},{10,11... | collective-permute-start | bytes 2359304 | tf_op jit(solution)/shard_map/ppermute | solution.py:278
  208.7 21.0 %all-to-all-start.7 = ((bf16[8,24,3200]{2,1,0:T(8,128)(2,1)}), bf16[8,24,3200]{2,1,0:T(8,128)(2,1)}, u32[]{:S(2)}, u32[]{:S(2)}) async-start(bf16[8,24,3200]{2,1,0:T(8,128)(2,1)} %pad_maximum_fusion.4), calls=%async_computation.7 | async-start | bytes 2457600 | tf_op jit(solution)/shard_map/all_to_all | solution.py:262
  213.4 2.4 copy-start.16
  213.4 2.6 %copy-start.10 = (f32[128,3072]{1,0:T(8,128)S(1)}, f32[128,3072]{1,0:T(8,128)}, u32[]{:S(2)}) copy-start(f32[128,3072]{1,0:T(8,128)} %fusion.23) | copy-start | bytes 4718596
  216.1 13.7 %copy-start.15 = (bf16[256,192]{1,0:T(8,128)(2,1)S(1)}, bf16[256,192]{1,0:T(8,128)(2,1)}, u32[]{:S(2)}) copy-start(bf16[256,192]{1,0:T(8,128)(2,1)} %get-tuple-element.123) | copy-start | bytes 294916
  230.8 4.3 %copy-start.18 = (bf16[256,64]{1,0:T(8,128)(2,1)S(1)}, bf16[256,64]{1,0:T(8,128)(2,1)}, u32[]{:S(2)}) copy-start(bf16[256,64]{1,0:T(8,128)(2,1)} %get-tuple-element.74) | copy-start | bytes 98308
  230.8 5.2 %copy-start.19 = (bf16[1,128,2]{1,2,0:T(2,128)(2,1)S(1)}, bf16[1,128,2]{1,2,0:T(2,128)(2,1)}, u32[]{:S(2)}) copy-start(bf16[1,128,2]{1,2,0:T(2,128)(2,1)} %param.9) | copy-start | bytes 1540
  232.5 18.3 %collective-permute-start.17 = (bf16[128,3072]{1,0:T(8,128)(2,1)S(1)}, bf16[128,3072]{1,0:T(8,128)(2,1)S(1)}, u32[]{:S(2)}, u32[]{:S(2)}) collective-permute-start(bf16[128,3072]{1,0:T(8,128)(2,1)S(1)} %fusion.4), channel_id=1, source_target_pairs={{0,128},{128,0},{1,129},{129,1},{2,130},{130,2},{3,131},{131,3},{4... | collective-permute-start | bytes 2359304 | tf_op jit(solution)/shard_map/ppermute | solution.py:379

commit v3 on v2

--- a/solution.py
+++ b/solution.py
@@ -308,7 +308,6 @@
         return exchanged(send, IN_PLANE), before
 
     came = [exchanged(rows_for([raw]), IN_PLANE)]
-    picks = own_picks(z, ids)
     gate_full = lax.all_gather(w_gate[0, 0], "dp", axis=0, tiled=True)
     up_full = lax.all_gather(w_up[0, 0], "dp", axis=0, tiled=True)
     down_full = lax.all_gather(w_down[0, 0], "dp", axis=1, tiled=True)
@@ -318,7 +317,7 @@
     act, back = expert_pass(came[0].reshape(-1, 2 * width), 1, COST, *weights)
     acts, backs = [act] + [None] * 4, [None] * 5
     back_0 = exchanged(back[0].reshape(EXPERTS_PLANE, group, width + LANES), IN_PLANE)
-    from_p1, from_m1, weights, picks, acts[0] = tie((from_p1, from_m1, weights, picks, acts[0]))
+    from_p1, from_m1, weights, acts[0], ids = tie((from_p1, from_m1, weights, acts[0], ids))
 
     from_m2, from_p2 = along_z(from_m1, 1), along_z(from_p1, -1)
 
@@ -332,6 +331,9 @@
 
     got, back_0 = in_plane(rows_for([from_p1, from_m1]), back_0)
     came.append(got)
+
+    picks = own_picks(z, ids)
+    from_m2, from_p2, picks = tie((from_m2, from_p2, picks))
 
     near_a, near_b, far_a, far_b = onward_rows(z, from_m2, from_p2)
     from_m3, from_p3 = along_z(near_a, 1), along_z(near_b, -1)

time: 254 us -> 252 us (level)
  waiting for transfers between devices: 81.3 us -> 73.2 us
  starting transfers between devices: 73.7 us -> 77.9 us
    ppermute x17, waiting for transfers between devices: 47.5 us -> 41 us  [along_z(): lax.ppermute(array, 'expert', [(i, (i + step) % size) for i in range(size)])]
    ppermute x17, starting transfers between devices: 28.1 us -> 32.9 us  [along_z(): lax.ppermute(array, 'expert', [(i, (i + step) % size) for i in range(size)])]
    unnamed x46 -> x44, local copies, waits for them, and re-layouts: 10.6 us -> 10.5 us
  transfers between devices with their start and end apart: 28 -> 28, of which waited for: 7 -> 9; matrix products, arithmetic and copies ran while one was open for 17% -> 18% of each run, Pallas kernels for 12% -> 12%
where the time goes in v3:
time: 252 us; the launch traced here: 249 us
  starting transfers between devices  77.9 us (31%)
  waiting for transfers between devices  73.2 us (29%)
  Pallas kernels  30.3 us (12%)
  matrix products  22.5 us (9%)
  local copies, waits for them, and re-layouts  17.4 us (7%)
  other arithmetic  17.3 us (7%)
  blocking collectives  9.18 us (4%)
    all_to_all x8, starting transfers between devices, exchanged(): lax.all_to_all(array, 'expert', split_axis=0, concat_axis=0, tiled=True,...  41.5 us
    ppermute x17, waiting for transfers between devices, along_z(): lax.ppermute(array, 'expert', [(i, (i + step) % size) for i in range(size)])  41 us
    ppermute x17, starting transfers between devices, along_z(): lax.ppermute(array, 'expert', [(i, (i + step) % size) for i in range(size)])  32.9 us
    all_to_all x8, waiting for transfers between devices, exchanged(): lax.all_to_all(array, 'expert', split_axis=0, concat_axis=0, tiled=True,...  18.9 us
    pallas_call x5, Pallas kernels, expert_pass(): pl.pallas_call(expert_kernel, out_shape=[jax.ShapeDtypeStruct((count, hid...  16.6 us
    dot_general x10, matrix products, contract_rows(): lax.dot_general(former, latter, (((0,), (0,)), ((), ())), preferred_eleme...  15.8 us
    ppermute x1, waiting for transfers between devices, body(): grad = lax.ppermute(grad, 'section', back_by_one)  13.3 us
    unnamed x44, local copies, waits for them, and re-layouts  10.5 us
  transfers between devices with their start and end apart: 28, of which 9 were waited for; matrix products, arithmetic and copies ran while one was open for 18% of the time, Pallas kernels for 12%

profile of v3, /device:TPU:32, one launch (start us, length us, event | category | flops | bytes accessed | tf_op | source)
XLA Modules:
  0.0 248.8 jit_solution(7594625104289997086)
XLA Ops:
  3.8 2.0 collective-permute-start.1
  5.9 2.4 plane_rows.3
  8.3 5.5 %all-to-all-start = ((bf16[8,8,6144]{2,1,0:T(8,128)(2,1)}), bf16[8,8,6144]{2,1,0:T(8,128)(2,1)}, u32[]{:S(2)}, u32[]{:S(2)}) async-start(bf16[8,8,6144]{2,1,0:T(8,128)(2,1)} %bitcast.10), calls=%async_computation | async-start | bytes 1572864 | tf_op jit(solution)/shard_map/all_to_all | solution.py:262
  14.0 2.6 %all-gather = bf16[1,1,3072,128]{2,3,1,0:T(8,128)(2,1)} all-gather(bf16[1,1,1536,128]{2,3,1,0:T(8,128)(2,1)S(1)} %copy.35), channel_id=2, replica_groups=mesh['section'=2,'expert'=64,'dp'=2] {'dp'}, dimensions={2}, use_global_device_ids=true | all-gather | bytes 1179648 | tf_op jit(solution)/shard_map/all_gather | solution.py:311
  16.8 2.5 %all-gather.1 = bf16[1,1,3072,128]{2,3,1,0:T(8,128)(2,1)} all-gather(bf16[1,1,1536,128]{2,3,1,0:T(8,128)(2,1)S(1)} %copy.36), channel_id=3, replica_groups=mesh['section'=2,'expert'=64,'dp'=2] {'dp'}, dimensions={2}, use_global_device_ids=true | all-gather | bytes 1179648 | tf_op jit(solution)/shard_map/all_gather | solution.py:312
  20.3 2.9 %fusion.53 = (bf16[256,3072]{1,0:T(8,128)(2,1)S(1)}, bf16[3072,256]{0,1:T(8,128)(2,1)}) fusion(bf16[3072,128]{0,1:T(8,128)(2,1)} %bitcast.66, bf16[3072,128]{0,1:T(8,128)(2,1)} %bitcast.65), kind=kLoop, calls=%fused_computation.80 | loop fusion | flops 3145728 | bytes 4718592 | tf_op jit(solution)/shard_map/transpose | solution.py:315
  23.2 3.2 %copy.38.wgu_ref = bf16[3072,256]{1,0:T(8,128)(2,1)} copy(bf16[3072,256]{0,1:T(8,128)(2,1)} %get-tuple-element.93) | data formatting | bytes 3145728 | tf_op jit(solution)/shard_map/concatenate | solution.py:314
  26.3 4.0 %all-gather.2 = bf16[1,1,128,3072]{2,3,1,0:T(8,128)(2,1)} all-gather(bf16[1,1,128,1536]{2,3,1,0:T(8,128)(2,1)} %copy.37), channel_id=4, replica_groups=mesh['section'=2,'expert'=64,'dp'=2] {'dp'}, dimensions={3}, use_global_device_ids=true | all-gather | bytes 1179648 | tf_op jit(solution)/shard_map/all_gather | solution.py:313
  32.9 2.2 expert_rows.5
  35.9 5.7 %all-to-all-start.1 = ((bf16[8,8,3200]{2,1,0:T(8,128)(2,1)}), bf16[8,8,3200]{2,1,0:T(8,128)(2,1)}, u32[]{:S(2)}, u32[]{:S(2)}) async-start(bf16[8,8,3200]{2,1,0:T(8,128)(2,1)} %bitcast.62), calls=%async_computation.1 | async-start | bytes 819200 | tf_op jit(solution)/shard_map/all_to_all | solution.py:262
  42.7 3.1 %collective-permute-start.2 = (bf16[128,6272]{1,0:T(8,128)(2,1)}, bf16[128,6272]{1,0:T(8,128)(2,1)S(1)}, u32[]{:S(2)}, u32[]{:S(2)}) collective-permute-start(bf16[128,6272]{1,0:T(8,128)(2,1)} %collective-permute-done.1.refs_1_.refs_3_), channel_id=1, source_target_pairs={{0,16},{2,18},{4,20},{6,22},{8,24},{10,26},{12,28},{14,30},{16,32}... | collective-permute-start | bytes 4816904 | tf_op jit(solution)/shard_map/ppermute | solution.py:270
  45.8 3.7 %plane_rows.4 = bf16[128,6144]{1,0:T(8,128)(2,1)S(1)} custom-call(s32[1]{0:T(128)} %bitcast.9.z_ref, bf16[128,6272]{1,0:T(8,128)(2,1)} %collective-permute-done.refs_0_.refs_2_, bf16[128,6272]{1,0:T(8,128)(2,1)} %collective-permute-done.1.refs_1_.refs_3_, bf16[128,6272]{1,0:T(8,128)(2,1)} %collective-permute-done.refs_0_.refs_2_, ...), custom_call_target="tpu_custom_call" | custom-call | tf_op jit(solution)/shard_map/plane_rows/pallas_call | solution.py:89
  51.0 5.3 %all-to-all-start.2 = ((bf16[8,16,6144]{2,1,0:T(8,128)(2,1)}), bf16[8,16,6144]{2,1,0:T(8,128)(2,1)}, u32[]{:S(2)}, u32[]{:S(2)}) async-start(bf16[8,16,6144]{2,1,0:T(8,128)(2,1)} %bitcast.61), calls=%async_computation.2 | async-start | bytes 3145728 | tf_op jit(solution)/shard_map/all_to_all | solution.py:262
  56.4 2.1 own_picks.1
  58.4 22.8 %collective-permute-done.2.mark_a.row_a.refs_1_.refs_3_ = bf16[128,6272]{1,0:T(8,128)(2,1)S(1)} collective-permute-done((bf16[128,6272]{1,0:T(8,128)(2,1)}, bf16[128,6272]{1,0:T(8,128)(2,1)S(1)}, u32[]{:S(2)}, u32[]{:S(2)}) %collective-permute-start.2) | collective-permute-done | bytes 1605664 | tf_op jit(solution)/shard_map/ppermute | solution.py:270
  82.6 3.3 %onward_rows.1 = (bf16[64,6144]{1,0:T(8,128)(2,1)}, bf16[64,6144]{1,0:T(8,128)(2,1)}, bf16[64,3072]{1,0:T(8,128)(2,1)}, bf16[64,3072]{1,0:T(8,128)(2,1)}) custom-call(s32[1]{0:T(128)} %bitcast.9.z_ref, bf16[128,6272]{1,0:T(8,128)(2,1)S(1)} %collective-permute-done.2.mark_a.row_a.refs_1_.refs_3_, ...), custom_call_target="tpu_custom_call" | custom-call | tf_op jit(solution)/shard_map/onward_rows/pallas_call | solution.py:142
  88.4 2.2 plane_rows.5
  91.8 5.4 %all-to-all-start.3 = ((bf16[8,16,6144]{2,1,0:T(8,128)(2,1)}), bf16[8,16,6144]{2,1,0:T(8,128)(2,1)}, u32[]{:S(2)}, u32[]{:S(2)}) async-start(bf16[8,16,6144]{2,1,0:T(8,128)(2,1)} %bitcast.60), calls=%async_computation.3 | async-start | bytes 3145728 | tf_op jit(solution)/shard_map/all_to_all | solution.py:262
  97.2 3.0 %collective-permute-start.4 = (bf16[64,3072]{1,0:T(8,128)(2,1)}, bf16[64,3072]{1,0:T(8,128)(2,1)}, u32[]{:S(2)}, u32[]{:S(2)}) collective-permute-start(bf16[64,3072]{1,0:T(8,128)(2,1)} %get-tuple-element.86), channel_id=1, source_target_pairs={{0,16},{2,18},{4,20},{6,22},{8,24},{10,26},{12,28},{14,30},{16,32}... | collective-permute-start | bytes 1179656 | tf_op jit(solution)/shard_map/ppermute | solution.py:270
  100.2 1.8 copy.39.wgu_ref
  102.0 3.7 %expert_rows.6 = (bf16[128,384]{1,0:T(8,128)(2,1)S(1)}, bf16[64,3200]{1,0:T(8,128)(2,1)}, bf16[64,3200]{1,0:T(8,128)(2,1)S(1)}) custom-call(bf16[128,6144]{1,0:T(8,128)(2,1)} %bitcast.17.row_ref, bf16[3072,256]{1,0:T(8,128)(2,1)S(1)} %copy.39.wgu_ref, bf16[256,3072]{1,0:T(8,128)(2,1)} %copy-done, bf16[3072,128]{1,0:T(8,128)(2,1)S(1)} %bitcast.56), custom_call_target="tpu_custom_call" | custom-call | flops 1 | bytes 3145728 | tf_op jit(solution)/shard_map/expert_rows/pallas_call | solution.py:249
  105.7 3.2 %collective-permute-start.10 = (bf16[64,3200]{1,0:T(8,128)(2,1)}, bf16[64,3200]{1,0:T(8,128)(2,1)}, u32[]{:S(2)}, u32[]{:S(2)}) collective-permute-start(bf16[64,3200]{1,0:T(8,128)(2,1)} %get-tuple-element.96), channel_id=1, source_target_pairs={{0,16},{2,18},{4,20},{6,22},{8,24},{10,26},{12,28},{14,30},{16,32}... | collective-permute-start | bytes 1228808 | tf_op jit(solution)/shard_map/ppermute | solution.py:270
  109.0 2.5 fusion.23
  111.5 6.2 %collective-permute-done.4 = bf16[64,3072]{1,0:T(8,128)(2,1)} collective-permute-done((bf16[64,3072]{1,0:T(8,128)(2,1)}, bf16[64,3072]{1,0:T(8,128)(2,1)}, u32[]{:S(2)}, u32[]{:S(2)}) %collective-permute-start.4) | collective-permute-done | bytes 393248 | tf_op jit(solution)/shard_map/ppermute | solution.py:270
  117.7 3.2 %collective-permute-start.11 = (bf16[64,3200]{1,0:T(8,128)(2,1)S(1)}, bf16[64,3200]{1,0:T(8,128)(2,1)}, u32[]{:S(2)}, u32[]{:S(2)}) collective-permute-start(bf16[64,3200]{1,0:T(8,128)(2,1)S(1)} %get-tuple-element.97), channel_id=1, source_target_pairs={{0,112},{2,114},{4,116},{6,118},{8,120},{10,122},{12,124},{14,126}... | collective-permute-start | bytes 1228808 | tf_op jit(solution)/shard_map/ppermute | solution.py:270
  120.9 2.0 collective-permute-start.7
  122.9 2.7 %pad_maximum_fusion.3 = bf16[8,16,6144]{2,1,0:T(8,128)(2,1)} fusion(bf16[8,8,6144]{2,1,0:T(8,128)(2,1)} %bitcast.19, bf16[8,8,6144]{2,1,0:T(8,128)(2,1)} %bitcast.18), kind=kLoop, calls=%fused_computation.17 | loop fusion | flops 3145728 | bytes 3145728 | tf_op jit(solution)/shard_map/concatenate | solution.py:284
  125.6 5.4 %all-to-all-start.4 = ((bf16[8,16,6144]{2,1,0:T(8,128)(2,1)}), bf16[8,16,6144]{2,1,0:T(8,128)(2,1)}, u32[]{:S(2)}, u32[]{:S(2)}) async-start(bf16[8,16,6144]{2,1,0:T(8,128)(2,1)} %pad_maximum_fusion.3), calls=%async_computation.4 | async-start | bytes 3145728 | tf_op jit(solution)/shard_map/all_to_all | solution.py:262
  131.0 3.7 %expert_rows.7 = (bf16[128,384]{1,0:T(8,128)(2,1)S(1)}, bf16[64,3200]{1,0:T(8,128)(2,1)}, bf16[64,3200]{1,0:T(8,128)(2,1)S(1)}) custom-call(bf16[128,6144]{1,0:T(8,128)(2,1)} %bitcast.20.row_ref, bf16[3072,256]{1,0:T(8,128)(2,1)S(1)} %copy.39.wgu_ref, bf16[256,3072]{1,0:T(8,128)(2,1)} %copy-done, bf16[3072,128]{1,0:T(8,128)(2,1)S(1)} %bitcast.57), custom_call_target="tpu_custom_call" | custom-call | flops 60000002048 | bytes 3145728 | tf_op jit(solution)/shard_map/expert_rows/pallas_call | solution.py:249
  134.8 3.2 %collective-permute-start.14 = (bf16[64,3200]{1,0:T(8,128)(2,1)}, bf16[64,3200]{1,0:T(8,128)(2,1)}, u32[]{:S(2)}, u32[]{:S(2)}) collective-permute-start(bf16[64,3200]{1,0:T(8,128)(2,1)} %get-tuple-element.113), channel_id=1, source_target_pairs={{0,32},{2,34},{4,36},{6,38},{8,40},{10,42},{12,44},{14,46},{16,48}... | collective-permute-start | bytes 1228808 | tf_op jit(solution)/shard_map/ppermute | solution.py:270
  138.9 2.0 maximum_bitcast_fusion
  140.9 6.0 %all-to-all-done.4 = bf16[8,16,6144]{2,1,0:T(8,128)(2,1)} async-done(((bf16[8,16,6144]{2,1,0:T(8,128)(2,1)}), bf16[8,16,6144]{2,1,0:T(8,128)(2,1)}, u32[]{:S(2)}, u32[]{:S(2)}) %all-to-all-start.4) | async-done | bytes 1572896 | tf_op jit(solution)/shard_map/all_to_all | solution.py:262
  146.9 4.2 %all-to-all-start.5 = ((bf16[8,8,6144]{2,1,0:T(8,128)(2,1)}), bf16[8,8,6144]{2,1,0:T(8,128)(2,1)}, u32[]{:S(2)}, u32[]{:S(2)}) async-start(bf16[8,8,6144]{2,1,0:T(8,128)(2,1)} %maximum_bitcast_fusion), calls=%async_computation.5 | async-start | bytes 1572864 | tf_op jit(solution)/shard_map/all_to_all | solution.py:262
  151.1 4.1 %expert_rows.8 = (bf16[128,384]{1,0:T(8,128)(2,1)S(1)}, bf16[64,3200]{1,0:T(8,128)(2,1)}, bf16[64,3200]{1,0:T(8,128)(2,1)}) custom-call(bf16[128,6144]{1,0:T(8,128)(2,1)} %bitcast.22.row_ref, bf16[3072,256]{1,0:T(8,128)(2,1)S(1)} %copy.39.wgu_ref, bf16[256,3072]{1,0:T(8,128)(2,1)} %copy-done, bf16[3072,128]{1,0:T(8,128)(2,1)S(1)} %bitcast.58), custom_call_target="tpu_custom_call" | custom-call | flops 60000002048 | bytes 3145728 | tf_op jit(solution)/shard_map/expert_rows/pallas_call | solution.py:249
  155.2 4.3 %collective-permute-start.12 = (bf16[64,3200]{1,0:T(8,128)(2,1)}, bf16[64,3200]{1,0:T(8,128)(2,1)}, u32[]{:S(2)}, u32[]{:S(2)}) collective-permute-start(bf16[64,3200]{1,0:T(8,128)(2,1)} %get-tuple-element.108), channel_id=1, source_target_pairs={{0,48},{2,50},{4,52},{6,54},{8,56},{10,58},{12,60},{14,62},{16,64}... | collective-permute-start | bytes 1228808 | tf_op jit(solution)/shard_map/ppermute | solution.py:270
  160.4 2.9 %pad_maximum_fusion = bf16[8,32,3200]{2,1,0:T(8,128)(2,1)} fusion(bf16[8,8,3200]{2,1,0:T(8,128)(2,1)} %bitcast.30, bf16[8,8,3200]{2,1,0:T(8,128)(2,1)} %bitcast.29, bf16[8,8,3200]{2,1,0:T(8,128)(2,1)} %bitcast.28, bf16[8,8,3200]{2,1,0:T(8,128)(2,1)} %bitcast.27), kind=kLoop, calls=%fused_computation.13 | loop fusion | flops 6553600 | bytes 3276800 | tf_op jit(solution)/shard_map/concatenate | solution.py:284
  164.3 2.9 %expert_rows.9 = (bf16[64,384]{1,0:T(8,128)(2,1)S(1)}, bf16[64,3200]{1,0:T(8,128)(2,1)}) custom-call(bf16[64,6144]{1,0:T(8,128)(2,1)} %bitcast.25.row_ref, bf16[3072,256]{1,0:T(8,128)(2,1)S(1)} %copy.39.wgu_ref, bf16[256,3072]{1,0:T(8,128)(2,1)S(1)} %copy-done.1, bf16[3072,128]{1,0:T(8,128)(2,1)S(1)} %bitcast.59), custom_call_target="tpu_custom_call" | custom-call | flops 1 | bytes 3145728 | tf_op jit(solution)/shard_map/expert_rows/pallas_call | solution.py:249
  167.3 4.5 %collective-permute-start.16 = (bf16[64,3200]{1,0:T(8,128)(2,1)}, bf16[64,3200]{1,0:T(8,128)(2,1)}, u32[]{:S(2)}, u32[]{:S(2)}) collective-permute-start(bf16[64,3200]{1,0:T(8,128)(2,1)} %get-tuple-element.121), channel_id=1, source_target_pairs={{0,64},{2,66},{4,68},{6,70},{8,72},{10,74},{12,76},{14,78},{16,80}... | collective-permute-start | bytes 1228808 | tf_op jit(solution)/shard_map/ppermute | solution.py:270
  171.7 5.6 %all-to-all-start.6 = ((bf16[8,32,3200]{2,1,0:T(8,128)(2,1)}), bf16[8,32,3200]{2,1,0:T(8,128)(2,1)S(1)}, u32[]{:S(2)}, u32[]{:S(2)}) async-start(bf16[8,32,3200]{2,1,0:T(8,128)(2,1)} %pad_maximum_fusion), calls=%async_computation.6 | async-start | bytes 3276800 | tf_op jit(solution)/shard_map/all_to_all | solution.py:262
  178.7 1.7 fusion.15
  182.0 1.7 fusion.13
  185.3 1.7 fusion.11
  195.6 9.6 %collective-permute-done.13 = bf16[64,3200]{1,0:T(8,128)(2,1)} collective-permute-done((bf16[64,3200]{1,0:T(8,128)(2,1)}, bf16[64,3200]{1,0:T(8,128)(2,1)}, u32[]{:S(2)}, u32[]{:S(2)}) %collective-permute-start.13) | collective-permute-done | bytes 409632 | tf_op jit(solution)/shard_map/ppermute | solution.py:270
  205.2 2.4 pad_maximum_fusion.4
  207.6 4.3 %all-to-all-start.7 = ((bf16[8,24,3200]{2,1,0:T(8,128)(2,1)}), bf16[8,24,3200]{2,1,0:T(8,128)(2,1)}, u32[]{:S(2)}, u32[]{:S(2)}) async-start(bf16[8,24,3200]{2,1,0:T(8,128)(2,1)} %pad_maximum_fusion.4), calls=%async_computation.7 | async-start | bytes 2457600 | tf_op jit(solution)/shard_map/all_to_all | solution.py:262
  215.0 12.6 %all-to-all-done.7 = bf16[8,24,3200]{2,1,0:T(8,128)(2,1)} async-done(((bf16[8,24,3200]{2,1,0:T(8,128)(2,1)}), bf16[8,24,3200]{2,1,0:T(8,128)(2,1)}, u32[]{:S(2)}, u32[]{:S(2)}) %all-to-all-start.7) | async-done | bytes 1228832 | tf_op jit(solution)/shard_map/all_to_all | solution.py:262
  230.2 2.9 %collective-permute-start.17 = (bf16[128,3072]{1,0:T(8,128)(2,1)S(1)}, bf16[128,3072]{1,0:T(8,128)(2,1)S(1)}, u32[]{:S(2)}, u32[]{:S(2)}) collective-permute-start(bf16[128,3072]{1,0:T(8,128)(2,1)S(1)} %fusion.4), channel_id=1, source_target_pairs={{0,128},{128,0},{1,129},{129,1},{2,130},{130,2},{3,131},{131,3},{4... | collective-permute-start | bytes 2359304 | tf_op jit(solution)/shard_map/ppermute | solution.py:381
  234.6 13.3 %collective-permute-done.17 = bf16[128,3072]{1,0:T(8,128)(2,1)S(1)} collective-permute-done((bf16[128,3072]{1,0:T(8,128)(2,1)S(1)}, bf16[128,3072]{1,0:T(8,128)(2,1)S(1)}, u32[]{:S(2)}, u32[]{:S(2)}) %collective-permute-start.17) | collective-permute-done | bytes 786464 | tf_op jit(solution)/shard_map/ppermute | solution.py:381
  (99 shorter events, 39.5 us)
Async XLA Ops:
  2.2 1.6 copy-start.10
  3.8 37.7 %collective-permute-start.1 = (bf16[128,6272]{1,0:T(8,128)(2,1)S(1)}, bf16[128,6272]{1,0:T(8,128)(2,1)}, u32[]{:S(2)}, u32[]{:S(2)}) collective-permute-start(bf16[128,6272]{1,0:T(8,128)(2,1)S(1)} %pad_maximum_fusion.1.refs_0_.refs_1_), channel_id=1, source_target_pairs={{0,16},{2,18},{4,20},{6,22},{8,24},{10,26},{12,28},{14,30},{16,32}... | collective-permute-start | bytes 4816904 | tf_op jit(solution)/shard_map/ppermute | solution.py:270
  5.8 36.8 %collective-permute-start = (bf16[128,6272]{1,0:T(8,128)(2,1)S(1)}, bf16[128,6272]{1,0:T(8,128)(2,1)}, u32[]{:S(2)}, u32[]{:S(2)}) collective-permute-start(bf16[128,6272]{1,0:T(8,128)(2,1)S(1)} %pad_maximum_fusion.1.refs_0_.refs_1_), channel_id=1, source_target_pairs={{0,112},{2,114},{4,116},{6,118},{8,120},{10,122},{12,124},{14,126}... | collective-permute-start | bytes 4816904 | tf_op jit(solution)/shard_map/ppermute | solution.py:270
  8.3 5.5 %copy-start.11 = (bf16[1,1,1536,128]{3,2,1,0:T(8,128)(2,1)S(1)}, bf16[1,1,1536,128]{3,2,1,0:T(8,128)(2,1)}, u32[]{:S(2)}) copy-start(bf16[1,1,1536,128]{3,2,1,0:T(8,128)(2,1)} %param.11) | copy-start | bytes 1179652
  8.3 8.4 %copy-start.12 = (bf16[1,1,1536,128]{3,2,1,0:T(8,128)(2,1)S(1)}, bf16[1,1,1536,128]{3,2,1,0:T(8,128)(2,1)}, u32[]{:S(2)}) copy-start(bf16[1,1,1536,128]{3,2,1,0:T(8,128)(2,1)} %param.12) | copy-start | bytes 1179652
  8.3 22.1 %all-to-all-start = ((bf16[8,8,6144]{2,1,0:T(8,128)(2,1)}), bf16[8,8,6144]{2,1,0:T(8,128)(2,1)}, u32[]{:S(2)}, u32[]{:S(2)}) async-start(bf16[8,8,6144]{2,1,0:T(8,128)(2,1)} %bitcast.10), calls=%async_computation | async-start | bytes 1572864 | tf_op jit(solution)/shard_map/all_to_all | solution.py:262
  14.0 5.3 %copy-start.13 = (bf16[1,1,128,1536]{3,2,1,0:T(8,128)(2,1)S(1)}, bf16[1,1,128,1536]{3,2,1,0:T(8,128)(2,1)}, u32[]{:S(2)}) copy-start(bf16[1,1,128,1536]{3,2,1,0:T(8,128)(2,1)} %param.13) | copy-start | bytes 1179652
  23.2 7.2 %copy-start = (bf16[256,3072]{1,0:T(8,128)(2,1)}, bf16[256,3072]{1,0:T(8,128)(2,1)S(1)}, u32[]{:S(2)}) copy-start(bf16[256,3072]{1,0:T(8,128)(2,1)S(1)} %get-tuple-element.94.wgu_t_ref) | copy-start | bytes 4718596
  30.4 1.1 copy-start.2
  31.5 1.4 copy-start.7
  35.1 0.8 copy-start.8
  35.9 15.2 %all-to-all-start.1 = ((bf16[8,8,3200]{2,1,0:T(8,128)(2,1)}), bf16[8,8,3200]{2,1,0:T(8,128)(2,1)}, u32[]{:S(2)}, u32[]{:S(2)}) async-start(bf16[8,8,3200]{2,1,0:T(8,128)(2,1)} %bitcast.62), calls=%async_computation.1 | async-start | bytes 819200 | tf_op jit(solution)/shard_map/all_to_all | solution.py:262
  42.7 38.6 %collective-permute-start.2 = (bf16[128,6272]{1,0:T(8,128)(2,1)}, bf16[128,6272]{1,0:T(8,128)(2,1)S(1)}, u32[]{:S(2)}, u32[]{:S(2)}) collective-permute-start(bf16[128,6272]{1,0:T(8,128)(2,1)} %collective-permute-done.1.refs_1_.refs_3_), channel_id=1, source_target_pairs={{0,16},{2,18},{4,20},{6,22},{8,24},{10,26},{12,28},{14,30},{16,32}... | collective-permute-start | bytes 4816904 | tf_op jit(solution)/shard_map/ppermute | solution.py:270
  45.8 36.8 %collective-permute-start.3 = (bf16[128,6272]{1,0:T(8,128)(2,1)}, bf16[128,6272]{1,0:T(8,128)(2,1)S(1)}, u32[]{:S(2)}, u32[]{:S(2)}) collective-permute-start(bf16[128,6272]{1,0:T(8,128)(2,1)} %collective-permute-done.refs_0_.refs_2_), channel_id=1, source_target_pairs={{0,112},{2,114},{4,116},{6,118},{8,120},{10,122},{12,124},{14,126}... | collective-permute-start | bytes 4816904 | tf_op jit(solution)/shard_map/ppermute | solution.py:270
  49.5 1.2 copy-start.6
  51.0 40.8 %all-to-all-start.2 = ((bf16[8,16,6144]{2,1,0:T(8,128)(2,1)}), bf16[8,16,6144]{2,1,0:T(8,128)(2,1)}, u32[]{:S(2)}, u32[]{:S(2)}) async-start(bf16[8,16,6144]{2,1,0:T(8,128)(2,1)} %bitcast.61), calls=%async_computation.2 | async-start | bytes 3145728 | tf_op jit(solution)/shard_map/all_to_all | solution.py:262
  85.9 35.0 %collective-permute-start.8 = (bf16[64,6144]{1,0:T(8,128)(2,1)}, bf16[64,6144]{1,0:T(8,128)(2,1)}, u32[]{:S(2)}, u32[]{:S(2)}) collective-permute-start(bf16[64,6144]{1,0:T(8,128)(2,1)} %get-tuple-element.98), channel_id=1, source_target_pairs={{0,112},{2,114},{4,116},{6,118},{8,120},{10,122},{12,124},{14,126}... | collective-permute-start | bytes 2359304 | tf_op jit(solution)/shard_map/ppermute | solution.py:270
  87.5 35.4 %collective-permute-start.9 = (bf16[64,6144]{1,0:T(8,128)(2,1)}, bf16[64,6144]{1,0:T(8,128)(2,1)}, u32[]{:S(2)}, u32[]{:S(2)}) collective-permute-start(bf16[64,6144]{1,0:T(8,128)(2,1)} %get-tuple-element.88), channel_id=1, source_target_pairs={{0,16},{2,18},{4,20},{6,22},{8,24},{10,26},{12,28},{14,30},{16,32}... | collective-permute-start | bytes 2359304 | tf_op jit(solution)/shard_map/ppermute | solution.py:270
  90.7 1.2 copy-start.5
  91.8 33.8 %all-to-all-start.3 = ((bf16[8,16,6144]{2,1,0:T(8,128)(2,1)}), bf16[8,16,6144]{2,1,0:T(8,128)(2,1)}, u32[]{:S(2)}, u32[]{:S(2)}) async-start(bf16[8,16,6144]{2,1,0:T(8,128)(2,1)} %bitcast.60), calls=%async_computation.3 | async-start | bytes 3145728 | tf_op jit(solution)/shard_map/all_to_all | solution.py:262
  97.2 20.4 %collective-permute-start.4 = (bf16[64,3072]{1,0:T(8,128)(2,1)}, bf16[64,3072]{1,0:T(8,128)(2,1)}, u32[]{:S(2)}, u32[]{:S(2)}) collective-permute-start(bf16[64,3072]{1,0:T(8,128)(2,1)} %get-tuple-element.86), channel_id=1, source_target_pairs={{0,16},{2,18},{4,20},{6,22},{8,24},{10,26},{12,28},{14,30},{16,32}... | collective-permute-start | bytes 1179656 | tf_op jit(solution)/shard_map/ppermute | solution.py:270
  100.2 20.7 %collective-permute-start.6 = (bf16[64,3072]{1,0:T(8,128)(2,1)}, bf16[64,3072]{1,0:T(8,128)(2,1)}, u32[]{:S(2)}, u32[]{:S(2)}) collective-permute-start(bf16[64,3072]{1,0:T(8,128)(2,1)} %get-tuple-element.87), channel_id=1, source_target_pairs={{0,112},{2,114},{4,116},{6,118},{8,120},{10,122},{12,124},{14,126}... | collective-permute-start | bytes 1179656 | tf_op jit(solution)/shard_map/ppermute | solution.py:270
  100.2 1.8 copy-start.3
  102.0 7.0 %copy-start.16 = (bf16[256,64]{1,0:T(8,128)(2,1)S(1)}, bf16[256,64]{1,0:T(8,128)(2,1)}, u32[]{:S(2)}) copy-start(bf16[256,64]{1,0:T(8,128)(2,1)} %get-tuple-element.80) | copy-start | bytes 98308
  105.7 25.3 %collective-permute-start.10 = (bf16[64,3200]{1,0:T(8,128)(2,1)}, bf16[64,3200]{1,0:T(8,128)(2,1)}, u32[]{:S(2)}, u32[]{:S(2)}) collective-permute-start(bf16[64,3200]{1,0:T(8,128)(2,1)} %get-tuple-element.96), channel_id=1, source_target_pairs={{0,16},{2,18},{4,20},{6,22},{8,24},{10,26},{12,28},{14,30},{16,32}... | collective-permute-start | bytes 1228808 | tf_op jit(solution)/shard_map/ppermute | solution.py:270
  117.7 13.4 %collective-permute-start.11 = (bf16[64,3200]{1,0:T(8,128)(2,1)S(1)}, bf16[64,3200]{1,0:T(8,128)(2,1)}, u32[]{:S(2)}, u32[]{:S(2)}) collective-permute-start(bf16[64,3200]{1,0:T(8,128)(2,1)S(1)} %get-tuple-element.97), channel_id=1, source_target_pairs={{0,112},{2,114},{4,116},{6,118},{8,120},{10,122},{12,124},{14,126}... | collective-permute-start | bytes 1228808 | tf_op jit(solution)/shard_map/ppermute | solution.py:270
  120.9 13.9 %collective-permute-start.5 = (bf16[64,3072]{1,0:T(8,128)(2,1)}, bf16[64,3072]{1,0:T(8,128)(2,1)}, u32[]{:S(2)}, u32[]{:S(2)}) collective-permute-start(bf16[64,3072]{1,0:T(8,128)(2,1)} %collective-permute-done.4), channel_id=1, source_target_pairs={{0,16},{2,18},{4,20},{6,22},{8,24},{10,26},{12,28},{14,30},{16,32}... | collective-permute-start | bytes 1179656 | tf_op jit(solution)/shard_map/ppermute | solution.py:270
  120.9 13.9 %collective-permute-start.7 = (bf16[64,3072]{1,0:T(8,128)(2,1)}, bf16[64,3072]{1,0:T(8,128)(2,1)}, u32[]{:S(2)}, u32[]{:S(2)}) collective-permute-start(bf16[64,3072]{1,0:T(8,128)(2,1)} %collective-permute-done.6), channel_id=1, source_target_pairs={{0,112},{2,114},{4,116},{6,118},{8,120},{10,122},{12,124},{14,126}... | collective-permute-start | bytes 1179656 | tf_op jit(solution)/shard_map/ppermute | solution.py:270
  125.6 21.3 %all-to-all-start.4 = ((bf16[8,16,6144]{2,1,0:T(8,128)(2,1)}), bf16[8,16,6144]{2,1,0:T(8,128)(2,1)}, u32[]{:S(2)}, u32[]{:S(2)}) async-start(bf16[8,16,6144]{2,1,0:T(8,128)(2,1)} %pad_maximum_fusion.3), calls=%async_computation.4 | async-start | bytes 3145728 | tf_op jit(solution)/shard_map/all_to_all | solution.py:262
  134.8 20.5 %collective-permute-start.14 = (bf16[64,3200]{1,0:T(8,128)(2,1)}, bf16[64,3200]{1,0:T(8,128)(2,1)}, u32[]{:S(2)}, u32[]{:S(2)}) collective-permute-start(bf16[64,3200]{1,0:T(8,128)(2,1)} %get-tuple-element.113), channel_id=1, source_target_pairs={{0,32},{2,34},{4,36},{6,38},{8,40},{10,42},{12,44},{14,46},{16,48}... | collective-permute-start | bytes 1228808 | tf_op jit(solution)/shard_map/ppermute | solution.py:270
  137.9 17.3 %collective-permute-start.15 = (bf16[64,3200]{1,0:T(8,128)(2,1)S(1)}, bf16[64,3200]{1,0:T(8,128)(2,1)}, u32[]{:S(2)}, u32[]{:S(2)}) collective-permute-start(bf16[64,3200]{1,0:T(8,128)(2,1)S(1)} %get-tuple-element.114), channel_id=1, source_target_pairs={{0,96},{2,98},{4,100},{6,102},{8,104},{10,106},{12,108},{14,110},{... | collective-permute-start | bytes 1228808 | tf_op jit(solution)/shard_map/ppermute | solution.py:270
  146.9 16.3 %all-to-all-start.5 = ((bf16[8,8,6144]{2,1,0:T(8,128)(2,1)}), bf16[8,8,6144]{2,1,0:T(8,128)(2,1)}, u32[]{:S(2)}, u32[]{:S(2)}) async-start(bf16[8,8,6144]{2,1,0:T(8,128)(2,1)} %maximum_bitcast_fusion), calls=%async_computation.5 | async-start | bytes 1572864 | tf_op jit(solution)/shard_map/all_to_all | solution.py:262
  155.2 40.4 %collective-permute-start.12 = (bf16[64,3200]{1,0:T(8,128)(2,1)}, bf16[64,3200]{1,0:T(8,128)(2,1)}, u32[]{:S(2)}, u32[]{:S(2)}) collective-permute-start(bf16[64,3200]{1,0:T(8,128)(2,1)} %get-tuple-element.108), channel_id=1, source_target_pairs={{0,48},{2,50},{4,52},{6,54},{8,56},{10,58},{12,60},{14,62},{16,64}... | collective-permute-start | bytes 1228808 | tf_op jit(solution)/shard_map/ppermute | solution.py:270
  159.5 45.6 %collective-permute-start.13 = (bf16[64,3200]{1,0:T(8,128)(2,1)}, bf16[64,3200]{1,0:T(8,128)(2,1)}, u32[]{:S(2)}, u32[]{:S(2)}) collective-permute-start(bf16[64,3200]{1,0:T(8,128)(2,1)} %get-tuple-element.109), channel_id=1, source_target_pairs={{0,80},{2,82},{4,84},{6,86},{8,88},{10,90},{12,92},{14,94},{16,96}... | collective-permute-start | bytes 1228808 | tf_op jit(solution)/shard_map/ppermute | solution.py:270
  160.4 2.9 %copy-start.1 = (bf16[256,3072]{1,0:T(8,128)(2,1)S(1)}, bf16[256,3072]{1,0:T(8,128)(2,1)}, u32[]{:S(2)}) copy-start(bf16[256,3072]{1,0:T(8,128)(2,1)} %copy-done) | copy-start | bytes 4718596
  163.2 1.1 copy-start.4
  167.3 37.9 %collective-permute-start.16 = (bf16[64,3200]{1,0:T(8,128)(2,1)}, bf16[64,3200]{1,0:T(8,128)(2,1)}, u32[]{:S(2)}, u32[]{:S(2)}) collective-permute-start(bf16[64,3200]{1,0:T(8,128)(2,1)} %get-tuple-element.121), channel_id=1, source_target_pairs={{0,64},{2,66},{4,68},{6,70},{8,72},{10,74},{12,76},{14,78},{16,80}... | collective-permute-start | bytes 1228808 | tf_op jit(solution)/shard_map/ppermute | solution.py:270
  171.7 35.9 %all-to-all-start.6 = ((bf16[8,32,3200]{2,1,0:T(8,128)(2,1)}), bf16[8,32,3200]{2,1,0:T(8,128)(2,1)S(1)}, u32[]{:S(2)}, u32[]{:S(2)}) async-start(bf16[8,32,3200]{2,1,0:T(8,128)(2,1)} %pad_maximum_fusion), calls=%async_computation.6 | async-start | bytes 3276800 | tf_op jit(solution)/shard_map/all_to_all | solution.py:262
  190.0 4.8 %collective-permute-start.19 = (bf16[128,1536]{1,0:T(8,128)(2,1)S(1)}, bf16[128,1536]{1,0:T(8,128)(2,1)S(1)}, u32[]{:S(2)}, u32[]{:S(2)}) collective-permute-start(bf16[128,1536]{1,0:T(8,128)(2,1)S(1)} %constant_dynamic-slice_fusion), channel_id=1, source_target_pairs={{0,1},{1,0},{2,3},{3,2},{4,5},{5,4},{6,7},{7,6},{8,9},{9,8},{10,11... | collective-permute-start | bytes 1179656 | tf_op jit(solution)/shard_map/ppermute | solution.py:278
  194.3 17.6 %collective-permute-start.18 = (bf16[1536,256]{1,0:T(8,128)(2,1)}, bf16[1536,256]{1,0:T(8,128)(2,1)}, u32[]{:S(2)}, u32[]{:S(2)}) collective-permute-start(bf16[1536,256]{1,0:T(8,128)(2,1)} %constant_dynamic-slice_fusion.1), channel_id=1, source_target_pairs={{0,1},{1,0},{2,3},{3,2},{4,5},{5,4},{6,7},{7,6},{8,9},{9,8},{10,11... | collective-permute-start | bytes 2359304 | tf_op jit(solution)/shard_map/ppermute | solution.py:278
  207.6 19.9 %all-to-all-start.7 = ((bf16[8,24,3200]{2,1,0:T(8,128)(2,1)}), bf16[8,24,3200]{2,1,0:T(8,128)(2,1)}, u32[]{:S(2)}, u32[]{:S(2)}) async-start(bf16[8,24,3200]{2,1,0:T(8,128)(2,1)} %pad_maximum_fusion.4), calls=%async_computation.7 | async-start | bytes 2457600 | tf_op jit(solution)/shard_map/all_to_all | solution.py:262
  211.9 2.4 copy-start.15
  211.9 2.6 %copy-start.9 = (f32[128,3072]{1,0:T(8,128)S(1)}, f32[128,3072]{1,0:T(8,128)}, u32[]{:S(2)}) copy-start(f32[128,3072]{1,0:T(8,128)} %fusion.23) | copy-start | bytes 4718596
  214.5 13.0 %copy-start.14 = (bf16[256,192]{1,0:T(8,128)(2,1)S(1)}, bf16[256,192]{1,0:T(8,128)(2,1)}, u32[]{:S(2)}) copy-start(bf16[256,192]{1,0:T(8,128)(2,1)} %get-tuple-element.129) | copy-start | bytes 294916
  228.6 4.6 %copy-start.17 = (bf16[256,64]{1,0:T(8,128)(2,1)S(1)}, bf16[256,64]{1,0:T(8,128)(2,1)}, u32[]{:S(2)}) copy-start(bf16[256,64]{1,0:T(8,128)(2,1)} %get-tuple-element.80) | copy-start | bytes 98308
  228.6 5.5 %copy-start.18 = (bf16[1,128,2]{1,2,0:T(2,128)(2,1)S(1)}, bf16[1,128,2]{1,2,0:T(2,128)(2,1)}, u32[]{:S(2)}) copy-start(bf16[1,128,2]{1,2,0:T(2,128)(2,1)} %param.9) | copy-start | bytes 1540
  230.2 17.7 %collective-permute-start.17 = (bf16[128,3072]{1,0:T(8,128)(2,1)S(1)}, bf16[128,3072]{1,0:T(8,128)(2,1)S(1)}, u32[]{:S(2)}, u32[]{:S(2)}) collective-permute-start(bf16[128,3072]{1,0:T(8,128)(2,1)S(1)} %fusion.4), channel_id=1, source_target_pairs={{0,128},{128,0},{1,129},{129,1},{2,130},{130,2},{3,131},{131,3},{4... | collective-permute-start | bytes 2359304 | tf_op jit(solution)/shard_map/ppermute | solution.py:381

commit v4 on v3

--- a/solution.py
+++ b/solution.py
@@ -58,8 +58,8 @@
 
 
 def plane_kernel(count, x_steps, z_ref, *refs):
-    mark_refs, row_refs = refs[:count], refs[count : 2 * count]
-    out_ref, table = refs[2 * count :]
+    mark_refs, tok_refs, up_refs = refs[:count], refs[count : 2 * count], refs[2 * count : 3 * count]
+    out_ref, table = refs[3 * count :]
     step = pl.program_id(0)
 
     @pl.when(step == 0)
@@ -69,20 +69,27 @@
             table[2 * place] = plain
             table[2 * place + 1] = scaled
 
-    kind = (step >= x_steps).astype(jnp.int32)
-    total = None
-    for place in range(count):
-        part = jnp.dot(
-            table[2 * place + kind], row_refs[place][...], preferred_element_type=jnp.float32
-        )
-        total = part if total is None else total + part
-    out_ref[...] = total.astype(jnp.bfloat16)
-
-
-def plane_rows(z, sources):
-    rows, full = sources[0].shape
-    count = len(sources)
-    width = (full - LANES) // 2
+    def product(kind, sides):
+        total = None
+        for place in range(count):
+            part = jnp.dot(
+                table[2 * place + kind], sides[place][...], preferred_element_type=jnp.float32
+            )
+            total = part if total is None else total + part
+        out_ref[...] = total.astype(jnp.bfloat16)
+
+    @pl.when(step < x_steps)
+    def _():
+        product(0, tok_refs)
+
+    @pl.when(step >= x_steps)
+    def _():
+        product(1, up_refs)
+
+
+def plane_rows(z, toks, ups):
+    rows, width = ups[0].shape
+    count = len(toks)
     total = EXPERTS_PLANE * rows // TOK_MB * CAP * count
     tile = width // 2
     steps = width // tile
@@ -90,17 +97,18 @@
         functools.partial(plane_kernel, count, steps),
         grid=(2 * steps,),
         in_specs=[pl.BlockSpec(memory_space=pltpu.SMEM)]
-        + [pl.BlockSpec((rows, LANES), lambda i: (0, 2 * width // LANES))] * count
-        + [pl.BlockSpec((rows, tile), lambda i: (0, i))] * count,
+        + [pl.BlockSpec((rows, LANES), lambda i: (0, width // LANES))] * count
+        + [pl.BlockSpec((rows, tile), lambda i: (0, jnp.minimum(i, steps - 1)))] * count
+        + [pl.BlockSpec((rows, tile), lambda i: (0, jnp.maximum(i - steps, 0)))] * count,
         out_specs=pl.BlockSpec((total, tile), lambda i: (0, i)),
         out_shape=jax.ShapeDtypeStruct((total, 2 * width), jnp.bfloat16),
         scratch_shapes=[pltpu.VMEM((2 * count, total, rows), jnp.bfloat16)],
         compiler_params=pltpu.CompilerParams(vmem_limit_bytes=VMEM_LIMIT),
         name="plane_rows",
-    )(z, *sources, *sources)
-
-
-def onward_kernel(steps, z_ref, mark_a, mark_b, row_a, row_b, near_a, near_b, far_a, far_b, table):
+    )(z, *toks, *toks, *ups)
+
+
+def onward_kernel(steps, z_ref, mark_a, mark_b, tok_a, tok_b, up_a, up_b, near_a, near_b, far_a, far_b, table):
     step = pl.program_id(0)
     slots = near_a.shape[0]
 
@@ -118,31 +126,31 @@
 
     @pl.when(step < steps)
     def _():
-        both = product(table[0], row_a)
+        both = product(table[0], tok_a)
         near_a[...] = both[:slots]
         far_a[...] = both[slots:]
-        near_b[...] = product(table[2, :slots, :], row_b)
+        near_b[...] = product(table[2, :slots, :], tok_b)
 
     @pl.when(step >= steps)
     def _():
-        near_a[...] = product(table[1, :slots, :], row_a)
-        both = product(table[3], row_b)
+        near_a[...] = product(table[1, :slots, :], up_a)
+        both = product(table[3], up_b)
         near_b[...] = both[:slots]
         far_b[...] = both[slots:]
 
 
-def onward_rows(z, source_a, source_b):
-    rows, full = source_a.shape
-    width = (full - LANES) // 2
+def onward_rows(z, tok_a, tok_b, up_a, up_b):
+    rows, width = up_a.shape
     total = EXPERTS_PLANE * rows // TOK_MB * CAP
     tile = width // 2
     steps = width // tile
-    marks = pl.BlockSpec((rows, LANES), lambda i: (0, 2 * width // LANES))
-    block = pl.BlockSpec((rows, tile), lambda i: (0, i))
+    marks = pl.BlockSpec((rows, LANES), lambda i: (0, width // LANES))
+    early = pl.BlockSpec((rows, tile), lambda i: (0, jnp.minimum(i, steps - 1)))
+    late = pl.BlockSpec((rows, tile), lambda i: (0, jnp.maximum(i - steps, 0)))
     return pl.pallas_call(
         functools.partial(onward_kernel, steps),
         grid=(2 * steps,),
-        in_specs=[pl.BlockSpec(memory_space=pltpu.SMEM), marks, marks, block, block],
+        in_specs=[pl.BlockSpec(memory_space=pltpu.SMEM), marks, marks, early, early, late, late],
         out_specs=[
             pl.BlockSpec((total, tile), lambda i: (0, i)),
             pl.BlockSpec((total, tile), lambda i: (0, i)),
@@ -154,7 +162,7 @@
         scratch_shapes=[pltpu.VMEM((4, 2 * total, rows), jnp.bfloat16)],
         compiler_params=pltpu.CompilerParams(vmem_limit_bytes=VMEM_LIMIT),
         name="onward_rows",
-    )(z, source_a, source_b, source_a, source_b)
+    )(z, tok_a, tok_b, tok_a, tok_b, up_a, up_b)
 
 
 def own_kernel(z_ref, ids_ref, *pick_refs):
@@ -196,6 +204,7 @@
             jax.ShapeDtypeStruct((2 * rows, group * len(offsets)), jnp.bfloat16)
             for offsets in RETURNS
         ],
+        cost_estimate=pl.CostEstimate(flops=COST, bytes_accessed=1 << 17, transcendentals=0),
         name="own_picks",
     )(z, ids)
 
@@ -295,19 +304,20 @@
     z = (lax.axis_index("expert") // EXPERTS_PLANE).astype(jnp.int32).reshape(1)
     tie = lax.optimization_barrier
 
+    up_m1, up_p1 = along_z(upstream, 1), along_z(upstream, -1)
     marks = jnp.concatenate([ids.astype(jnp.bfloat16), comb], axis=1)
-    raw = jnp.concatenate([tokens, upstream, jnp.pad(marks, ((0, 0), (0, LANES - 4)))], axis=1)
-    from_m1, from_p1 = along_z(raw, 1), along_z(raw, -1)
-
-    def rows_for(sources):
-        send = plane_rows(z, sources)
-        return send.reshape(EXPERTS_PLANE, group * len(sources), 2 * width)
+    marked = jnp.concatenate([tokens, jnp.pad(marks, ((0, 0), (0, LANES - 4)))], axis=1)
+    tok_m1, tok_p1 = along_z(marked, 1), along_z(marked, -1)
+
+    def rows_for(toks, ups):
+        send = plane_rows(z, toks, ups)
+        return send.reshape(EXPERTS_PLANE, group * len(toks), 2 * width)
 
     def in_plane(send, before):
         send, before = tie((send, before))
         return exchanged(send, IN_PLANE), before
 
-    came = [exchanged(rows_for([raw]), IN_PLANE)]
+    came = [exchanged(rows_for([marked], [upstream]), IN_PLANE)]
     gate_full = lax.all_gather(w_gate[0, 0], "dp", axis=0, tiled=True)
     up_full = lax.all_gather(w_up[0, 0], "dp", axis=0, tiled=True)
     down_full = lax.all_gather(w_down[0, 0], "dp", axis=1, tiled=True)
@@ -317,9 +327,10 @@
     act, back = expert_pass(came[0].reshape(-1, 2 * width), 1, COST, *weights)
     acts, backs = [act] + [None] * 4, [None] * 5
     back_0 = exchanged(back[0].reshape(EXPERTS_PLANE, group, width + LANES), IN_PLANE)
-    from_p1, from_m1, weights, acts[0], ids = tie((from_p1, from_m1, weights, acts[0], ids))
-
-    from_m2, from_p2 = along_z(from_m1, 1), along_z(from_p1, -1)
+    tok_p1, tok_m1, weights, acts[0], ids = tie((tok_p1, tok_m1, weights, acts[0], ids))
+
+    up_m2, up_p2 = along_z(up_m1, 1), along_z(up_p1, -1)
+    tok_m2, tok_p2 = along_z(tok_m1, 1), along_z(tok_p1, -1)
 
     def expert(turn, cost=1):
         return expert_pass(
@@ -329,29 +340,30 @@
             *weights,
         )
 
-    got, back_0 = in_plane(rows_for([from_p1, from_m1]), back_0)
+    tok_p1, tok_m1, _ = tie((tok_p1, tok_m1, (up_m2, up_p2)))
+    got, back_0 = in_plane(rows_for([tok_p1, tok_m1], [up_p1, up_m1]), back_0)
     came.append(got)
 
     picks = own_picks(z, ids)
-    from_m2, from_p2, picks = tie((from_m2, from_p2, picks))
-
-    near_a, near_b, far_a, far_b = onward_rows(z, from_m2, from_p2)
+    tok_m2, tok_p2, picks = tie((tok_m2, tok_p2, picks))
+
+    near_a, near_b, far_a, far_b = onward_rows(z, tok_m2, tok_p2, up_m2, up_p2)
     from_m3, from_p3 = along_z(near_a, 1), along_z(near_b, -1)
-    four_a = along_z(along_z(far_a, 1), 1)
-    four_b = along_z(along_z(far_b, -1), -1)
-    from_p2, from_m2, near_a = tie((from_p2, from_m2, near_a))
-    send, came[1] = tie((rows_for([from_p2, from_m2]), came[1]))
+    three = side_by_side([from_p3, from_m3])
+    far_a, far_b = along_z(far_a, 1), along_z(far_b, -1)
+    tok_p2, tok_m2, near_a = tie((tok_p2, tok_m2, near_a))
+    send, came[1] = tie((rows_for([tok_p2, tok_m2], [up_p2, up_m2]), came[1]))
     came.append(exchanged(send, IN_PLANE))
 
     acts[1], backs[1] = expert(1)
-    send = side_by_side([from_p3, from_m3])
-    got, came[2] = in_plane(send, came[2])
+    got, came[2] = in_plane(three, came[2])
     came.append(got)
 
     first = [along_z(backs[1][i], by) for i, by in enumerate(CHUNKS[1])]
-    came[2], first = tie((came[2], first))
     acts[2], backs[2] = expert(2, COST)
-    four_a, four_b, backs[1], backs[2] = tie((four_a, four_b, backs[1], backs[2]))
+    far_a, far_b, _ = tie((far_a, far_b, backs[2]))
+    four_a, four_b = along_z(far_a, 1), along_z(far_b, -1)
+    four_a, four_b, first = tie((four_a, four_b, first))
     send = jnp.concatenate([four_a, four_b], axis=1).reshape(EXPERTS_PLANE, group, 2 * width)
     got, came[3] = in_plane(send, came[3])
     came.append(got)

time: 252 us -> 246 us (0.976)
  waiting for transfers between devices: 73.2 us -> 65.1 us
  local copies, waits for them, and re-layouts: 17.4 us -> 20.2 us
    all_to_all x8, waiting for transfers between devices: 18.9 us -> 13.2 us  [exchanged(): lax.all_to_all(array, 'expert', split_axis=0, concat_axis=0, tiled=True,...]
    dot_general x10, matrix products: 15.8 us -> 11.5 us  [contract_rows(): lax.dot_general(former, latter, (((0,), (0,)), ((), ())), preferred_eleme...]
    unnamed x44 -> x64, local copies, waits for them, and re-layouts: 10.5 us -> 13.3 us
    ppermute x17 -> x21, waiting for transfers between devices: 41 us -> 40.1 us  [along_z(): lax.ppermute(array, 'expert', [(i, (i + step) % size) for i in range(size)])]
    ppermute x17 -> x21, starting transfers between devices: 32.9 us -> 32.5 us  [along_z(): lax.ppermute(array, 'expert', [(i, (i + step) % size) for i in range(size)])]
  transfers between devices with their start and end apart: 28 -> 32, of which waited for: 9 -> 12; matrix products, arithmetic and copies ran while one was open for 18% -> 18% of each run, Pallas kernels for 12% -> 13%
where the time goes in v4:
time: 246 us; the launch traced here: 243 us
  starting transfers between devices  77.3 us (31%)
  waiting for transfers between devices  65.1 us (26%)
  Pallas kernels  32.6 us (13%)
  local copies, waits for them, and re-layouts  20.2 us (8%)
  matrix products  20 us (8%)
  other arithmetic  17.2 us (7%)
  blocking collectives  9.18 us (4%)
    all_to_all x8, starting transfers between devices, exchanged(): lax.all_to_all(array, 'expert', split_axis=0, concat_axis=0, tiled=True,...  41.6 us
    ppermute x21, waiting for transfers between devices, along_z(): lax.ppermute(array, 'expert', [(i, (i + step) % size) for i in range(size)])  40.1 us
    ppermute x21, starting transfers between devices, along_z(): lax.ppermute(array, 'expert', [(i, (i + step) % size) for i in range(size)])  32.5 us
    pallas_call x5, Pallas kernels, expert_pass(): pl.pallas_call(expert_kernel, out_shape=[jax.ShapeDtypeStruct((count, hid...  15.4 us
    unnamed x64, local copies, waits for them, and re-layouts  13.3 us
    all_to_all x8, waiting for transfers between devices, exchanged(): lax.all_to_all(array, 'expert', split_axis=0, concat_axis=0, tiled=True,...  13.2 us
    ppermute x1, waiting for transfers between devices, body(): grad = lax.ppermute(grad, 'section', back_by_one)  11.8 us
    dot_general x10, matrix products, contract_rows(): lax.dot_general(former, latter, (((0,), (0,)), ((), ())), preferred_eleme...  11.5 us
  transfers between devices with their start and end apart: 32, of which 12 were waited for; matrix products, arithmetic and copies ran while one was open for 18% of the time, Pallas kernels for 13%

profile of v4, /device:TPU:32, one launch (start us, length us, event | category | flops | bytes accessed | tf_op | source)
XLA Modules:
  0.0 242.8 jit_solution(1596450468489551125)
XLA Ops:
  7.6 2.1 collective-permute-start
  9.7 2.4 plane_rows.3
  12.2 5.5 %all-to-all-start = ((bf16[8,8,6144]{2,1,0:T(8,128)(2,1)}), bf16[8,8,6144]{2,1,0:T(8,128)(2,1)S(1)}, u32[]{:S(2)}, u32[]{:S(2)}) async-start(bf16[8,8,6144]{2,1,0:T(8,128)(2,1)} %bitcast.10), calls=%async_computation | async-start | bytes 1572864 | tf_op jit(solution)/shard_map/all_to_all | solution.py:271
  17.9 2.6 %all-gather = bf16[1,1,3072,128]{2,3,1,0:T(8,128)(2,1)} all-gather(bf16[1,1,1536,128]{2,3,1,0:T(8,128)(2,1)S(1)} %copy.35), channel_id=2, replica_groups=mesh['section'=2,'expert'=64,'dp'=2] {'dp'}, dimensions={2}, use_global_device_ids=true | all-gather | bytes 1179648 | tf_op jit(solution)/shard_map/all_gather | solution.py:321
  20.7 2.5 %all-gather.1 = bf16[1,1,3072,128]{2,3,1,0:T(8,128)(2,1)} all-gather(bf16[1,1,1536,128]{2,3,1,0:T(8,128)(2,1)S(1)} %copy.36), channel_id=3, replica_groups=mesh['section'=2,'expert'=64,'dp'=2] {'dp'}, dimensions={2}, use_global_device_ids=true | all-gather | bytes 1179648 | tf_op jit(solution)/shard_map/all_gather | solution.py:322
  24.1 3.0 %fusion.53 = (bf16[256,3072]{1,0:T(8,128)(2,1)S(1)}, bf16[3072,256]{0,1:T(8,128)(2,1)}) fusion(bf16[3072,128]{0,1:T(8,128)(2,1)} %bitcast.75, bf16[3072,128]{0,1:T(8,128)(2,1)} %bitcast.74), kind=kLoop, calls=%fused_computation.80 | loop fusion | flops 3145728 | bytes 4718592 | tf_op jit(solution)/shard_map/transpose | solution.py:325
  27.1 3.2 %copy.38.wgu_ref = bf16[3072,256]{1,0:T(8,128)(2,1)} copy(bf16[3072,256]{0,1:T(8,128)(2,1)} %get-tuple-element.98) | data formatting | bytes 3145728 | tf_op jit(solution)/shard_map/concatenate | solution.py:324
  30.4 4.0 %all-gather.2 = bf16[1,1,128,3072]{2,3,1,0:T(8,128)(2,1)} all-gather(bf16[1,1,128,1536]{2,3,1,0:T(8,128)(2,1)} %copy.37), channel_id=4, replica_groups=mesh['section'=2,'expert'=64,'dp'=2] {'dp'}, dimensions={3}, use_global_device_ids=true | all-gather | bytes 1179648 | tf_op jit(solution)/shard_map/all_gather | solution.py:323
  34.4 3.2 %collective-permute-start.7 = (bf16[128,3072]{1,0:T(8,128)(2,1)}, bf16[128,3072]{1,0:T(8,128)(2,1)}, u32[]{:S(2)}, u32[]{:S(2)}) collective-permute-start(bf16[128,3072]{1,0:T(8,128)(2,1)} %collective-permute-done.6.refs_4_), channel_id=1, source_target_pairs={{0,112},{2,114},{4,116},{6,118},{8,120},{10,122},{12,124},{14,126}... | collective-permute-start | bytes 2359304 | tf_op jit(solution)/shard_map/ppermute | solution.py:279
  42.3 5.7 %all-to-all-start.1 = ((bf16[8,8,3200]{2,1,0:T(8,128)(2,1)}), bf16[8,8,3200]{2,1,0:T(8,128)(2,1)S(1)}, u32[]{:S(2)}, u32[]{:S(2)}) async-start(bf16[8,8,3200]{2,1,0:T(8,128)(2,1)} %bitcast.71), calls=%async_computation.1 | async-start | bytes 819200 | tf_op jit(solution)/shard_map/all_to_all | solution.py:271
  48.1 2.1 collective-permute-start.3
  50.2 5.6 %collective-permute-done.7.up_b.refs_4_ = bf16[128,3072]{1,0:T(8,128)(2,1)} collective-permute-done((bf16[128,3072]{1,0:T(8,128)(2,1)}, bf16[128,3072]{1,0:T(8,128)(2,1)}, u32[]{:S(2)}, u32[]{:S(2)}) %collective-permute-start.7) | collective-permute-done | bytes 786464 | tf_op jit(solution)/shard_map/ppermute | solution.py:279
  55.8 3.8 %collective-permute-done.5.up_a.refs_5_ = bf16[128,3072]{1,0:T(8,128)(2,1)} collective-permute-done((bf16[128,3072]{1,0:T(8,128)(2,1)}, bf16[128,3072]{1,0:T(8,128)(2,1)}, u32[]{:S(2)}, u32[]{:S(2)}) %collective-permute-start.5) | collective-permute-done | bytes 786464 | tf_op jit(solution)/shard_map/ppermute | solution.py:279
  59.6 4.0 %plane_rows.4 = bf16[128,6144]{1,0:T(8,128)(2,1)S(1)} custom-call(s32[1]{0:T(128)} %bitcast.8.z_ref, bf16[128,3200]{1,0:T(8,128)(2,1)} %collective-permute-done.refs_0_.refs_2_, bf16[128,3200]{1,0:T(8,128)(2,1)} %collective-permute-done.1.refs_1_.refs_3_, bf16[128,3200]{1,0:T(8,128)(2,1)} %collective-permute-done.refs_0_.refs_2_, ...), custom_call_target="tpu_custom_call" | custom-call | tf_op jit(solution)/shard_map/plane_rows/pallas_call | solution.py:96
  65.6 5.1 %all-to-all-start.2 = ((bf16[8,16,6144]{2,1,0:T(8,128)(2,1)}), bf16[8,16,6144]{2,1,0:T(8,128)(2,1)S(1)}, u32[]{:S(2)}, u32[]{:S(2)}) async-start(bf16[8,16,6144]{2,1,0:T(8,128)(2,1)} %bitcast.64), calls=%async_computation.2 | async-start | bytes 3145728 | tf_op jit(solution)/shard_map/all_to_all | solution.py:271
  70.7 2.1 own_picks.1
  72.8 3.4 %collective-permute-done.2.mark_a.tok_a.refs_1_.refs_3_ = bf16[128,3200]{1,0:T(8,128)(2,1)S(1)} collective-permute-done((bf16[128,3200]{1,0:T(8,128)(2,1)}, bf16[128,3200]{1,0:T(8,128)(2,1)S(1)}, u32[]{:S(2)}, u32[]{:S(2)}) %collective-permute-start.2) | collective-permute-done | bytes 819232 | tf_op jit(solution)/shard_map/ppermute | solution.py:279
  76.2 4.8 %onward_rows.1 = (bf16[64,6144]{1,0:T(8,128)(2,1)}, bf16[64,6144]{1,0:T(8,128)(2,1)}, bf16[64,3072]{1,0:T(8,128)(2,1)S(1)}, bf16[64,3072]{1,0:T(8,128)(2,1)S(1)}) custom-call(s32[1]{0:T(128)} %bitcast.8.z_ref, bf16[128,3200]{1,0:T(8,128)(2,1)S(1)} %collective-permute-done.2.mark_a.tok_a.refs_1_.refs_3_, ...), custom_call_target="tpu_custom_call" | custom-call | tf_op jit(solution)/shard_map/onward_rows/pallas_call | solution.py:150
  81.7 2.9 %collective-permute-start.10 = (bf16[64,6144]{1,0:T(8,128)(2,1)}, bf16[64,6144]{1,0:T(8,128)(2,1)}, u32[]{:S(2)}, u32[]{:S(2)}) collective-permute-start(bf16[64,6144]{1,0:T(8,128)(2,1)} %get-tuple-element.91), channel_id=1, source_target_pairs={{0,112},{2,114},{4,116},{6,118},{8,120},{10,122},{12,124},{14,126}... | collective-permute-start | bytes 2359304 | tf_op jit(solution)/shard_map/ppermute | solution.py:279
  84.6 3.9 %plane_rows.5 = bf16[128,6144]{1,0:T(8,128)(2,1)S(1)} custom-call(s32[1]{0:T(128)} %bitcast.8.z_ref, bf16[128,3200]{1,0:T(8,128)(2,1)} %collective-permute-done.3.mark_b.tok_b.refs_0_.refs_2_, bf16[128,3200]{1,0:T(8,128)(2,1)S(1)} %collective-permute-done.2.mark_a.tok_a.refs_1_.refs_3_, ...), custom_call_target="tpu_custom_call" | custom-call | tf_op jit(solution)/shard_map/plane_rows/pallas_call | solution.py:96
  91.0 4.3 %all-to-all-start.3 = ((bf16[8,16,6144]{2,1,0:T(8,128)(2,1)}), bf16[8,16,6144]{2,1,0:T(8,128)(2,1)}, u32[]{:S(2)}, u32[]{:S(2)}) async-start(bf16[8,16,6144]{2,1,0:T(8,128)(2,1)} %bitcast.63), calls=%async_computation.3 | async-start | bytes 3145728 | tf_op jit(solution)/shard_map/all_to_all | solution.py:271
  97.1 3.0 %collective-permute-start.9 = (bf16[64,3072]{1,0:T(8,128)(2,1)}, bf16[64,3072]{1,0:T(8,128)(2,1)}, u32[]{:S(2)}, u32[]{:S(2)}) collective-permute-start(bf16[64,3072]{1,0:T(8,128)(2,1)} %copy-done.15), channel_id=1, source_target_pairs={{0,112},{2,114},{4,116},{6,118},{8,120},{10,122},{12,124},{14,126}... | collective-permute-start | bytes 1179656 | tf_op jit(solution)/shard_map/ppermute | solution.py:279
  100.1 2.8 %collective-permute-done.10 = bf16[64,6144]{1,0:T(8,128)(2,1)} collective-permute-done((bf16[64,6144]{1,0:T(8,128)(2,1)}, bf16[64,6144]{1,0:T(8,128)(2,1)}, u32[]{:S(2)}, u32[]{:S(2)}) %collective-permute-start.10) | collective-permute-done | bytes 786464 | tf_op jit(solution)/shard_map/ppermute | solution.py:279
  102.9 2.5 %collective-permute-done.11 = bf16[64,6144]{1,0:T(8,128)(2,1)} collective-permute-done((bf16[64,6144]{1,0:T(8,128)(2,1)}, bf16[64,6144]{1,0:T(8,128)(2,1)}, u32[]{:S(2)}, u32[]{:S(2)}) %collective-permute-start.11) | collective-permute-done | bytes 786464 | tf_op jit(solution)/shard_map/ppermute | solution.py:279
  105.4 2.8 %pad_maximum_fusion.2 = bf16[8,16,6144]{2,1,0:T(8,128)(2,1)} fusion(bf16[8,8,6144]{2,1,0:T(8,128)(2,1)} %bitcast.17, bf16[8,8,6144]{2,1,0:T(8,128)(2,1)} %bitcast.16), kind=kLoop, calls=%fused_computation.16 | loop fusion | flops 3145728 | bytes 3145728 | tf_op jit(solution)/shard_map/concatenate | solution.py:293
  108.2 3.6 %expert_rows.7 = (bf16[128,384]{1,0:T(8,128)(2,1)S(1)}, bf16[64,3200]{1,0:T(8,128)(2,1)}, bf16[64,3200]{1,0:T(8,128)(2,1)}) custom-call(bf16[128,6144]{1,0:T(8,128)(2,1)S(1)} %bitcast.55, bf16[3072,256]{1,0:T(8,128)(2,1)S(1)} %copy.39.wgu_ref, bf16[256,3072]{1,0:T(8,128)(2,1)} %copy-done, bf16[3072,128]{1,0:T(8,128)(2,1)S(1)} %bitcast.59), custom_call_target="tpu_custom_call" | custom-call | flops 1 | bytes 3145728 | tf_op jit(solution)/shard_map/expert_rows/pallas_call | solution.py:258
  115.9 4.3 %all-to-all-start.4 = ((bf16[8,16,6144]{2,1,0:T(8,128)(2,1)}), bf16[8,16,6144]{2,1,0:T(8,128)(2,1)}, u32[]{:S(2)}, u32[]{:S(2)}) async-start(bf16[8,16,6144]{2,1,0:T(8,128)(2,1)} %pad_maximum_fusion.2), calls=%async_computation.4 | async-start | bytes 3145728 | tf_op jit(solution)/shard_map/all_to_all | solution.py:271
  120.2 3.7 %expert_rows.6 = (bf16[128,384]{1,0:T(8,128)(2,1)S(1)}, bf16[64,3200]{1,0:T(8,128)(2,1)}, bf16[64,3200]{1,0:T(8,128)(2,1)S(1)}) custom-call(bf16[128,6144]{1,0:T(8,128)(2,1)} %bitcast.19.row_ref, bf16[3072,256]{1,0:T(8,128)(2,1)S(1)} %copy.39.wgu_ref, bf16[256,3072]{1,0:T(8,128)(2,1)} %copy-done, bf16[3072,128]{1,0:T(8,128)(2,1)S(1)} %bitcast.60), custom_call_target="tpu_custom_call" | custom-call | flops 60000002048 | bytes 3145728 | tf_op jit(solution)/shard_map/expert_rows/pallas_call | solution.py:258
  124.0 2.3 collective-permute-start.13
  126.3 2.6 %fusion.23 = f32[128,3072]{1,0:T(8,128)} fusion(bf16[64,3200]{1,0:T(8,128)(2,1)} %bitcast.76, bf16[256,64]{1,0:T(8,128)(2,1)S(1)} %copy-done.26), kind=kOutput, calls=%fused_computation.42 | convolution fusion | flops 50339840 | bytes 1998848 | tf_op jit(solution)/shard_map/dot_general | solution.py:389
  129.6 3.4 %collective-permute-start.19 = (bf16[64,3200]{1,0:T(8,128)(2,1)S(1)}, bf16[64,3200]{1,0:T(8,128)(2,1)}, u32[]{:S(2)}, u32[]{:S(2)}) collective-permute-start(bf16[64,3200]{1,0:T(8,128)(2,1)S(1)} %get-tuple-element.102), channel_id=1, source_target_pairs={{0,96},{2,98},{4,100},{6,102},{8,104},{10,106},{12,108},{14,110},{... | collective-permute-start | bytes 1228808 | tf_op jit(solution)/shard_map/ppermute | solution.py:279
  133.0 6.5 %collective-permute-done.12 = bf16[64,3072]{1,0:T(8,128)(2,1)} collective-permute-done((bf16[64,3072]{1,0:T(8,128)(2,1)}, bf16[64,3072]{1,0:T(8,128)(2,1)}, u32[]{:S(2)}, u32[]{:S(2)}) %collective-permute-start.12) | collective-permute-done | bytes 393248 | tf_op jit(solution)/shard_map/ppermute | solution.py:279
  139.5 5.6 %collective-permute-done.13 = bf16[64,3072]{1,0:T(8,128)(2,1)} collective-permute-done((bf16[64,3072]{1,0:T(8,128)(2,1)}, bf16[64,3072]{1,0:T(8,128)(2,1)}, u32[]{:S(2)}, u32[]{:S(2)}) %collective-permute-start.13) | collective-permute-done | bytes 393248 | tf_op jit(solution)/shard_map/ppermute | solution.py:279
  145.1 2.0 maximum_bitcast_fusion
  147.2 5.5 %all-to-all-start.5 = ((bf16[8,8,6144]{2,1,0:T(8,128)(2,1)}), bf16[8,8,6144]{2,1,0:T(8,128)(2,1)}, u32[]{:S(2)}, u32[]{:S(2)}) async-start(bf16[8,8,6144]{2,1,0:T(8,128)(2,1)} %maximum_bitcast_fusion), calls=%async_computation.5 | async-start | bytes 1572864 | tf_op jit(solution)/shard_map/all_to_all | solution.py:271
  152.7 4.1 %expert_rows.8 = (bf16[128,384]{1,0:T(8,128)(2,1)S(1)}, bf16[64,3200]{1,0:T(8,128)(2,1)}, bf16[64,3200]{1,0:T(8,128)(2,1)}) custom-call(bf16[128,6144]{1,0:T(8,128)(2,1)} %bitcast.22.row_ref, bf16[3072,256]{1,0:T(8,128)(2,1)S(1)} %copy.39.wgu_ref, bf16[256,3072]{1,0:T(8,128)(2,1)} %copy-done, bf16[3072,128]{1,0:T(8,128)(2,1)S(1)} %bitcast.61), custom_call_target="tpu_custom_call" | custom-call | flops 60000002048 | bytes 3145728 | tf_op jit(solution)/shard_map/expert_rows/pallas_call | solution.py:258
  156.8 2.4 collective-permute-start.16
  159.1 2.9 %collective-permute-start.17 = (bf16[64,3200]{1,0:T(8,128)(2,1)}, bf16[64,3200]{1,0:T(8,128)(2,1)}, u32[]{:S(2)}, u32[]{:S(2)}) collective-permute-start(bf16[64,3200]{1,0:T(8,128)(2,1)} %get-tuple-element.113), channel_id=1, source_target_pairs={{0,80},{2,82},{4,84},{6,86},{8,88},{10,90},{12,92},{14,94},{16,96}... | collective-permute-start | bytes 1228808 | tf_op jit(solution)/shard_map/ppermute | solution.py:279
  162.1 2.9 %pad_maximum_fusion = bf16[8,32,3200]{2,1,0:T(8,128)(2,1)} fusion(bf16[8,8,3200]{2,1,0:T(8,128)(2,1)} %bitcast.30, bf16[8,8,3200]{2,1,0:T(8,128)(2,1)} %bitcast.29, bf16[8,8,3200]{2,1,0:T(8,128)(2,1)} %bitcast.28, bf16[8,8,3200]{2,1,0:T(8,128)(2,1)} %bitcast.27), kind=kLoop, calls=%fused_computation.13 | loop fusion | flops 6553600 | bytes 3276800 | tf_op jit(solution)/shard_map/concatenate | solution.py:293
  166.1 2.9 %expert_rows.9 = (bf16[64,384]{1,0:T(8,128)(2,1)S(1)}, bf16[64,3200]{1,0:T(8,128)(2,1)}) custom-call(bf16[64,6144]{1,0:T(8,128)(2,1)} %bitcast.25.row_ref, bf16[3072,256]{1,0:T(8,128)(2,1)S(1)} %copy.39.wgu_ref, bf16[256,3072]{1,0:T(8,128)(2,1)S(1)} %copy-done.1, bf16[3072,128]{1,0:T(8,128)(2,1)S(1)} %bitcast.62), custom_call_target="tpu_custom_call" | custom-call | flops 1 | bytes 3145728 | tf_op jit(solution)/shard_map/expert_rows/pallas_call | solution.py:258
  170.1 5.8 %all-to-all-start.6 = ((bf16[8,32,3200]{2,1,0:T(8,128)(2,1)}), bf16[8,32,3200]{2,1,0:T(8,128)(2,1)S(1)}, u32[]{:S(2)}, u32[]{:S(2)}) async-start(bf16[8,32,3200]{2,1,0:T(8,128)(2,1)} %pad_maximum_fusion), calls=%async_computation.6 | async-start | bytes 3276800 | tf_op jit(solution)/shard_map/all_to_all | solution.py:271
  191.0 9.9 %collective-permute-done.17 = bf16[64,3200]{1,0:T(8,128)(2,1)} collective-permute-done((bf16[64,3200]{1,0:T(8,128)(2,1)}, bf16[64,3200]{1,0:T(8,128)(2,1)}, u32[]{:S(2)}, u32[]{:S(2)}) %collective-permute-start.17) | collective-permute-done | bytes 409632 | tf_op jit(solution)/shard_map/ppermute | solution.py:279
  200.9 2.4 pad_maximum_fusion.3
  203.3 5.4 %all-to-all-start.7 = ((bf16[8,24,3200]{2,1,0:T(8,128)(2,1)}), bf16[8,24,3200]{2,1,0:T(8,128)(2,1)}, u32[]{:S(2)}, u32[]{:S(2)}) async-start(bf16[8,24,3200]{2,1,0:T(8,128)(2,1)} %pad_maximum_fusion.3), calls=%async_computation.7 | async-start | bytes 2457600 | tf_op jit(solution)/shard_map/all_to_all | solution.py:271
  212.9 9.8 %all-to-all-done.7 = bf16[8,24,3200]{2,1,0:T(8,128)(2,1)} async-done(((bf16[8,24,3200]{2,1,0:T(8,128)(2,1)}), bf16[8,24,3200]{2,1,0:T(8,128)(2,1)}, u32[]{:S(2)}, u32[]{:S(2)}) %all-to-all-start.7) | async-done | bytes 1228832 | tf_op jit(solution)/shard_map/all_to_all | solution.py:271
  223.8 2.2 fusion.4
  226.0 2.6 %collective-permute-start.21 = (bf16[128,3072]{1,0:T(8,128)(2,1)S(1)}, bf16[128,3072]{1,0:T(8,128)(2,1)S(1)}, u32[]{:S(2)}, u32[]{:S(2)}) collective-permute-start(bf16[128,3072]{1,0:T(8,128)(2,1)S(1)} %fusion.4), channel_id=1, source_target_pairs={{0,128},{128,0},{1,129},{129,1},{2,130},{130,2},{3,131},{131,3},{4... | collective-permute-start | bytes 2359304 | tf_op jit(solution)/shard_map/ppermute | solution.py:393
  230.1 11.8 %collective-permute-done.21 = bf16[128,3072]{1,0:T(8,128)(2,1)S(1)} collective-permute-done((bf16[128,3072]{1,0:T(8,128)(2,1)S(1)}, bf16[128,3072]{1,0:T(8,128)(2,1)S(1)}, u32[]{:S(2)}, u32[]{:S(2)}) %collective-permute-start.21) | collective-permute-done | bytes 786464 | tf_op jit(solution)/shard_map/ppermute | solution.py:393
  (127 shorter events, 49.4 us)
Async XLA Ops:
  0.6 9.1 %copy-start.13 = (bf16[1,128,3072]{2,1,0:T(8,128)(2,1)S(1)}, bf16[1,128,3072]{2,1,0:T(8,128)(2,1)}, u32[]{:S(2)}) copy-start(bf16[1,128,3072]{2,1,0:T(8,128)(2,1)} %param.10) | copy-start | bytes 2359300
  0.6 33.8 %collective-permute-start.6 = (bf16[128,3072]{1,0:T(8,128)(2,1)}, bf16[128,3072]{1,0:T(8,128)(2,1)}, u32[]{:S(2)}, u32[]{:S(2)}) collective-permute-start(bf16[128,3072]{1,0:T(8,128)(2,1)} %bitcast.68), channel_id=1, source_target_pairs={{0,112},{2,114},{4,116},{6,118},{8,120},{10,122},{12,124},{14,126}... | collective-permute-start | bytes 2359304 | tf_op jit(solution)/shard_map/ppermute | solution.py:279
  2.6 35.1 %collective-permute-start.4 = (bf16[128,3072]{1,0:T(8,128)(2,1)}, bf16[128,3072]{1,0:T(8,128)(2,1)}, u32[]{:S(2)}, u32[]{:S(2)}) collective-permute-start(bf16[128,3072]{1,0:T(8,128)(2,1)} %bitcast.69), channel_id=1, source_target_pairs={{0,16},{2,18},{4,20},{6,22},{8,24},{10,26},{12,28},{14,30},{16,32}... | collective-permute-start | bytes 2359304 | tf_op jit(solution)/shard_map/ppermute | solution.py:279
  4.3 7.8 %copy-start.25 = (s32[1,128,2]{2,1,0:T(8,128)}, s32[1,128,2]{2,1,0:T(8,128)S(1)}, u32[]{:S(2)}) copy-start(s32[1,128,2]{2,1,0:T(8,128)S(1)} %copy.33) | copy-start | bytes 3076
  5.6 42.4 %collective-permute-start.1 = (bf16[128,3200]{1,0:T(8,128)(2,1)S(1)}, bf16[128,3200]{1,0:T(8,128)(2,1)}, u32[]{:S(2)}, u32[]{:S(2)}) collective-permute-start(bf16[128,3200]{1,0:T(8,128)(2,1)S(1)} %pad_maximum_fusion.4.refs_0_.refs_1_), channel_id=1, source_target_pairs={{0,16},{2,18},{4,20},{6,22},{8,24},{10,26},{12,28},{14,30},{16,32}... | collective-permute-start | bytes 2457608 | tf_op jit(solution)/shard_map/ppermute | solution.py:279
  7.6 40.4 %collective-permute-start = (bf16[128,3200]{1,0:T(8,128)(2,1)S(1)}, bf16[128,3200]{1,0:T(8,128)(2,1)}, u32[]{:S(2)}, u32[]{:S(2)}) collective-permute-start(bf16[128,3200]{1,0:T(8,128)(2,1)S(1)} %pad_maximum_fusion.4.refs_0_.refs_1_), channel_id=1, source_target_pairs={{0,112},{2,114},{4,116},{6,118},{8,120},{10,122},{12,124},{14,126}... | collective-permute-start | bytes 2457608 | tf_op jit(solution)/shard_map/ppermute | solution.py:279
  12.2 5.5 %copy-start.20 = (bf16[1,1,1536,128]{3,2,1,0:T(8,128)(2,1)S(1)}, bf16[1,1,1536,128]{3,2,1,0:T(8,128)(2,1)}, u32[]{:S(2)}) copy-start(bf16[1,1,1536,128]{3,2,1,0:T(8,128)(2,1)} %param.11) | copy-start | bytes 1179652
  12.2 8.4 %copy-start.21 = (bf16[1,1,1536,128]{3,2,1,0:T(8,128)(2,1)S(1)}, bf16[1,1,1536,128]{3,2,1,0:T(8,128)(2,1)}, u32[]{:S(2)}) copy-start(bf16[1,1,1536,128]{3,2,1,0:T(8,128)(2,1)} %param.12) | copy-start | bytes 1179652
  12.2 25.5 %all-to-all-start = ((bf16[8,8,6144]{2,1,0:T(8,128)(2,1)}), bf16[8,8,6144]{2,1,0:T(8,128)(2,1)S(1)}, u32[]{:S(2)}, u32[]{:S(2)}) async-start(bf16[8,8,6144]{2,1,0:T(8,128)(2,1)} %bitcast.10), calls=%async_computation | async-start | bytes 1572864 | tf_op jit(solution)/shard_map/all_to_all | solution.py:271
  17.9 5.3 %copy-start.22 = (bf16[1,1,128,1536]{3,2,1,0:T(8,128)(2,1)S(1)}, bf16[1,1,128,1536]{3,2,1,0:T(8,128)(2,1)}, u32[]{:S(2)}) copy-start(bf16[1,1,128,1536]{3,2,1,0:T(8,128)(2,1)} %param.13) | copy-start | bytes 1179652
  27.1 10.5 %copy-start = (bf16[256,3072]{1,0:T(8,128)(2,1)}, bf16[256,3072]{1,0:T(8,128)(2,1)S(1)}, u32[]{:S(2)}) copy-start(bf16[256,3072]{1,0:T(8,128)(2,1)S(1)} %get-tuple-element.99.wgu_t_ref) | copy-start | bytes 4718596
  34.4 21.4 %collective-permute-start.7 = (bf16[128,3072]{1,0:T(8,128)(2,1)}, bf16[128,3072]{1,0:T(8,128)(2,1)}, u32[]{:S(2)}, u32[]{:S(2)}) collective-permute-start(bf16[128,3072]{1,0:T(8,128)(2,1)} %collective-permute-done.6.refs_4_), channel_id=1, source_target_pairs={{0,112},{2,114},{4,116},{6,118},{8,120},{10,122},{12,124},{14,126}... | collective-permute-start | bytes 2359304 | tf_op jit(solution)/shard_map/ppermute | solution.py:279
  37.7 22.0 %collective-permute-start.5 = (bf16[128,3072]{1,0:T(8,128)(2,1)}, bf16[128,3072]{1,0:T(8,128)(2,1)}, u32[]{:S(2)}, u32[]{:S(2)}) collective-permute-start(bf16[128,3072]{1,0:T(8,128)(2,1)} %collective-permute-done.4.refs_5_), channel_id=1, source_target_pairs={{0,16},{2,18},{4,20},{6,22},{8,24},{10,26},{12,28},{14,30},{16,32}... | collective-permute-start | bytes 2359304 | tf_op jit(solution)/shard_map/ppermute | solution.py:279
  37.7 3.9 %copy-start.10 = (bf16[8,8,6144]{2,1,0:T(8,128)(2,1)}, bf16[8,8,6144]{2,1,0:T(8,128)(2,1)S(1)}, u32[]{:S(2)}) copy-start(bf16[8,8,6144]{2,1,0:T(8,128)(2,1)S(1)} %all-to-all-done) | copy-start | bytes 2359300
  42.3 22.5 %all-to-all-start.1 = ((bf16[8,8,3200]{2,1,0:T(8,128)(2,1)}), bf16[8,8,3200]{2,1,0:T(8,128)(2,1)S(1)}, u32[]{:S(2)}, u32[]{:S(2)}) async-start(bf16[8,8,3200]{2,1,0:T(8,128)(2,1)} %bitcast.71), calls=%async_computation.1 | async-start | bytes 819200 | tf_op jit(solution)/shard_map/all_to_all | solution.py:271
  48.0 28.1 %collective-permute-start.2 = (bf16[128,3200]{1,0:T(8,128)(2,1)}, bf16[128,3200]{1,0:T(8,128)(2,1)S(1)}, u32[]{:S(2)}, u32[]{:S(2)}) collective-permute-start(bf16[128,3200]{1,0:T(8,128)(2,1)} %collective-permute-done.1.refs_1_.refs_3_), channel_id=1, source_target_pairs={{0,16},{2,18},{4,20},{6,22},{8,24},{10,26},{12,28},{14,30},{16,32}... | collective-permute-start | bytes 2457608 | tf_op jit(solution)/shard_map/ppermute | solution.py:279
  48.1 28.0 %collective-permute-start.3 = (bf16[128,3200]{1,0:T(8,128)(2,1)}, bf16[128,3200]{1,0:T(8,128)(2,1)}, u32[]{:S(2)}, u32[]{:S(2)}) collective-permute-start(bf16[128,3200]{1,0:T(8,128)(2,1)} %collective-permute-done.refs_0_.refs_2_), channel_id=1, source_target_pairs={{0,112},{2,114},{4,116},{6,118},{8,120},{10,122},{12,124},{14,126}... | collective-permute-start | bytes 2457608 | tf_op jit(solution)/shard_map/ppermute | solution.py:279
  65.6 25.4 %all-to-all-start.2 = ((bf16[8,16,6144]{2,1,0:T(8,128)(2,1)}), bf16[8,16,6144]{2,1,0:T(8,128)(2,1)S(1)}, u32[]{:S(2)}, u32[]{:S(2)}) async-start(bf16[8,16,6144]{2,1,0:T(8,128)(2,1)} %bitcast.64), calls=%async_computation.2 | async-start | bytes 3145728 | tf_op jit(solution)/shard_map/all_to_all | solution.py:271
  81.7 2.9 %copy-start.15 = (bf16[64,3072]{1,0:T(8,128)(2,1)}, bf16[64,3072]{1,0:T(8,128)(2,1)S(1)}, u32[]{:S(2)}) copy-start(bf16[64,3072]{1,0:T(8,128)(2,1)S(1)} %get-tuple-element.90) | copy-start | bytes 1179652
  81.7 21.2 %collective-permute-start.10 = (bf16[64,6144]{1,0:T(8,128)(2,1)}, bf16[64,6144]{1,0:T(8,128)(2,1)}, u32[]{:S(2)}, u32[]{:S(2)}) collective-permute-start(bf16[64,6144]{1,0:T(8,128)(2,1)} %get-tuple-element.91), channel_id=1, source_target_pairs={{0,112},{2,114},{4,116},{6,118},{8,120},{10,122},{12,124},{14,126}... | collective-permute-start | bytes 2359304 | tf_op jit(solution)/shard_map/ppermute | solution.py:279
  84.6 20.8 %collective-permute-start.11 = (bf16[64,6144]{1,0:T(8,128)(2,1)}, bf16[64,6144]{1,0:T(8,128)(2,1)}, u32[]{:S(2)}, u32[]{:S(2)}) collective-permute-start(bf16[64,6144]{1,0:T(8,128)(2,1)} %get-tuple-element.92), channel_id=1, source_target_pairs={{0,16},{2,18},{4,20},{6,22},{8,24},{10,26},{12,28},{14,30},{16,32}... | collective-permute-start | bytes 2359304 | tf_op jit(solution)/shard_map/ppermute | solution.py:279
  91.0 17.3 %copy-start.2 = (bf16[8,16,6144]{2,1,0:T(8,128)(2,1)}, bf16[8,16,6144]{2,1,0:T(8,128)(2,1)S(1)}, u32[]{:S(2)}) copy-start(bf16[8,16,6144]{2,1,0:T(8,128)(2,1)S(1)} %all-to-all-done.2) | copy-start | bytes 4718596
  91.0 24.9 %all-to-all-start.3 = ((bf16[8,16,6144]{2,1,0:T(8,128)(2,1)}), bf16[8,16,6144]{2,1,0:T(8,128)(2,1)}, u32[]{:S(2)}, u32[]{:S(2)}) async-start(bf16[8,16,6144]{2,1,0:T(8,128)(2,1)} %bitcast.63), calls=%async_computation.3 | async-start | bytes 3145728 | tf_op jit(solution)/shard_map/all_to_all | solution.py:271
  97.0 27.0 %collective-permute-start.8 = (bf16[64,3072]{1,0:T(8,128)(2,1)}, bf16[64,3072]{1,0:T(8,128)(2,1)}, u32[]{:S(2)}, u32[]{:S(2)}) collective-permute-start(bf16[64,3072]{1,0:T(8,128)(2,1)} %copy-done.16), channel_id=1, source_target_pairs={{0,16},{2,18},{4,20},{6,22},{8,24},{10,26},{12,28},{14,30},{16,32}... | collective-permute-start | bytes 1179656 | tf_op jit(solution)/shard_map/ppermute | solution.py:279
  97.1 26.9 %collective-permute-start.9 = (bf16[64,3072]{1,0:T(8,128)(2,1)}, bf16[64,3072]{1,0:T(8,128)(2,1)}, u32[]{:S(2)}, u32[]{:S(2)}) collective-permute-start(bf16[64,3072]{1,0:T(8,128)(2,1)} %copy-done.15), channel_id=1, source_target_pairs={{0,112},{2,114},{4,116},{6,118},{8,120},{10,122},{12,124},{14,126}... | collective-permute-start | bytes 1179656 | tf_op jit(solution)/shard_map/ppermute | solution.py:279
  111.9 17.7 %collective-permute-start.14 = (bf16[64,3200]{1,0:T(8,128)(2,1)}, bf16[64,3200]{1,0:T(8,128)(2,1)}, u32[]{:S(2)}, u32[]{:S(2)}) collective-permute-start(bf16[64,3200]{1,0:T(8,128)(2,1)} %get-tuple-element.106), channel_id=1, source_target_pairs={{0,16},{2,18},{4,20},{6,22},{8,24},{10,26},{12,28},{14,30},{16,32}... | collective-permute-start | bytes 1228808 | tf_op jit(solution)/shard_map/ppermute | solution.py:279
  111.9 8.4 %copy-start.6 = (bf16[1,1,128,3072]{2,3,1,0:T(8,128)(2,1)S(1)}, bf16[1,1,128,3072]{2,3,1,0:T(8,128)(2,1)}, u32[]{:S(2)}) copy-start(bf16[1,1,128,3072]{2,3,1,0:T(8,128)(2,1)} %all-gather.2) | copy-start | bytes 2359300
  111.9 21.1 %collective-permute-start.15 = (bf16[64,3200]{1,0:T(8,128)(2,1)}, bf16[64,3200]{1,0:T(8,128)(2,1)}, u32[]{:S(2)}, u32[]{:S(2)}) collective-permute-start(bf16[64,3200]{1,0:T(8,128)(2,1)} %get-tuple-element.107), channel_id=1, source_target_pairs={{0,112},{2,114},{4,116},{6,118},{8,120},{10,122},{12,124},{14,126}... | collective-permute-start | bytes 1228808 | tf_op jit(solution)/shard_map/ppermute | solution.py:279
  115.9 31.2 %all-to-all-start.4 = ((bf16[8,16,6144]{2,1,0:T(8,128)(2,1)}), bf16[8,16,6144]{2,1,0:T(8,128)(2,1)}, u32[]{:S(2)}, u32[]{:S(2)}) async-start(bf16[8,16,6144]{2,1,0:T(8,128)(2,1)} %pad_maximum_fusion.2), calls=%async_computation.4 | async-start | bytes 3145728 | tf_op jit(solution)/shard_map/all_to_all | solution.py:271
  120.2 6.0 %copy-start.26 = (bf16[256,64]{1,0:T(8,128)(2,1)S(1)}, bf16[256,64]{1,0:T(8,128)(2,1)}, u32[]{:S(2)}) copy-start(bf16[256,64]{1,0:T(8,128)(2,1)} %get-tuple-element.81) | copy-start | bytes 98308
  124.0 15.5 %collective-permute-start.12 = (bf16[64,3072]{1,0:T(8,128)(2,1)}, bf16[64,3072]{1,0:T(8,128)(2,1)}, u32[]{:S(2)}, u32[]{:S(2)}) collective-permute-start(bf16[64,3072]{1,0:T(8,128)(2,1)} %collective-permute-done.8), channel_id=1, source_target_pairs={{0,16},{2,18},{4,20},{6,22},{8,24},{10,26},{12,28},{14,30},{16,32}... | collective-permute-start | bytes 1179656 | tf_op jit(solution)/shard_map/ppermute | solution.py:279
  124.0 21.1 %collective-permute-start.13 = (bf16[64,3072]{1,0:T(8,128)(2,1)}, bf16[64,3072]{1,0:T(8,128)(2,1)}, u32[]{:S(2)}, u32[]{:S(2)}) collective-permute-start(bf16[64,3072]{1,0:T(8,128)(2,1)} %collective-permute-done.9), channel_id=1, source_target_pairs={{0,112},{2,114},{4,116},{6,118},{8,120},{10,122},{12,124},{14,126}... | collective-permute-start | bytes 1179656 | tf_op jit(solution)/shard_map/ppermute | solution.py:279
  128.9 27.9 %collective-permute-start.18 = (bf16[64,3200]{1,0:T(8,128)(2,1)}, bf16[64,3200]{1,0:T(8,128)(2,1)}, u32[]{:S(2)}, u32[]{:S(2)}) collective-permute-start(bf16[64,3200]{1,0:T(8,128)(2,1)} %get-tuple-element.101), channel_id=1, source_target_pairs={{0,32},{2,34},{4,36},{6,38},{8,40},{10,42},{12,44},{14,46},{16,48}... | collective-permute-start | bytes 1228808 | tf_op jit(solution)/shard_map/ppermute | solution.py:279
  129.6 27.2 %collective-permute-start.19 = (bf16[64,3200]{1,0:T(8,128)(2,1)S(1)}, bf16[64,3200]{1,0:T(8,128)(2,1)}, u32[]{:S(2)}, u32[]{:S(2)}) collective-permute-start(bf16[64,3200]{1,0:T(8,128)(2,1)S(1)} %get-tuple-element.102), channel_id=1, source_target_pairs={{0,96},{2,98},{4,100},{6,102},{8,104},{10,106},{12,108},{14,110},{... | collective-permute-start | bytes 1228808 | tf_op jit(solution)/shard_map/ppermute | solution.py:279
  147.2 17.8 %all-to-all-start.5 = ((bf16[8,8,6144]{2,1,0:T(8,128)(2,1)}), bf16[8,8,6144]{2,1,0:T(8,128)(2,1)}, u32[]{:S(2)}, u32[]{:S(2)}) async-start(bf16[8,8,6144]{2,1,0:T(8,128)(2,1)} %maximum_bitcast_fusion), calls=%async_computation.5 | async-start | bytes 1572864 | tf_op jit(solution)/shard_map/all_to_all | solution.py:271
  156.8 34.3 %collective-permute-start.16 = (bf16[64,3200]{1,0:T(8,128)(2,1)}, bf16[64,3200]{1,0:T(8,128)(2,1)}, u32[]{:S(2)}, u32[]{:S(2)}) collective-permute-start(bf16[64,3200]{1,0:T(8,128)(2,1)} %get-tuple-element.112), channel_id=1, source_target_pairs={{0,48},{2,50},{4,52},{6,54},{8,56},{10,58},{12,60},{14,62},{16,64}... | collective-permute-start | bytes 1228808 | tf_op jit(solution)/shard_map/ppermute | solution.py:279
  159.1 41.8 %collective-permute-start.17 = (bf16[64,3200]{1,0:T(8,128)(2,1)}, bf16[64,3200]{1,0:T(8,128)(2,1)}, u32[]{:S(2)}, u32[]{:S(2)}) collective-permute-start(bf16[64,3200]{1,0:T(8,128)(2,1)} %get-tuple-element.113), channel_id=1, source_target_pairs={{0,80},{2,82},{4,84},{6,86},{8,88},{10,90},{12,92},{14,94},{16,96}... | collective-permute-start | bytes 1228808 | tf_op jit(solution)/shard_map/ppermute | solution.py:279
  169.0 31.9 %collective-permute-start.20 = (bf16[64,3200]{1,0:T(8,128)(2,1)}, bf16[64,3200]{1,0:T(8,128)(2,1)}, u32[]{:S(2)}, u32[]{:S(2)}) collective-permute-start(bf16[64,3200]{1,0:T(8,128)(2,1)} %get-tuple-element.123), channel_id=1, source_target_pairs={{0,64},{2,66},{4,68},{6,70},{8,72},{10,74},{12,76},{14,78},{16,80}... | collective-permute-start | bytes 1228808 | tf_op jit(solution)/shard_map/ppermute | solution.py:279
  170.1 5.8 %copy-start.11 = (bf16[8,8,6144]{2,1,0:T(8,128)(2,1)S(1)}, bf16[8,8,6144]{2,1,0:T(8,128)(2,1)}, u32[]{:S(2)}) copy-start(bf16[8,8,6144]{2,1,0:T(8,128)(2,1)} %copy-done.10) | copy-start | bytes 2359300
  170.1 33.2 %all-to-all-start.6 = ((bf16[8,32,3200]{2,1,0:T(8,128)(2,1)}), bf16[8,32,3200]{2,1,0:T(8,128)(2,1)S(1)}, u32[]{:S(2)}, u32[]{:S(2)}) async-start(bf16[8,32,3200]{2,1,0:T(8,128)(2,1)} %pad_maximum_fusion), calls=%async_computation.6 | async-start | bytes 3276800 | tf_op jit(solution)/shard_map/all_to_all | solution.py:271
  186.3 3.9 %collective-permute-start.23 = (bf16[128,1536]{1,0:T(8,128)(2,1)S(1)}, bf16[128,1536]{1,0:T(8,128)(2,1)S(1)}, u32[]{:S(2)}, u32[]{:S(2)}) collective-permute-start(bf16[128,1536]{1,0:T(8,128)(2,1)S(1)} %constant_dynamic-slice_fusion), channel_id=1, source_target_pairs={{0,1},{1,0},{2,3},{3,2},{4,5},{5,4},{6,7},{7,6},{8,9},{9,8},{10,11... | collective-permute-start | bytes 1179656 | tf_op jit(solution)/shard_map/ppermute | solution.py:287
  188.7 12.2 %copy-start.17 = (bf16[3072,256]{1,0:T(8,128)(2,1)}, bf16[3072,256]{1,0:T(8,128)(2,1)S(1)}, u32[]{:S(2)}) copy-start(bf16[3072,256]{1,0:T(8,128)(2,1)S(1)} %fusion.2) | copy-start | bytes 4718596
  189.7 19.0 %collective-permute-start.22 = (bf16[1536,256]{1,0:T(8,128)(2,1)}, bf16[1536,256]{1,0:T(8,128)(2,1)S(1)}, u32[]{:S(2)}, u32[]{:S(2)}) collective-permute-start(bf16[1536,256]{1,0:T(8,128)(2,1)} %constant_dynamic-slice_fusion.1), channel_id=1, source_target_pairs={{0,1},{1,0},{2,3},{3,2},{4,5},{5,4},{6,7},{7,6},{8,9},{9,8},{10,11... | collective-permute-start | bytes 2359304 | tf_op jit(solution)/shard_map/ppermute | solution.py:287
  203.3 19.5 %all-to-all-start.7 = ((bf16[8,24,3200]{2,1,0:T(8,128)(2,1)}), bf16[8,24,3200]{2,1,0:T(8,128)(2,1)}, u32[]{:S(2)}, u32[]{:S(2)}) async-start(bf16[8,24,3200]{2,1,0:T(8,128)(2,1)} %pad_maximum_fusion.3), calls=%async_computation.7 | async-start | bytes 2457600 | tf_op jit(solution)/shard_map/all_to_all | solution.py:271
  211.3 11.5 %copy-start.23 = (bf16[256,192]{1,0:T(8,128)(2,1)S(1)}, bf16[256,192]{1,0:T(8,128)(2,1)}, u32[]{:S(2)}) copy-start(bf16[256,192]{1,0:T(8,128)(2,1)} %get-tuple-element.131) | copy-start | bytes 294916
  223.8 4.8 %copy-start.27 = (bf16[256,64]{1,0:T(8,128)(2,1)S(1)}, bf16[256,64]{1,0:T(8,128)(2,1)}, u32[]{:S(2)}) copy-start(bf16[256,64]{1,0:T(8,128)(2,1)} %get-tuple-element.81) | copy-start | bytes 98308
  223.8 5.8 %copy-start.28 = (bf16[1,128,2]{1,2,0:T(2,128)(2,1)S(1)}, bf16[1,128,2]{1,2,0:T(2,128)(2,1)}, u32[]{:S(2)}) copy-start(bf16[1,128,2]{1,2,0:T(2,128)(2,1)} %param.9) | copy-start | bytes 1540
  226.0 16.0 %collective-permute-start.21 = (bf16[128,3072]{1,0:T(8,128)(2,1)S(1)}, bf16[128,3072]{1,0:T(8,128)(2,1)S(1)}, u32[]{:S(2)}, u32[]{:S(2)}) collective-permute-start(bf16[128,3072]{1,0:T(8,128)(2,1)S(1)} %fusion.4), channel_id=1, source_target_pairs={{0,128},{128,0},{1,129},{129,1},{2,130},{130,2},{3,131},{131,3},{4... | collective-permute-start | bytes 2359304 | tf_op jit(solution)/shard_map/ppermute | solution.py:393
  (13 other events, 20.7 us)

commit v5 on v4

--- a/solution.py
+++ b/solution.py
@@ -388,6 +388,7 @@
     def product(left, right):
         return jnp.dot(left, right, preferred_element_type=jnp.float32)
 
+    back_0, _ = tie((back_0, back_a))
     grad = product(boths[0], back_0[:, :width]) + product(boths[1], back_a[:, :width])
     grad = (grad + product(boths[2], back_b[:, :width])).astype(jnp.bfloat16)
     grad = lax.ppermute(grad, "section", back_by_one)

time: 246 us -> 244 us (level)
  starting transfers between devices: 77.3 us -> 81.4 us
  matrix products: 20 us -> 17 us
  waiting for transfers between devices: 65.1 us -> 62.1 us
    ppermute x21, starting transfers between devices: 32.5 us -> 35.8 us  [along_z(): lax.ppermute(array, 'expert', [(i, (i + step) % size) for i in range(size)])]
    dot_general x6, matrix products: 8.51 us -> 5.48 us  [product(): return jnp.dot(left, right, preferred_element_type=jnp.float32)]
    unnamed x64 -> x62, local copies, waits for them, and re-layouts: 13.3 us -> 15 us
  transfers between devices with their start and end apart: 32 -> 32, of which waited for: 12 -> 12; matrix products, arithmetic and copies ran while one was open for 18% -> 16% of each run, Pallas kernels for 13% -> 13%
where the time goes in v5:
time: 244 us; the launch traced here: 240 us
  starting transfers between devices  81.4 us (33%)
  waiting for transfers between devices  62.1 us (25%)
  Pallas kernels  32.2 us (13%)
  local copies, waits for them, and re-layouts  20.9 us (9%)
  matrix products  17 us (7%)
  other arithmetic  15.7 us (6%)
  blocking collectives  9.19 us (4%)
    all_to_all x8, starting transfers between devices, exchanged(): lax.all_to_all(array, 'expert', split_axis=0, concat_axis=0, tiled=True,...  42 us
    ppermute x21, waiting for transfers between devices, along_z(): lax.ppermute(array, 'expert', [(i, (i + step) % size) for i in range(size)])  39.6 us
    ppermute x21, starting transfers between devices, along_z(): lax.ppermute(array, 'expert', [(i, (i + step) % size) for i in range(size)])  35.8 us
    pallas_call x5, Pallas kernels, expert_pass(): pl.pallas_call(expert_kernel, out_shape=[jax.ShapeDtypeStruct((count, hid...  15 us
    unnamed x62, local copies, waits for them, and re-layouts  15 us
    all_to_all x8, waiting for transfers between devices, exchanged(): lax.all_to_all(array, 'expert', split_axis=0, concat_axis=0, tiled=True,...  12.7 us
    dot_general x10, matrix products, contract_rows(): lax.dot_general(former, latter, (((0,), (0,)), ((), ())), preferred_eleme...  11.6 us
    pallas_call x3, Pallas kernels, plane_rows(): pl.pallas_call(functools.partial(plane_kernel, count, steps), grid=(2 * s...  10.3 us
  transfers between devices with their start and end apart: 32, of which 12 were waited for; matrix products, arithmetic and copies ran while one was open for 16% of the time, Pallas kernels for 13%

profile of v5, /device:TPU:32, one launch (start us, length us, event | category | flops | bytes accessed | tf_op | source)
XLA Modules:
  0.0 239.6 jit_solution(5222849195073544695)
XLA Ops:
  7.6 2.1 collective-permute-start
  9.7 2.4 %plane_rows.3 = bf16[64,6144]{1,0:T(8,128)(2,1)} custom-call(s32[1]{0:T(128)} %bitcast.8.z_ref, bf16[128,3200]{1,0:T(8,128)(2,1)S(1)} %pad_maximum_fusion.4.refs_0_.refs_1_, bf16[128,3200]{1,0:T(8,128)(2,1)S(1)} %pad_maximum_fusion.4.refs_0_.refs_1_, bf16[128,3072]{1,0:T(8,128)(2,1)S(1)} %bitcast.70), custom_call_target="tpu_custom_call" | custom-call | tf_op jit(solution)/shard_map/plane_rows/pallas_call | solution.py:96
  12.2 5.5 %all-to-all-start = ((bf16[8,8,6144]{2,1,0:T(8,128)(2,1)}), bf16[8,8,6144]{2,1,0:T(8,128)(2,1)S(1)}, u32[]{:S(2)}, u32[]{:S(2)}) async-start(bf16[8,8,6144]{2,1,0:T(8,128)(2,1)} %bitcast.10), calls=%async_computation | async-start | bytes 1572864 | tf_op jit(solution)/shard_map/all_to_all | solution.py:271
  17.9 2.6 %all-gather = bf16[1,1,3072,128]{2,3,1,0:T(8,128)(2,1)} all-gather(bf16[1,1,1536,128]{2,3,1,0:T(8,128)(2,1)S(1)} %copy.35), channel_id=2, replica_groups=mesh['section'=2,'expert'=64,'dp'=2] {'dp'}, dimensions={2}, use_global_device_ids=true | all-gather | bytes 1179648 | tf_op jit(solution)/shard_map/all_gather | solution.py:321
  20.7 2.5 %all-gather.1 = bf16[1,1,3072,128]{2,3,1,0:T(8,128)(2,1)} all-gather(bf16[1,1,1536,128]{2,3,1,0:T(8,128)(2,1)S(1)} %copy.36), channel_id=3, replica_groups=mesh['section'=2,'expert'=64,'dp'=2] {'dp'}, dimensions={2}, use_global_device_ids=true | all-gather | bytes 1179648 | tf_op jit(solution)/shard_map/all_gather | solution.py:322
  24.1 2.9 %fusion.53 = (bf16[256,3072]{1,0:T(8,128)(2,1)S(1)}, bf16[3072,256]{0,1:T(8,128)(2,1)}) fusion(bf16[3072,128]{0,1:T(8,128)(2,1)} %bitcast.75, bf16[3072,128]{0,1:T(8,128)(2,1)} %bitcast.74), kind=kLoop, calls=%fused_computation.80 | loop fusion | flops 3145728 | bytes 4718592 | tf_op jit(solution)/shard_map/transpose | solution.py:325
  27.1 3.2 %copy.38.wgu_ref = bf16[3072,256]{1,0:T(8,128)(2,1)} copy(bf16[3072,256]{0,1:T(8,128)(2,1)} %get-tuple-element.98) | data formatting | bytes 3145728 | tf_op jit(solution)/shard_map/concatenate | solution.py:324
  30.2 4.1 %all-gather.2 = bf16[1,1,128,3072]{2,3,1,0:T(8,128)(2,1)} all-gather(bf16[1,1,128,1536]{2,3,1,0:T(8,128)(2,1)} %copy.37), channel_id=4, replica_groups=mesh['section'=2,'expert'=64,'dp'=2] {'dp'}, dimensions={3}, use_global_device_ids=true | all-gather | bytes 1179648 | tf_op jit(solution)/shard_map/all_gather | solution.py:323
  34.3 3.2 %collective-permute-start.7 = (bf16[128,3072]{1,0:T(8,128)(2,1)}, bf16[128,3072]{1,0:T(8,128)(2,1)}, u32[]{:S(2)}, u32[]{:S(2)}) collective-permute-start(bf16[128,3072]{1,0:T(8,128)(2,1)} %collective-permute-done.6.refs_4_), channel_id=1, source_target_pairs={{0,112},{2,114},{4,116},{6,118},{8,120},{10,122},{12,124},{14,126}... | collective-permute-start | bytes 2359304 | tf_op jit(solution)/shard_map/ppermute | solution.py:279
  42.2 5.7 %all-to-all-start.1 = ((bf16[8,8,3200]{2,1,0:T(8,128)(2,1)}), bf16[8,8,3200]{2,1,0:T(8,128)(2,1)S(1)}, u32[]{:S(2)}, u32[]{:S(2)}) async-start(bf16[8,8,3200]{2,1,0:T(8,128)(2,1)} %bitcast.71), calls=%async_computation.1 | async-start | bytes 819200 | tf_op jit(solution)/shard_map/all_to_all | solution.py:271
  48.0 2.1 collective-permute-start.3
  50.1 5.6 %collective-permute-done.7.up_b.refs_4_ = bf16[128,3072]{1,0:T(8,128)(2,1)} collective-permute-done((bf16[128,3072]{1,0:T(8,128)(2,1)}, bf16[128,3072]{1,0:T(8,128)(2,1)}, u32[]{:S(2)}, u32[]{:S(2)}) %collective-permute-start.7) | collective-permute-done | bytes 786464 | tf_op jit(solution)/shard_map/ppermute | solution.py:279
  55.7 4.0 %collective-permute-done.5.up_a.refs_5_ = bf16[128,3072]{1,0:T(8,128)(2,1)} collective-permute-done((bf16[128,3072]{1,0:T(8,128)(2,1)}, bf16[128,3072]{1,0:T(8,128)(2,1)}, u32[]{:S(2)}, u32[]{:S(2)}) %collective-permute-start.5) | collective-permute-done | bytes 786464 | tf_op jit(solution)/shard_map/ppermute | solution.py:279
  59.7 4.0 %plane_rows.4 = bf16[128,6144]{1,0:T(8,128)(2,1)S(1)} custom-call(s32[1]{0:T(128)} %bitcast.8.z_ref, bf16[128,3200]{1,0:T(8,128)(2,1)} %collective-permute-done.refs_0_.refs_2_, bf16[128,3200]{1,0:T(8,128)(2,1)} %collective-permute-done.1.refs_1_.refs_3_, bf16[128,3200]{1,0:T(8,128)(2,1)} %collective-permute-done.refs_0_.refs_2_, ...), custom_call_target="tpu_custom_call" | custom-call | tf_op jit(solution)/shard_map/plane_rows/pallas_call | solution.py:96
  65.7 5.1 %all-to-all-start.2 = ((bf16[8,16,6144]{2,1,0:T(8,128)(2,1)}), bf16[8,16,6144]{2,1,0:T(8,128)(2,1)S(1)}, u32[]{:S(2)}, u32[]{:S(2)}) async-start(bf16[8,16,6144]{2,1,0:T(8,128)(2,1)} %bitcast.64), calls=%async_computation.2 | async-start | bytes 3145728 | tf_op jit(solution)/shard_map/all_to_all | solution.py:271
  70.8 2.1 own_picks.1
  72.9 3.2 %collective-permute-done.2.mark_a.tok_a.refs_1_.refs_3_ = bf16[128,3200]{1,0:T(8,128)(2,1)S(1)} collective-permute-done((bf16[128,3200]{1,0:T(8,128)(2,1)}, bf16[128,3200]{1,0:T(8,128)(2,1)S(1)}, u32[]{:S(2)}, u32[]{:S(2)}) %collective-permute-start.2) | collective-permute-done | bytes 819232 | tf_op jit(solution)/shard_map/ppermute | solution.py:279
  76.2 4.8 %onward_rows.1 = (bf16[64,6144]{1,0:T(8,128)(2,1)}, bf16[64,6144]{1,0:T(8,128)(2,1)}, bf16[64,3072]{1,0:T(8,128)(2,1)S(1)}, bf16[64,3072]{1,0:T(8,128)(2,1)S(1)}) custom-call(s32[1]{0:T(128)} %bitcast.8.z_ref, bf16[128,3200]{1,0:T(8,128)(2,1)S(1)} %collective-permute-done.2.mark_a.tok_a.refs_1_.refs_3_, ...), custom_call_target="tpu_custom_call" | custom-call | tf_op jit(solution)/shard_map/onward_rows/pallas_call | solution.py:150
  82.4 2.9 %collective-permute-start.10 = (bf16[64,6144]{1,0:T(8,128)(2,1)}, bf16[64,6144]{1,0:T(8,128)(2,1)}, u32[]{:S(2)}, u32[]{:S(2)}) collective-permute-start(bf16[64,6144]{1,0:T(8,128)(2,1)} %get-tuple-element.91), channel_id=1, source_target_pairs={{0,112},{2,114},{4,116},{6,118},{8,120},{10,122},{12,124},{14,126}... | collective-permute-start | bytes 2359304 | tf_op jit(solution)/shard_map/ppermute | solution.py:279
  85.4 3.9 %plane_rows.5 = bf16[128,6144]{1,0:T(8,128)(2,1)S(1)} custom-call(s32[1]{0:T(128)} %bitcast.8.z_ref, bf16[128,3200]{1,0:T(8,128)(2,1)} %collective-permute-done.3.mark_b.tok_b.refs_0_.refs_2_, bf16[128,3200]{1,0:T(8,128)(2,1)S(1)} %collective-permute-done.2.mark_a.tok_a.refs_1_.refs_3_, ...), custom_call_target="tpu_custom_call" | custom-call | tf_op jit(solution)/shard_map/plane_rows/pallas_call | solution.py:96
  90.9 5.0 %all-to-all-start.3 = ((bf16[8,16,6144]{2,1,0:T(8,128)(2,1)}), bf16[8,16,6144]{2,1,0:T(8,128)(2,1)}, u32[]{:S(2)}, u32[]{:S(2)}) async-start(bf16[8,16,6144]{2,1,0:T(8,128)(2,1)} %bitcast.63), calls=%async_computation.3 | async-start | bytes 3145728 | tf_op jit(solution)/shard_map/all_to_all | solution.py:271
  97.7 2.3 collective-permute-start.9
  100.1 3.6 %collective-permute-done.10 = bf16[64,6144]{1,0:T(8,128)(2,1)} collective-permute-done((bf16[64,6144]{1,0:T(8,128)(2,1)}, bf16[64,6144]{1,0:T(8,128)(2,1)}, u32[]{:S(2)}, u32[]{:S(2)}) %collective-permute-start.10) | collective-permute-done | bytes 786464 | tf_op jit(solution)/shard_map/ppermute | solution.py:279
  103.7 2.5 %collective-permute-done.11 = bf16[64,6144]{1,0:T(8,128)(2,1)} collective-permute-done((bf16[64,6144]{1,0:T(8,128)(2,1)}, bf16[64,6144]{1,0:T(8,128)(2,1)}, u32[]{:S(2)}, u32[]{:S(2)}) %collective-permute-start.11) | collective-permute-done | bytes 786464 | tf_op jit(solution)/shard_map/ppermute | solution.py:279
  106.2 2.8 %pad_maximum_fusion.2 = bf16[8,16,6144]{2,1,0:T(8,128)(2,1)} fusion(bf16[8,8,6144]{2,1,0:T(8,128)(2,1)} %bitcast.17, bf16[8,8,6144]{2,1,0:T(8,128)(2,1)} %bitcast.16), kind=kLoop, calls=%fused_computation.16 | loop fusion | flops 3145728 | bytes 3145728 | tf_op jit(solution)/shard_map/concatenate | solution.py:293
  108.9 3.6 %expert_rows.7 = (bf16[128,384]{1,0:T(8,128)(2,1)S(1)}, bf16[64,3200]{1,0:T(8,128)(2,1)}, bf16[64,3200]{1,0:T(8,128)(2,1)}) custom-call(bf16[128,6144]{1,0:T(8,128)(2,1)S(1)} %bitcast.55, bf16[3072,256]{1,0:T(8,128)(2,1)S(1)} %copy.39.wgu_ref, bf16[256,3072]{1,0:T(8,128)(2,1)} %copy-done, bf16[3072,128]{1,0:T(8,128)(2,1)S(1)} %bitcast.59), custom_call_target="tpu_custom_call" | custom-call | flops 1 | bytes 3145728 | tf_op jit(solution)/shard_map/expert_rows/pallas_call | solution.py:258
  112.5 2.0 collective-permute-start.15
  114.6 2.1 all-to-all-done.3
  116.6 4.3 %all-to-all-start.4 = ((bf16[8,16,6144]{2,1,0:T(8,128)(2,1)}), bf16[8,16,6144]{2,1,0:T(8,128)(2,1)}, u32[]{:S(2)}, u32[]{:S(2)}) async-start(bf16[8,16,6144]{2,1,0:T(8,128)(2,1)} %pad_maximum_fusion.2), calls=%async_computation.4 | async-start | bytes 3145728 | tf_op jit(solution)/shard_map/all_to_all | solution.py:271
  120.9 3.3 %expert_rows.6 = (bf16[128,384]{1,0:T(8,128)(2,1)S(1)}, bf16[64,3200]{1,0:T(8,128)(2,1)S(1)}, bf16[64,3200]{1,0:T(8,128)(2,1)S(1)}) custom-call(bf16[128,6144]{1,0:T(8,128)(2,1)} %bitcast.19.row_ref, bf16[3072,256]{1,0:T(8,128)(2,1)S(1)} %copy.39.wgu_ref, bf16[256,3072]{1,0:T(8,128)(2,1)} %copy-done, bf16[3072,128]{1,0:T(8,128)(2,1)S(1)} %bitcast.60), custom_call_target="tpu_custom_call" | custom-call | flops 60000002048 | bytes 3145728 | tf_op jit(solution)/shard_map/expert_rows/pallas_call | solution.py:258
  127.9 3.3 %collective-permute-start.19 = (bf16[64,3200]{1,0:T(8,128)(2,1)S(1)}, bf16[64,3200]{1,0:T(8,128)(2,1)}, u32[]{:S(2)}, u32[]{:S(2)}) collective-permute-start(bf16[64,3200]{1,0:T(8,128)(2,1)S(1)} %get-tuple-element.102), channel_id=1, source_target_pairs={{0,96},{2,98},{4,100},{6,102},{8,104},{10,106},{12,108},{14,110},{... | collective-permute-start | bytes 1228808 | tf_op jit(solution)/shard_map/ppermute | solution.py:279
  131.2 8.6 %collective-permute-done.12 = bf16[64,3072]{1,0:T(8,128)(2,1)} collective-permute-done((bf16[64,3072]{1,0:T(8,128)(2,1)}, bf16[64,3072]{1,0:T(8,128)(2,1)}, u32[]{:S(2)}, u32[]{:S(2)}) %collective-permute-start.12) | collective-permute-done | bytes 393248 | tf_op jit(solution)/shard_map/ppermute | solution.py:279
  139.8 3.0 %collective-permute-done.13 = bf16[64,3072]{1,0:T(8,128)(2,1)} collective-permute-done((bf16[64,3072]{1,0:T(8,128)(2,1)}, bf16[64,3072]{1,0:T(8,128)(2,1)}, u32[]{:S(2)}, u32[]{:S(2)}) %collective-permute-start.13) | collective-permute-done | bytes 393248 | tf_op jit(solution)/shard_map/ppermute | solution.py:279
  142.8 2.0 maximum_bitcast_fusion
  144.9 5.5 %all-to-all-start.5 = ((bf16[8,8,6144]{2,1,0:T(8,128)(2,1)}), bf16[8,8,6144]{2,1,0:T(8,128)(2,1)}, u32[]{:S(2)}, u32[]{:S(2)}) async-start(bf16[8,8,6144]{2,1,0:T(8,128)(2,1)} %maximum_bitcast_fusion), calls=%async_computation.5 | async-start | bytes 1572864 | tf_op jit(solution)/shard_map/all_to_all | solution.py:271
  150.4 4.1 %expert_rows.8 = (bf16[128,384]{1,0:T(8,128)(2,1)S(1)}, bf16[64,3200]{1,0:T(8,128)(2,1)}, bf16[64,3200]{1,0:T(8,128)(2,1)}) custom-call(bf16[128,6144]{1,0:T(8,128)(2,1)} %bitcast.22.row_ref, bf16[3072,256]{1,0:T(8,128)(2,1)S(1)} %copy.39.wgu_ref, bf16[256,3072]{1,0:T(8,128)(2,1)} %copy-done, bf16[3072,128]{1,0:T(8,128)(2,1)S(1)} %bitcast.61), custom_call_target="tpu_custom_call" | custom-call | flops 60000002048 | bytes 3145728 | tf_op jit(solution)/shard_map/expert_rows/pallas_call | solution.py:258
  154.5 6.4 %collective-permute-start.16 = (bf16[64,3200]{1,0:T(8,128)(2,1)}, bf16[64,3200]{1,0:T(8,128)(2,1)}, u32[]{:S(2)}, u32[]{:S(2)}) collective-permute-start(bf16[64,3200]{1,0:T(8,128)(2,1)} %get-tuple-element.112), channel_id=1, source_target_pairs={{0,48},{2,50},{4,52},{6,54},{8,56},{10,58},{12,60},{14,62},{16,64}... | collective-permute-start | bytes 1228808 | tf_op jit(solution)/shard_map/ppermute | solution.py:279
  160.9 2.8 %pad_maximum_fusion = bf16[8,32,3200]{2,1,0:T(8,128)(2,1)} fusion(bf16[8,8,3200]{2,1,0:T(8,128)(2,1)} %bitcast.30, bf16[8,8,3200]{2,1,0:T(8,128)(2,1)} %bitcast.29, bf16[8,8,3200]{2,1,0:T(8,128)(2,1)} %bitcast.28, bf16[8,8,3200]{2,1,0:T(8,128)(2,1)} %bitcast.27), kind=kLoop, calls=%fused_computation.13 | loop fusion | flops 6553600 | bytes 3276800 | tf_op jit(solution)/shard_map/concatenate | solution.py:293
  164.8 2.9 %expert_rows.9 = (bf16[64,384]{1,0:T(8,128)(2,1)S(1)}, bf16[64,3200]{1,0:T(8,128)(2,1)}) custom-call(bf16[64,6144]{1,0:T(8,128)(2,1)} %bitcast.25.row_ref, bf16[3072,256]{1,0:T(8,128)(2,1)S(1)} %copy.39.wgu_ref, bf16[256,3072]{1,0:T(8,128)(2,1)S(1)} %copy-done.1, bf16[3072,128]{1,0:T(8,128)(2,1)S(1)} %bitcast.62), custom_call_target="tpu_custom_call" | custom-call | flops 1 | bytes 3145728 | tf_op jit(solution)/shard_map/expert_rows/pallas_call | solution.py:258
  167.8 4.2 %collective-permute-start.20 = (bf16[64,3200]{1,0:T(8,128)(2,1)}, bf16[64,3200]{1,0:T(8,128)(2,1)}, u32[]{:S(2)}, u32[]{:S(2)}) collective-permute-start(bf16[64,3200]{1,0:T(8,128)(2,1)} %get-tuple-element.123), channel_id=1, source_target_pairs={{0,64},{2,66},{4,68},{6,70},{8,72},{10,74},{12,76},{14,78},{16,80}... | collective-permute-start | bytes 1228808 | tf_op jit(solution)/shard_map/ppermute | solution.py:279
  172.0 5.8 %all-to-all-start.6 = ((bf16[8,32,3200]{2,1,0:T(8,128)(2,1)}), bf16[8,32,3200]{2,1,0:T(8,128)(2,1)S(1)}, u32[]{:S(2)}, u32[]{:S(2)}) async-start(bf16[8,32,3200]{2,1,0:T(8,128)(2,1)} %pad_maximum_fusion), calls=%async_computation.6 | async-start | bytes 3276800 | tf_op jit(solution)/shard_map/all_to_all | solution.py:271
  192.1 8.9 %collective-permute-done.17 = bf16[64,3200]{1,0:T(8,128)(2,1)} collective-permute-done((bf16[64,3200]{1,0:T(8,128)(2,1)}, bf16[64,3200]{1,0:T(8,128)(2,1)}, u32[]{:S(2)}, u32[]{:S(2)}) %collective-permute-start.17) | collective-permute-done | bytes 409632 | tf_op jit(solution)/shard_map/ppermute | solution.py:279
  201.0 2.4 pad_maximum_fusion.3
  203.7 5.0 %all-to-all-start.7 = ((bf16[8,24,3200]{2,1,0:T(8,128)(2,1)}), bf16[8,24,3200]{2,1,0:T(8,128)(2,1)}, u32[]{:S(2)}, u32[]{:S(2)}) async-start(bf16[8,24,3200]{2,1,0:T(8,128)(2,1)} %pad_maximum_fusion.3), calls=%async_computation.7 | async-start | bytes 2457600 | tf_op jit(solution)/shard_map/all_to_all | solution.py:271
  211.8 10.2 %all-to-all-done.7 = bf16[8,24,3200]{2,1,0:T(8,128)(2,1)} async-done(((bf16[8,24,3200]{2,1,0:T(8,128)(2,1)}), bf16[8,24,3200]{2,1,0:T(8,128)(2,1)}, u32[]{:S(2)}, u32[]{:S(2)}) %all-to-all-start.7) | async-done | bytes 1228832 | tf_op jit(solution)/shard_map/all_to_all | solution.py:271
  223.0 2.1 fusion.4
  225.1 2.9 %collective-permute-start.21 = (bf16[128,3072]{1,0:T(8,128)(2,1)S(1)}, bf16[128,3072]{1,0:T(8,128)(2,1)S(1)}, u32[]{:S(2)}, u32[]{:S(2)}) collective-permute-start(bf16[128,3072]{1,0:T(8,128)(2,1)S(1)} %fusion.4), channel_id=1, source_target_pairs={{0,128},{128,0},{1,129},{129,1},{2,130},{130,2},{3,131},{131,3},{4... | collective-permute-start | bytes 2359304 | tf_op jit(solution)/shard_map/ppermute | solution.py:394
  228.8 9.9 %collective-permute-done.21 = bf16[128,3072]{1,0:T(8,128)(2,1)S(1)} collective-permute-done((bf16[128,3072]{1,0:T(8,128)(2,1)S(1)}, bf16[128,3072]{1,0:T(8,128)(2,1)S(1)}, u32[]{:S(2)}, u32[]{:S(2)}) %collective-permute-start.21) | collective-permute-done | bytes 786464 | tf_op jit(solution)/shard_map/ppermute | solution.py:394
  (125 shorter events, 44.7 us)
Async XLA Ops:
  0.6 9.1 %copy-start.13 = (bf16[1,128,3072]{2,1,0:T(8,128)(2,1)S(1)}, bf16[1,128,3072]{2,1,0:T(8,128)(2,1)}, u32[]{:S(2)}) copy-start(bf16[1,128,3072]{2,1,0:T(8,128)(2,1)} %param.10) | copy-start | bytes 2359300
  0.6 33.7 %collective-permute-start.6 = (bf16[128,3072]{1,0:T(8,128)(2,1)}, bf16[128,3072]{1,0:T(8,128)(2,1)}, u32[]{:S(2)}, u32[]{:S(2)}) collective-permute-start(bf16[128,3072]{1,0:T(8,128)(2,1)} %bitcast.68), channel_id=1, source_target_pairs={{0,112},{2,114},{4,116},{6,118},{8,120},{10,122},{12,124},{14,126}... | collective-permute-start | bytes 2359304 | tf_op jit(solution)/shard_map/ppermute | solution.py:279
  2.6 35.0 %collective-permute-start.4 = (bf16[128,3072]{1,0:T(8,128)(2,1)}, bf16[128,3072]{1,0:T(8,128)(2,1)}, u32[]{:S(2)}, u32[]{:S(2)}) collective-permute-start(bf16[128,3072]{1,0:T(8,128)(2,1)} %bitcast.69), channel_id=1, source_target_pairs={{0,16},{2,18},{4,20},{6,22},{8,24},{10,26},{12,28},{14,30},{16,32}... | collective-permute-start | bytes 2359304 | tf_op jit(solution)/shard_map/ppermute | solution.py:279
  4.3 7.8 %copy-start.25 = (s32[1,128,2]{2,1,0:T(8,128)}, s32[1,128,2]{2,1,0:T(8,128)S(1)}, u32[]{:S(2)}) copy-start(s32[1,128,2]{2,1,0:T(8,128)S(1)} %copy.33) | copy-start | bytes 3076
  5.6 42.3 %collective-permute-start.1 = (bf16[128,3200]{1,0:T(8,128)(2,1)S(1)}, bf16[128,3200]{1,0:T(8,128)(2,1)}, u32[]{:S(2)}, u32[]{:S(2)}) collective-permute-start(bf16[128,3200]{1,0:T(8,128)(2,1)S(1)} %pad_maximum_fusion.4.refs_0_.refs_1_), channel_id=1, source_target_pairs={{0,16},{2,18},{4,20},{6,22},{8,24},{10,26},{12,28},{14,30},{16,32}... | collective-permute-start | bytes 2457608 | tf_op jit(solution)/shard_map/ppermute | solution.py:279
  7.6 40.3 %collective-permute-start = (bf16[128,3200]{1,0:T(8,128)(2,1)S(1)}, bf16[128,3200]{1,0:T(8,128)(2,1)}, u32[]{:S(2)}, u32[]{:S(2)}) collective-permute-start(bf16[128,3200]{1,0:T(8,128)(2,1)S(1)} %pad_maximum_fusion.4.refs_0_.refs_1_), channel_id=1, source_target_pairs={{0,112},{2,114},{4,116},{6,118},{8,120},{10,122},{12,124},{14,126}... | collective-permute-start | bytes 2457608 | tf_op jit(solution)/shard_map/ppermute | solution.py:279
  12.2 5.5 %copy-start.20 = (bf16[1,1,1536,128]{3,2,1,0:T(8,128)(2,1)S(1)}, bf16[1,1,1536,128]{3,2,1,0:T(8,128)(2,1)}, u32[]{:S(2)}) copy-start(bf16[1,1,1536,128]{3,2,1,0:T(8,128)(2,1)} %param.11) | copy-start | bytes 1179652
  12.2 8.4 %copy-start.21 = (bf16[1,1,1536,128]{3,2,1,0:T(8,128)(2,1)S(1)}, bf16[1,1,1536,128]{3,2,1,0:T(8,128)(2,1)}, u32[]{:S(2)}) copy-start(bf16[1,1,1536,128]{3,2,1,0:T(8,128)(2,1)} %param.12) | copy-start | bytes 1179652
  12.2 25.4 %all-to-all-start = ((bf16[8,8,6144]{2,1,0:T(8,128)(2,1)}), bf16[8,8,6144]{2,1,0:T(8,128)(2,1)S(1)}, u32[]{:S(2)}, u32[]{:S(2)}) async-start(bf16[8,8,6144]{2,1,0:T(8,128)(2,1)} %bitcast.10), calls=%async_computation | async-start | bytes 1572864 | tf_op jit(solution)/shard_map/all_to_all | solution.py:271
  17.9 5.3 %copy-start.22 = (bf16[1,1,128,1536]{3,2,1,0:T(8,128)(2,1)S(1)}, bf16[1,1,128,1536]{3,2,1,0:T(8,128)(2,1)}, u32[]{:S(2)}) copy-start(bf16[1,1,128,1536]{3,2,1,0:T(8,128)(2,1)} %param.13) | copy-start | bytes 1179652
  27.1 10.5 %copy-start = (bf16[256,3072]{1,0:T(8,128)(2,1)}, bf16[256,3072]{1,0:T(8,128)(2,1)S(1)}, u32[]{:S(2)}) copy-start(bf16[256,3072]{1,0:T(8,128)(2,1)S(1)} %get-tuple-element.99.wgu_t_ref) | copy-start | bytes 4718596
  34.3 21.4 %collective-permute-start.7 = (bf16[128,3072]{1,0:T(8,128)(2,1)}, bf16[128,3072]{1,0:T(8,128)(2,1)}, u32[]{:S(2)}, u32[]{:S(2)}) collective-permute-start(bf16[128,3072]{1,0:T(8,128)(2,1)} %collective-permute-done.6.refs_4_), channel_id=1, source_target_pairs={{0,112},{2,114},{4,116},{6,118},{8,120},{10,122},{12,124},{14,126}... | collective-permute-start | bytes 2359304 | tf_op jit(solution)/shard_map/ppermute | solution.py:279
  37.6 22.2 %collective-permute-start.5 = (bf16[128,3072]{1,0:T(8,128)(2,1)}, bf16[128,3072]{1,0:T(8,128)(2,1)}, u32[]{:S(2)}, u32[]{:S(2)}) collective-permute-start(bf16[128,3072]{1,0:T(8,128)(2,1)} %collective-permute-done.4.refs_5_), channel_id=1, source_target_pairs={{0,16},{2,18},{4,20},{6,22},{8,24},{10,26},{12,28},{14,30},{16,32}... | collective-permute-start | bytes 2359304 | tf_op jit(solution)/shard_map/ppermute | solution.py:279
  37.6 3.9 %copy-start.10 = (bf16[8,8,6144]{2,1,0:T(8,128)(2,1)}, bf16[8,8,6144]{2,1,0:T(8,128)(2,1)S(1)}, u32[]{:S(2)}) copy-start(bf16[8,8,6144]{2,1,0:T(8,128)(2,1)S(1)} %all-to-all-done) | copy-start | bytes 2359300
  42.2 22.7 %all-to-all-start.1 = ((bf16[8,8,3200]{2,1,0:T(8,128)(2,1)}), bf16[8,8,3200]{2,1,0:T(8,128)(2,1)S(1)}, u32[]{:S(2)}, u32[]{:S(2)}) async-start(bf16[8,8,3200]{2,1,0:T(8,128)(2,1)} %bitcast.71), calls=%async_computation.1 | async-start | bytes 819200 | tf_op jit(solution)/shard_map/all_to_all | solution.py:271
  47.9 28.2 %collective-permute-start.2 = (bf16[128,3200]{1,0:T(8,128)(2,1)}, bf16[128,3200]{1,0:T(8,128)(2,1)S(1)}, u32[]{:S(2)}, u32[]{:S(2)}) collective-permute-start(bf16[128,3200]{1,0:T(8,128)(2,1)} %collective-permute-done.1.refs_1_.refs_3_), channel_id=1, source_target_pairs={{0,16},{2,18},{4,20},{6,22},{8,24},{10,26},{12,28},{14,30},{16,32}... | collective-permute-start | bytes 2457608 | tf_op jit(solution)/shard_map/ppermute | solution.py:279
  48.0 28.1 %collective-permute-start.3 = (bf16[128,3200]{1,0:T(8,128)(2,1)}, bf16[128,3200]{1,0:T(8,128)(2,1)}, u32[]{:S(2)}, u32[]{:S(2)}) collective-permute-start(bf16[128,3200]{1,0:T(8,128)(2,1)} %collective-permute-done.refs_0_.refs_2_), channel_id=1, source_target_pairs={{0,112},{2,114},{4,116},{6,118},{8,120},{10,122},{12,124},{14,126}... | collective-permute-start | bytes 2457608 | tf_op jit(solution)/shard_map/ppermute | solution.py:279
  65.7 25.2 %all-to-all-start.2 = ((bf16[8,16,6144]{2,1,0:T(8,128)(2,1)}), bf16[8,16,6144]{2,1,0:T(8,128)(2,1)S(1)}, u32[]{:S(2)}, u32[]{:S(2)}) async-start(bf16[8,16,6144]{2,1,0:T(8,128)(2,1)} %bitcast.64), calls=%async_computation.2 | async-start | bytes 3145728 | tf_op jit(solution)/shard_map/all_to_all | solution.py:271
  82.4 21.2 %collective-permute-start.10 = (bf16[64,6144]{1,0:T(8,128)(2,1)}, bf16[64,6144]{1,0:T(8,128)(2,1)}, u32[]{:S(2)}, u32[]{:S(2)}) collective-permute-start(bf16[64,6144]{1,0:T(8,128)(2,1)} %get-tuple-element.91), channel_id=1, source_target_pairs={{0,112},{2,114},{4,116},{6,118},{8,120},{10,122},{12,124},{14,126}... | collective-permute-start | bytes 2359304 | tf_op jit(solution)/shard_map/ppermute | solution.py:279
  85.4 20.8 %collective-permute-start.11 = (bf16[64,6144]{1,0:T(8,128)(2,1)}, bf16[64,6144]{1,0:T(8,128)(2,1)}, u32[]{:S(2)}, u32[]{:S(2)}) collective-permute-start(bf16[64,6144]{1,0:T(8,128)(2,1)} %get-tuple-element.92), channel_id=1, source_target_pairs={{0,16},{2,18},{4,20},{6,22},{8,24},{10,26},{12,28},{14,30},{16,32}... | collective-permute-start | bytes 2359304 | tf_op jit(solution)/shard_map/ppermute | solution.py:279
  90.9 18.0 %copy-start.2 = (bf16[8,16,6144]{2,1,0:T(8,128)(2,1)}, bf16[8,16,6144]{2,1,0:T(8,128)(2,1)S(1)}, u32[]{:S(2)}) copy-start(bf16[8,16,6144]{2,1,0:T(8,128)(2,1)S(1)} %all-to-all-done.2) | copy-start | bytes 4718596
  90.9 25.7 %all-to-all-start.3 = ((bf16[8,16,6144]{2,1,0:T(8,128)(2,1)}), bf16[8,16,6144]{2,1,0:T(8,128)(2,1)}, u32[]{:S(2)}, u32[]{:S(2)}) async-start(bf16[8,16,6144]{2,1,0:T(8,128)(2,1)} %bitcast.63), calls=%async_computation.3 | async-start | bytes 3145728 | tf_op jit(solution)/shard_map/all_to_all | solution.py:271
  97.6 27.4 %collective-permute-start.8 = (bf16[64,3072]{1,0:T(8,128)(2,1)}, bf16[64,3072]{1,0:T(8,128)(2,1)}, u32[]{:S(2)}, u32[]{:S(2)}) collective-permute-start(bf16[64,3072]{1,0:T(8,128)(2,1)} %copy-done.17), channel_id=1, source_target_pairs={{0,16},{2,18},{4,20},{6,22},{8,24},{10,26},{12,28},{14,30},{16,32}... | collective-permute-start | bytes 1179656 | tf_op jit(solution)/shard_map/ppermute | solution.py:279
  97.7 27.3 %collective-permute-start.9 = (bf16[64,3072]{1,0:T(8,128)(2,1)}, bf16[64,3072]{1,0:T(8,128)(2,1)}, u32[]{:S(2)}, u32[]{:S(2)}) collective-permute-start(bf16[64,3072]{1,0:T(8,128)(2,1)} %copy-done.16), channel_id=1, source_target_pairs={{0,112},{2,114},{4,116},{6,118},{8,120},{10,122},{12,124},{14,126}... | collective-permute-start | bytes 1179656 | tf_op jit(solution)/shard_map/ppermute | solution.py:279
  112.5 15.4 %collective-permute-start.14 = (bf16[64,3200]{1,0:T(8,128)(2,1)}, bf16[64,3200]{1,0:T(8,128)(2,1)}, u32[]{:S(2)}, u32[]{:S(2)}) collective-permute-start(bf16[64,3200]{1,0:T(8,128)(2,1)} %get-tuple-element.106), channel_id=1, source_target_pairs={{0,16},{2,18},{4,20},{6,22},{8,24},{10,26},{12,28},{14,30},{16,32}... | collective-permute-start | bytes 1228808 | tf_op jit(solution)/shard_map/ppermute | solution.py:279
  112.5 8.4 %copy-start.6 = (bf16[1,1,128,3072]{2,3,1,0:T(8,128)(2,1)S(1)}, bf16[1,1,128,3072]{2,3,1,0:T(8,128)(2,1)}, u32[]{:S(2)}) copy-start(bf16[1,1,128,3072]{2,3,1,0:T(8,128)(2,1)} %all-gather.2) | copy-start | bytes 2359300
  112.5 18.7 %collective-permute-start.15 = (bf16[64,3200]{1,0:T(8,128)(2,1)}, bf16[64,3200]{1,0:T(8,128)(2,1)}, u32[]{:S(2)}, u32[]{:S(2)}) collective-permute-start(bf16[64,3200]{1,0:T(8,128)(2,1)} %get-tuple-element.107), channel_id=1, source_target_pairs={{0,112},{2,114},{4,116},{6,118},{8,120},{10,122},{12,124},{14,126}... | collective-permute-start | bytes 1228808 | tf_op jit(solution)/shard_map/ppermute | solution.py:279
  116.6 28.2 %all-to-all-start.4 = ((bf16[8,16,6144]{2,1,0:T(8,128)(2,1)}), bf16[8,16,6144]{2,1,0:T(8,128)(2,1)}, u32[]{:S(2)}, u32[]{:S(2)}) async-start(bf16[8,16,6144]{2,1,0:T(8,128)(2,1)} %pad_maximum_fusion.2), calls=%async_computation.4 | async-start | bytes 3145728 | tf_op jit(solution)/shard_map/all_to_all | solution.py:271
  125.1 14.8 %collective-permute-start.12 = (bf16[64,3072]{1,0:T(8,128)(2,1)}, bf16[64,3072]{1,0:T(8,128)(2,1)}, u32[]{:S(2)}, u32[]{:S(2)}) collective-permute-start(bf16[64,3072]{1,0:T(8,128)(2,1)} %collective-permute-done.8), channel_id=1, source_target_pairs={{0,16},{2,18},{4,20},{6,22},{8,24},{10,26},{12,28},{14,30},{16,32}... | collective-permute-start | bytes 1179656 | tf_op jit(solution)/shard_map/ppermute | solution.py:279
  125.1 17.8 %collective-permute-start.13 = (bf16[64,3072]{1,0:T(8,128)(2,1)}, bf16[64,3072]{1,0:T(8,128)(2,1)}, u32[]{:S(2)}, u32[]{:S(2)}) collective-permute-start(bf16[64,3072]{1,0:T(8,128)(2,1)} %collective-permute-done.9), channel_id=1, source_target_pairs={{0,112},{2,114},{4,116},{6,118},{8,120},{10,122},{12,124},{14,126}... | collective-permute-start | bytes 1179656 | tf_op jit(solution)/shard_map/ppermute | solution.py:279
  127.1 27.4 %collective-permute-start.18 = (bf16[64,3200]{1,0:T(8,128)(2,1)}, bf16[64,3200]{1,0:T(8,128)(2,1)}, u32[]{:S(2)}, u32[]{:S(2)}) collective-permute-start(bf16[64,3200]{1,0:T(8,128)(2,1)} %copy-done.15), channel_id=1, source_target_pairs={{0,32},{2,34},{4,36},{6,38},{8,40},{10,42},{12,44},{14,46},{16,48}... | collective-permute-start | bytes 1228808 | tf_op jit(solution)/shard_map/ppermute | solution.py:279
  127.9 26.6 %collective-permute-start.19 = (bf16[64,3200]{1,0:T(8,128)(2,1)S(1)}, bf16[64,3200]{1,0:T(8,128)(2,1)}, u32[]{:S(2)}, u32[]{:S(2)}) collective-permute-start(bf16[64,3200]{1,0:T(8,128)(2,1)S(1)} %get-tuple-element.102), channel_id=1, source_target_pairs={{0,96},{2,98},{4,100},{6,102},{8,104},{10,106},{12,108},{14,110},{... | collective-permute-start | bytes 1228808 | tf_op jit(solution)/shard_map/ppermute | solution.py:279
  144.9 18.8 %all-to-all-start.5 = ((bf16[8,8,6144]{2,1,0:T(8,128)(2,1)}), bf16[8,8,6144]{2,1,0:T(8,128)(2,1)}, u32[]{:S(2)}, u32[]{:S(2)}) async-start(bf16[8,8,6144]{2,1,0:T(8,128)(2,1)} %maximum_bitcast_fusion), calls=%async_computation.5 | async-start | bytes 1572864 | tf_op jit(solution)/shard_map/all_to_all | solution.py:271
  154.5 37.6 %collective-permute-start.16 = (bf16[64,3200]{1,0:T(8,128)(2,1)}, bf16[64,3200]{1,0:T(8,128)(2,1)}, u32[]{:S(2)}, u32[]{:S(2)}) collective-permute-start(bf16[64,3200]{1,0:T(8,128)(2,1)} %get-tuple-element.112), channel_id=1, source_target_pairs={{0,48},{2,50},{4,52},{6,54},{8,56},{10,58},{12,60},{14,62},{16,64}... | collective-permute-start | bytes 1228808 | tf_op jit(solution)/shard_map/ppermute | solution.py:279
  160.9 40.1 %collective-permute-start.17 = (bf16[64,3200]{1,0:T(8,128)(2,1)}, bf16[64,3200]{1,0:T(8,128)(2,1)}, u32[]{:S(2)}, u32[]{:S(2)}) collective-permute-start(bf16[64,3200]{1,0:T(8,128)(2,1)} %get-tuple-element.113), channel_id=1, source_target_pairs={{0,80},{2,82},{4,84},{6,86},{8,88},{10,90},{12,92},{14,94},{16,96}... | collective-permute-start | bytes 1228808 | tf_op jit(solution)/shard_map/ppermute | solution.py:279
  160.9 2.8 %copy-start.1 = (bf16[256,3072]{1,0:T(8,128)(2,1)S(1)}, bf16[256,3072]{1,0:T(8,128)(2,1)}, u32[]{:S(2)}) copy-start(bf16[256,3072]{1,0:T(8,128)(2,1)} %copy-done) | copy-start | bytes 4718596
  167.8 33.3 %collective-permute-start.20 = (bf16[64,3200]{1,0:T(8,128)(2,1)}, bf16[64,3200]{1,0:T(8,128)(2,1)}, u32[]{:S(2)}, u32[]{:S(2)}) collective-permute-start(bf16[64,3200]{1,0:T(8,128)(2,1)} %get-tuple-element.123), channel_id=1, source_target_pairs={{0,64},{2,66},{4,68},{6,70},{8,72},{10,74},{12,76},{14,78},{16,80}... | collective-permute-start | bytes 1228808 | tf_op jit(solution)/shard_map/ppermute | solution.py:279
  172.0 5.8 %copy-start.11 = (bf16[8,8,6144]{2,1,0:T(8,128)(2,1)S(1)}, bf16[8,8,6144]{2,1,0:T(8,128)(2,1)}, u32[]{:S(2)}) copy-start(bf16[8,8,6144]{2,1,0:T(8,128)(2,1)} %copy-done.10) | copy-start | bytes 2359300
  172.0 31.7 %all-to-all-start.6 = ((bf16[8,32,3200]{2,1,0:T(8,128)(2,1)}), bf16[8,32,3200]{2,1,0:T(8,128)(2,1)S(1)}, u32[]{:S(2)}, u32[]{:S(2)}) async-start(bf16[8,32,3200]{2,1,0:T(8,128)(2,1)} %pad_maximum_fusion), calls=%async_computation.6 | async-start | bytes 3276800 | tf_op jit(solution)/shard_map/all_to_all | solution.py:271
  188.2 3.0 %collective-permute-start.23 = (bf16[128,1536]{1,0:T(8,128)(2,1)S(1)}, bf16[128,1536]{1,0:T(8,128)(2,1)S(1)}, u32[]{:S(2)}, u32[]{:S(2)}) collective-permute-start(bf16[128,1536]{1,0:T(8,128)(2,1)S(1)} %constant_dynamic-slice_fusion), channel_id=1, source_target_pairs={{0,1},{1,0},{2,3},{3,2},{4,5},{5,4},{6,7},{7,6},{8,9},{9,8},{10,11... | collective-permute-start | bytes 1179656 | tf_op jit(solution)/shard_map/ppermute | solution.py:287
  190.7 12.8 %collective-permute-start.22 = (bf16[1536,256]{1,0:T(8,128)(2,1)S(1)}, bf16[1536,256]{1,0:T(8,128)(2,1)S(1)}, u32[]{:S(2)}, u32[]{:S(2)}) collective-permute-start(bf16[1536,256]{1,0:T(8,128)(2,1)S(1)} %constant_dynamic-slice_fusion.1), channel_id=1, source_target_pairs={{0,1},{1,0},{2,3},{3,2},{4,5},{5,4},{6,7},{7,6},{8,9},{9,8},{10,11... | collective-permute-start | bytes 2359304 | tf_op jit(solution)/shard_map/ppermute | solution.py:287
  203.6 6.0 %copy-start.24 = (bf16[256,256]{1,0:T(8,128)(2,1)S(1)}, bf16[256,256]{1,0:T(8,128)(2,1)}, u32[]{:S(2)}) copy-start(bf16[256,256]{1,0:T(8,128)(2,1)} %get-tuple-element.132) | copy-start | bytes 393220
  203.6 6.2 %copy-start.19 = (bf16[8,8,3200]{2,1,0:T(8,128)(2,1)S(1)}, bf16[8,8,3200]{2,1,0:T(8,128)(2,1)}, u32[]{:S(2)}) copy-start(bf16[8,8,3200]{2,1,0:T(8,128)(2,1)} %copy-done.18) | copy-start | bytes 1228804
  203.6 6.2 %copy-start.26 = (bf16[256,64]{1,0:T(8,128)(2,1)S(1)}, bf16[256,64]{1,0:T(8,128)(2,1)}, u32[]{:S(2)}) copy-start(bf16[256,64]{1,0:T(8,128)(2,1)} %get-tuple-element.82) | copy-start | bytes 98308
  203.7 18.3 %all-to-all-start.7 = ((bf16[8,24,3200]{2,1,0:T(8,128)(2,1)}), bf16[8,24,3200]{2,1,0:T(8,128)(2,1)}, u32[]{:S(2)}, u32[]{:S(2)}) async-start(bf16[8,24,3200]{2,1,0:T(8,128)(2,1)} %pad_maximum_fusion.3), calls=%async_computation.7 | async-start | bytes 2457600 | tf_op jit(solution)/shard_map/all_to_all | solution.py:271
  210.2 11.8 %copy-start.23 = (bf16[256,192]{1,0:T(8,128)(2,1)S(1)}, bf16[256,192]{1,0:T(8,128)(2,1)}, u32[]{:S(2)}) copy-start(bf16[256,192]{1,0:T(8,128)(2,1)} %get-tuple-element.133) | copy-start | bytes 294916
  223.0 5.3 %copy-start.27 = (bf16[1,128,2]{1,2,0:T(2,128)(2,1)S(1)}, bf16[1,128,2]{1,2,0:T(2,128)(2,1)}, u32[]{:S(2)}) copy-start(bf16[1,128,2]{1,2,0:T(2,128)(2,1)} %param.9) | copy-start | bytes 1540
  225.1 13.6 %collective-permute-start.21 = (bf16[128,3072]{1,0:T(8,128)(2,1)S(1)}, bf16[128,3072]{1,0:T(8,128)(2,1)S(1)}, u32[]{:S(2)}, u32[]{:S(2)}) collective-permute-start(bf16[128,3072]{1,0:T(8,128)(2,1)S(1)} %fusion.4), channel_id=1, source_target_pairs={{0,128},{128,0},{1,129},{129,1},{2,130},{130,2},{3,131},{131,3},{4... | collective-permute-start | bytes 2359304 | tf_op jit(solution)/shard_map/ppermute | solution.py:394
  (12 other events, 14.4 us)
